TPU v7x, 128 devices: a whole 4x4x4 slice. The times are simulated.
128 devices in a mesh: lat: 16 (over y_hi, z, core), wave: 8 (over x, y_lo).
Axes of the slice: x: 4, y: 4 (y_hi: 2, y_lo: 2; y = y_hi * 2 + y_lo), z: 4, core: 2. Of those that a mesh axis runs over, the one named last changes fastest.
Arguments:
- grad_grid: float32 [3, 6, 640, 2560], P(None, None, ('lat', 'wave')), may hold values from -6 to 6
- owner: int32 [640], replicated, may hold values from 0 to 639, each once
- legendre: float32 [640, 640, 1408], P('wave', 'lat'), may hold values from -0.25 to 0.25
- lat_weights: float32 [640], P('lat'), may hold values from 0.5 to 2
- modes_e: float32 [6, 6], replicated, may hold values from -2.5 to 2.5
- modes_f: float32 [6, 6], replicated, may hold values from -2.5 to 2.5
- rates: float32 [6], replicated, may hold values from 0.1 to 10
- height_matrix: float32 [6, 6], replicated, may hold values from -2.5 to 2.5
- heating_matrix: float32 [6, 6], replicated, may hold values from -2.5 to 2.5
Outputs:
- grad_out: float32 [3, 6, 640, 2560], P(None, None, ('lat', 'wave'))
Inputs may be any that keep to these rules, and one draw needn't show every extreme that they name: Each pair number appears once; slot j holds the wavenumbers owner[j] and 1279 - owner[j].
All inputs are finite; a program needn't handle non-finite values.
Results may differ from a plain program's by a relative error of at most 0.0001.
Values sent between devices are 32-bit elements; how exact they have to be, the bound alone decides.
No kernel may reach another device: no remote copies, remote signals or barrier semaphores. Data moves between devices by JAX's collectives and lax.ppermute only.
A program may use at most 256 MiB of HBM per device.

v0:
```python
import math

import jax
import jax.numpy as jnp
from jax import lax
from jax.sharding import PartitionSpec as P

TOP_HARMONIC = lax.Precision.HIGHEST


def fourier_table(lon_count, truncation):
    lon_index = lax.broadcasted_iota(jnp.int32, (lon_count, truncation), 0)
    wave_index = lax.broadcasted_iota(jnp.int32, (lon_count, truncation), 1)
    phases = (lon_index * wave_index % lon_count).astype(jnp.float32) * (2.0 * math.pi / lon_count)
    factor = math.sqrt(2.0 / lon_count)
    return jnp.concatenate([jnp.cos(phases) * factor, -jnp.sin(phases) * factor], axis=1)


def slot_masks(first_wave, slot_start, slot_count, truncation):
    packed = slot_start + lax.broadcasted_iota(jnp.int32, (slot_count, first_wave.shape[0]), 0)
    is_first = packed < truncation - first_wave[None, :]
    is_second = jnp.logical_and(jnp.logical_not(is_first), packed <= truncation)
    degree = jnp.where(is_first, first_wave[None, :] + packed, packed - 1)
    return (is_first, is_second, degree)


def legendre_terms(leg_table, fourier, first_wave, slot_start, slot_count, truncation):
    is_first, is_second, degree = slot_masks(first_wave, slot_start, slot_count, truncation)
    first_part = jnp.einsum(
        "plk,flrp->kpfr", leg_table, fourier[:, :, 0:2, :], precision=TOP_HARMONIC
    )
    second_part = jnp.einsum(
        "plk,flrp->kpfr", leg_table, fourier[:, :, 2:4, :], precision=TOP_HARMONIC
    )
    return jnp.where(
        is_first[:, :, None, None],
        first_part,
        jnp.where(is_second[:, :, None, None], second_part, 0.0),
    )


def semi_implicit(
    harmonic_coefficient_arrays,
    degree,
    truncation,
    modes_e,
    modes_f,
    rates,
    height_matrix,
    heating_matrix,
):
    levels = modes_e.shape[0]
    state_variables = harmonic_coefficient_arrays.reshape(
        harmonic_coefficient_arrays.shape[0], harmonic_coefficient_arrays.shape[1], 3, levels, 2
    )
    vorticity = state_variables[:, :, 0]
    spreading_rate = state_variables[:, :, 1]
    thermal_state = state_variables[:, :, 2]
    degree_float = degree.astype(jnp.float32)
    harmonic_order_factor = (
        degree_float * (degree_float + 1.0) / float(truncation * (truncation + 1))
    )[:, :, None, None]
    driving_sources = spreading_rate - jnp.einsum(
        "em,zhek->zhmk", heating_matrix, thermal_state, precision=TOP_HARMONIC
    )
    modal_part = jnp.einsum("em,zhek->zhmk", modes_e, driving_sources, precision=TOP_HARMONIC)
    modal_part = modal_part / (1.0 + 4.0 * harmonic_order_factor * rates[None, None, :, None])
    next_spreading_rate = jnp.einsum("em,zhek->zhmk", modes_f, modal_part, precision=TOP_HARMONIC)
    next_thermal_state = thermal_state - harmonic_order_factor * jnp.einsum(
        "em,zhek->zhmk", height_matrix, next_spreading_rate, precision=TOP_HARMONIC
    )
    next_rotation = vorticity / (1.0 + 4.0 * harmonic_order_factor * harmonic_order_factor)
    return jnp.stack([next_rotation, next_spreading_rate, next_thermal_state], axis=2).reshape(
        harmonic_coefficient_arrays.shape
    )


def legendre_back(leg_table, harmonic_coefficient_arrays, first_wave, slot_start, truncation):
    slot_count = harmonic_coefficient_arrays.shape[0]
    is_first, is_second, degree = slot_masks(first_wave, slot_start, slot_count, truncation)
    first_back = jnp.einsum(
        "plk,kpfr->flrp",
        leg_table,
        jnp.where(is_first[:, :, None, None], harmonic_coefficient_arrays, 0.0),
        precision=TOP_HARMONIC,
    )
    second_back = jnp.einsum(
        "plk,kpfr->flrp",
        leg_table,
        jnp.where(is_second[:, :, None, None], harmonic_coefficient_arrays, 0.0),
        precision=TOP_HARMONIC,
    )
    return (first_back, second_back)


def per_device(
    grad_grid, owner, legendre, lat_weights, modes_e, modes_f, rates, height_matrix, heating_matrix
):
    state_variables, levels, lat_rows, lon_count = grad_grid.shape
    truncation = 2 * owner.shape[0]
    width = state_variables * levels
    slots = legendre.shape[0]
    packed = legendre.shape[2]
    dft_table = fourier_table(lon_count, truncation)
    fourier = jnp.dot(
        grad_grid.reshape(width * lat_rows, lon_count),
        dft_table,
        precision=TOP_HARMONIC,
        preferred_element_type=jnp.float32,
    )
    fourier = fourier.reshape(width, lat_rows, 2, truncation)
    selected = jnp.concatenate([fourier[..., owner], fourier[..., truncation - 1 - owner]], axis=2)
    banded = lax.all_to_all(selected, "wave", split_axis=3, concat_axis=1, tiled=True)
    owned_pairs = lax.dynamic_slice_in_dim(owner, lax.axis_index("wave") * slots, slots, 0)
    partial_value = lax.psum_scatter(
        legendre_terms(
            legendre,
            banded,
            owned_pairs,
            jnp.int32(0),
            packed // lax.axis_size("lat") * lax.axis_size("lat"),
            truncation,
        ).reshape(packed // lax.axis_size("lat") * lax.axis_size("lat"), slots * width * 2),
        "lat",
        scatter_dimension=0,
        tiled=True,
    )
    share_len = partial_value.shape[0]
    share_base = lax.axis_index("lat") * share_len
    harmonic_coefficient_arrays = partial_value.reshape(share_len, slots, width, 2)
    is_first, is_second, degree = slot_masks(owned_pairs, share_base, share_len, truncation)
    harmonic_coefficient_arrays = semi_implicit(
        harmonic_coefficient_arrays,
        degree,
        truncation,
        modes_e,
        modes_f,
        rates,
        height_matrix,
        heating_matrix,
    )
    first_back, second_back = legendre_back(
        legendre,
        lax.all_gather(harmonic_coefficient_arrays, "lat", axis=0, tiled=True),
        owned_pairs,
        jnp.int32(0),
        truncation,
    )
    first_back, second_back = (first_back, second_back)
    weighted = jnp.concatenate([first_back, second_back], axis=2) * lat_weights[None, :, None, None]
    returned = lax.all_to_all(weighted, "wave", split_axis=1, concat_axis=3, tiled=True)
    spectral = jnp.zeros((width, lat_rows, 2, truncation), jnp.float32)
    spectral = spectral.at[..., owner].set(returned[:, :, 0:2, :])
    spectral = spectral.at[..., truncation - 1 - owner].set(returned[:, :, 2:4, :])
    gridded = lax.dot_general(
        spectral.reshape(width * lat_rows, 2 * truncation),
        dft_table,
        (((1,), (1,)), ((), ())),
        precision=TOP_HARMONIC,
        preferred_element_type=jnp.float32,
    )
    return gridded.reshape(state_variables, levels, lat_rows, lon_count)


def solution(mesh):
    in_specs = (
        P(None, None, ("lat", "wave"), None),
        P(),
        P("wave", "lat", None),
        P("lat"),
        P(),
        P(),
        P(),
        P(),
        P(),
    )
    out_specs = P(None, None, ("lat", "wave"), None)
    return jax.shard_map(
        per_device, mesh=mesh, in_specs=in_specs, out_specs=out_specs, check_vma=False
    )
```

profile of v0, /device:TPU:1, one launch (start us, length us, event | category | flops | bytes accessed | tf_op | source)
XLA Modules:
  0.0 965.6 jit_solution(2496397361754402069)
XLA Ops:
  6.5 55.2 %negate_multiply_fusion = (f32[2560,1280]{1,0:T(8,128)}, f32[2560,1280]{1,0:T(8,128)}) fusion(), kind=kLoop, calls=%fused_computation.23 | loop fusion | flops 39321600 | bytes 26214400 | tf_op jit(solution)/shard_map/mul | solution.py:16
  61.7 0.5 copy.167
  62.5 19.2 %fusion.25 = f32[90,2560]{1,0:T(8,128)S(1)} fusion(f32[90,2560]{1,0:T(8,128)S(1)} %reshape.260, f32[2560,1280]{1,0:T(8,128)} %get-tuple-element.21, f32[2560,1280]{1,0:T(8,128)} %get-tuple-element.22), kind=kOutput, calls=%fused_computation.34 | convolution fusion | flops 7084441600 | bytes 28057600 | tf_op jit(solution)/shard_map/dot_general | solution.py:105
  81.7 0.6 reshape.261
  82.3 5.9 copy.168
  88.2 12.5 %gather_fusion = f32[640,18,5,2]{1,3,2,0:T(2,128)S(1)} fusion(f32[18,5,2,1280]{0,2,3,1:T(2,128)} %copy.168, s32[1024]{0:T(1024)S(1)} %get-tuple-element.24), kind=kCustom, calls=%fused_computation | custom fusion | bytes 924160 | tf_op jit(solution)/shard_map/gather | solution.py:112
  100.7 13.6 %gather_fusion.1 = f32[640,18,5,2]{1,3,2,0:T(2,128)} fusion(f32[18,5,2,1280]{0,2,3,1:T(2,128)} %copy.168, s32[1024]{0:T(1024)S(1)} %get-tuple-element.23), kind=kCustom, calls=%fused_computation.1 | custom fusion | bytes 924160 | tf_op jit(solution)/shard_map/gather | solution.py:112
  114.3 8.7 fusion.46
  123.0 10.4 %reshape.309 = f32[8,1,28800]{2,1,0:T(1,128)} reshape(f32[640,5,4,18]{3,2,1,0:T(4,128)} %fusion.46) | data formatting | bytes 1843200
  133.4 5.8 all-to-all-start
  139.6 0.9 iota_compare_fusion
  140.5 12.1 %all-to-all-done = f32[8,1,28800]{2,1,0:T(1,128)S(1)} async-done(((f32[8,1,28800]{2,1,0:T(1,128)}), f32[8,1,28800]{2,1,0:T(1,128)S(1)}, u32[]{:S(2)}, u32[]{:S(2)}) %all-to-all-start) | async-done | bytes 921632 | tf_op jit(solution)/shard_map/all_to_all | solution.py:113
  153.2 2.9 reduce
  156.1 11.8 %reshape.310 = f32[640,5,4,18]{3,2,1,0:T(4,128)} reshape(f32[8,28800]{1,0:T(8,128)S(1)} %reduce) | data formatting | bytes 1843200
  167.9 6.7 copy.170
  174.6 0.6 fusion.45
  175.2 1.5 copy.208
  176.7 2.7 copy.207
  179.4 22.9 %fusion.10 = f32[80,18,2,1408]{3,1,2,0:T(8,128)} fusion(f32[18,40,2,80]{1,0,2,3:T(8,128)S(1)} %copy.208, f32[80,40,1408]{2,1,0:T(8,128)} %param.11), kind=kOutput, calls=%fused_computation.17 | convolution fusion | flops 1946419200 | bytes 34703360 | tf_op jit(solution)/shard_map/plk,flrp->kpfr/dot_general | solution.py:32
  202.3 29.9 %fusion.2 = f32[1408,80,18,2]{0,2,3,1:T(8,128)} fusion(f32[80,18,2,1408]{3,1,2,0:T(8,128)} %fusion.10, f32[18,40,2,80]{1,0,2,3:T(8,128)} %copy.207, f32[80,40,1408]{2,1,0:T(8,128)} %param.11, pred[1408,80]{0,1:T(8,128)(4,1)S(1)} %copy-done.2, pred[1408,80]{0,1:T(8,128)(4,1)S(1)} %copy-done.3), kind=kOutput, calls=%fused_computation.8 | convolution fusion | flops 1954529280 | bytes 51148800 | tf_op jit(solution)/shard_map/plk,flrp->kpfr/dot_general | solution.py:29
  232.2 23.8 %copy.173 = f32[1408,80,18,2]{0,3,2,1:T(2,128)} copy(f32[1408,80,18,2]{0,2,3,1:T(8,128)} %fusion.2) | data formatting | bytes 32440320 | tf_op jit(solution)/shard_map/jit(_where)/select_n | solution.py:35
  256.0 19.9 %reshape.262 = f32[1408,2880]{0,1:T(8,128)} reshape(f32[1408,80,18,2]{0,3,2,1:T(2,128)} %copy.173) | data formatting | bytes 32440320 | tf_op jit(solution)/shard_map/reshape | solution.py:123
  276.0 0.5 copy-done.10
  276.5 0.6 dynamic-slice
  278.0 194.2 %all-reduce.3.cloned.1.call-done = f32[1408,2880]{0,1:T(8,128)} async-done(((f32[1408,2880]{0,1:T(8,128)}), f32[1408,2880]{0,1:T(8,128)}) %all-reduce.3.cloned.1.call-update) | async-done | bytes 16220176
  472.2 2.3 constant_dynamic-slice_fusion
  475.0 0.7 fusion.28
  475.8 0.7 fusion.27
  476.5 0.7 fusion.36
  477.4 0.7 fusion.30
  478.8 2.4 copy.182
  481.3 153.2 %all-gather.2.cloned.1.call-done = f32[1408,80,18,2]{1,3,2,0:T(2,128)} async-done(((f32[88,80,18,2]{1,3,2,0:T(2,128)}), f32[1408,80,18,2]{1,3,2,0:T(2,128)}) %all-gather.2.cloned.1.call-update) | async-done | bytes 16220176 | tf_op jit(solution)/shard_map/all_gather | solution.py:144
  634.5 33.9 %copy.183 = f32[1408,80,18,2]{0,2,3,1:T(8,128)} copy(f32[1408,80,18,2]{1,3,2,0:T(2,128)} %all-gather.2.cloned.1.call-done) | data formatting | bytes 32440320 | tf_op jit(solution)/shard_map/all_gather | solution.py:144
  668.4 25.7 %fusion.5 = f32[80,18,2,40]{3,1,2,0:T(8,128)S(1)} fusion(f32[1408,80,18,2]{0,2,3,1:T(8,128)} %copy.183, f32[80,40,1408]{2,1,0:T(8,128)} %param.11, pred[1408,80]{0,1:T(8,128)(4,1)S(1)} %copy-done.3), kind=kOutput, calls=%fused_computation.11 | convolution fusion | flops 1950474240 | bytes 34816000 | tf_op jit(solution)/shard_map/plk,kpfr->flrp/dot_general | solution.py:81
  694.1 27.9 %fusion.3 = f32[80,18,2,40]{3,1,2,0:T(8,128)} fusion(f32[1408,80,18,2]{0,2,3,1:T(8,128)} %copy.183, f32[80,40,1408]{2,1,0:T(8,128)} %param.11, pred[1408,80]{0,1:T(8,128)(4,1)S(1)} %copy-done.2), kind=kOutput, calls=%fused_computation.9 | convolution fusion | flops 1950474240 | bytes 34816000 | tf_op jit(solution)/shard_map/plk,kpfr->flrp/dot_general | solution.py:87
  722.0 0.7 copy.184
  722.7 2.1 copy.186
  725.4 23.0 %all_to_all.36 = f32[18,40,4,80]{3,2,0,1:T(4,128)S(1)} all-to-all(f32[18,40,4,80]{3,2,0,1:T(4,128)S(1)} %copy.187), channel_id=1, replica_groups=mesh['lat'=16,'wave'=8] {'wave'}, dimensions={1} | all-to-all | bytes 1843200 | tf_op jit(solution)/shard_map/all_to_all | solution.py:151
  748.8 0.8 all_to_all.33
  749.6 1.1 slice_bitcast_fusion
  750.7 3.5 copy.190
  754.2 3.9 copy.191
  758.1 4.3 broadcast_in_dim.50
  762.4 81.0 %scatter_fusion = f32[18,5,2,1280]{0,2,3,1:T(2,128)} fusion(f32[18,5,2,1280]{0,2,3,1:T(2,128)} %broadcast_in_dim.50, s32[640]{0:T(1024)S(1)} %get-tuple-element.15, f32[640,18,5,2]{1,3,2,0:T(2,128)} %copy.190), kind=kCustom, calls=%fused_computation.2 | custom fusion | bytes 1384960 | tf_op jit(solution)/shard_map/scatter | solution.py:153
  843.4 73.0 %scatter_fusion.1 = f32[18,5,2,1280]{0,2,3,1:T(2,128)} fusion(f32[18,5,2,1280]{0,2,3,1:T(2,128)} %scatter_fusion, s32[640]{0:T(1024)S(1)} %get-tuple-element.14, f32[640,18,5,2]{1,3,2,0:T(2,128)S(1)} %copy.191), kind=kCustom, calls=%fused_computation.3 | custom fusion | bytes 1384960 | tf_op jit(solution)/shard_map/scatter | solution.py:154
  916.4 7.1 copy.192
  923.5 0.7 dot_general.44
  924.2 34.2 %fusion = f32[3,6,5,2560]{3,1,2,0:T(8,128)} fusion(f32[2560,1280]{1,0:T(8,128)} %get-tuple-element.21, f32[2560,1280]{1,0:T(8,128)} %get-tuple-element.22, f32[3,6,5,2560]{3,1,0,2:T(8,128)S(1)} %dot_general.44), kind=kOutput, calls=%fused_computation.5 | convolution fusion | flops 7084441600 | bytes 28057600 | tf_op jit(solution)/shard_map/dot_general | solution.py:155
  (41 shorter events, 3.6 us)
Async XLA Ops:
  6.5 468.5 %copy-start = (f32[6,6]{1,0:T(8,128)S(1)}, f32[6,6]{1,0:T(8,128)}, u32[]{:S(2)}) copy-start(f32[6,6]{1,0:T(8,128)} %param.17) | copy-start | bytes 436
  6.5 55.2 %copy-start.1 = (f32[3,6,5,2560]{3,1,2,0:T(8,128)S(1)}, f32[3,6,5,2560]{3,1,2,0:T(8,128)}, u32[]{:S(2)}) copy-start(f32[3,6,5,2560]{3,1,2,0:T(8,128)} %param.9) | copy-start | bytes 2764804
  62.5 25.7 %copy-start.4 = (s32[640]{0:T(1024)S(1)}, s32[640]{0:T(1024)}, u32[]{:S(2)}) copy-start(s32[640]{0:T(1024)} %param.10) | copy-start | bytes 7684
  133.4 19.2 %all-to-all-start = ((f32[8,1,28800]{2,1,0:T(1,128)}), f32[8,1,28800]{2,1,0:T(1,128)S(1)}, u32[]{:S(2)}, u32[]{:S(2)}) async-start(f32[8,1,28800]{2,1,0:T(1,128)} %reshape.309), calls=%async_computation | async-start | bytes 1843200 | tf_op jit(solution)/shard_map/all_to_all | solution.py:113
  139.3 333.0 %all-reduce.3.cloned.1.call-start = ((), (), s32[]{:S(2)}) async-start(), calls=%async_computation.3 | async-start | bytes 32440320
  179.4 22.9 %copy-start.2 = (pred[1408,80]{0,1:T(8,128)(4,1)S(1)}, pred[1408,80]{0,1:T(8,128)(4,1)}, u32[]{:S(2)}) copy-start(pred[1408,80]{0,1:T(8,128)(4,1)} %get-tuple-element.20) | copy-start | bytes 337924
  179.4 22.9 %copy-start.3 = (pred[1408,80]{0,1:T(8,128)(4,1)S(1)}, pred[1408,80]{0,1:T(8,128)(4,1)}, u32[]{:S(2)}) copy-start(pred[1408,80]{0,1:T(8,128)(4,1)} %get-tuple-element.19) | copy-start | bytes 337924
  275.9 0.7 copy-start.10
  275.9 2.0 copy-start.7
  275.9 199.9 %copy-start.9 = (f32[6,6]{1,0:T(8,128)S(1)}, f32[6,6]{1,0:T(8,128)}, u32[]{:S(2)}) copy-start(f32[6,6]{1,0:T(8,128)} %param.13) | copy-start | bytes 436
  275.9 200.6 %copy-start.5 = (f32[6,6]{1,0:T(8,128)S(1)}, f32[6,6]{1,0:T(8,128)}, u32[]{:S(2)}) copy-start(f32[6,6]{1,0:T(8,128)} %param.14) | copy-start | bytes 436
  275.9 201.4 %copy-start.6 = (f32[6,6]{1,0:T(8,128)S(1)}, f32[6,6]{1,0:T(8,128)}, u32[]{:S(2)}) copy-start(f32[6,6]{1,0:T(8,128)} %param.16) | copy-start | bytes 436
  275.9 358.5 %all-gather.2.cloned.1.call-start = ((), (), s32[]{:S(2)}) async-start(), calls=%async_computation.2 | async-start | bytes 27574272 | tf_op jit(solution)/shard_map/all_gather | solution.py:144
  694.1 30.7 %copy-start.8 = (f32[40]{0:T(128)S(1)}, f32[40]{0:T(128)}, u32[]{:S(2)}) copy-start(f32[40]{0:T(128)} %param.12) | copy-start | bytes 484
Sparse Core Ops, SparseCore 0:
  276.1 196.1 all-reduce.2
  481.4 153.0 all-gather.1
where the time goes:
time: 979 us; the launch traced here: 966 us
  waiting for transfers between devices  360 us (37%)
  local copies, waits for them, and re-layouts  331 us (34%)
  matrix products  163 us (17%)
  other arithmetic  68.6 us (7%)
  blocking collectives  23 us (2%)
  between operations  14.8 us (2%)
    unnamed x3, waiting for transfers between devices  194 us
    all_gather x1, waiting for transfers between devices, per_device(): lax.all_gather(harmonic_coefficient_arrays, 'lat', axis=0, tiled=True)  153 us
    scatter x1, local copies, waits for them, and re-layouts, per_device(): spectral = spectral.at[..., owner].set(returned[:, :, 0:2, :])  81 us
    scatter x2, local copies, waits for them, and re-layouts, per_device(): spectral.at[..., truncation - 1 - owner].set(returned[:, :, 2:4, :])  80 us
    mul x1, other arithmetic, fourier_table(): -jnp.sin(phases) * factor  55.2 us
    dot_general x1, matrix products, per_device(): lax.dot_general(spectral.reshape(width * lat_rows, 2 * truncation), dft_t...  34.2 us
    all_gather x1, local copies, waits for them, and re-layouts, per_device(): lax.all_gather(harmonic_coefficient_arrays, 'lat', axis=0, tiled=True)  33.9 us
    unnamed x29, local copies, waits for them, and re-layouts  30.4 us
  transfers between devices with their start and end apart: 3, of which 3 were waited for; matrix products, arithmetic and copies ran while one was open for 0% of the time, Pallas kernels for 0%

commit v1 on v0

v1 whole, which is shorter than its diff:
```python
import math

import jax
import jax.numpy as jnp
import numpy as np
from jax import lax
from jax.experimental import pallas as pl
from jax.experimental.pallas import tpu as pltpu
from jax.sharding import Mesh, PartitionSpec as P

NLON = 2560
NM = 1280
PAIRS = 640
LAT = 640
PACK = 1408
FL = 18
ROWS = 5
N1 = 20
N2 = 128
HALF = 40
BF = jnp.bfloat16
F32 = jnp.float32
CHUNKS = ((0, 10),)
VMEM_BYTES = 40 * 1024 * 1024


def split(x):
    high = x.astype(BF)
    return high, (x - high.astype(F32)).astype(BF)


def dot3(x, weight_high, weight_low, dims):
    high, low = split(x)
    out = lax.dot_general(high, weight_high, dims, preferred_element_type=F32)
    out += lax.dot_general(low, weight_high, dims, preferred_element_type=F32)
    return out + lax.dot_general(high, weight_low, dims, preferred_element_type=F32)


NN = (((1,), (0,)), ((), ()))
NT = (((1,), (1,)), ((), ()))


def constant_tables():
    scale = math.sqrt(2.0 / NLON)
    wave1 = np.arange(N1)[:, None]
    lon2 = np.arange(N2)[None, :]
    turn = 2.0 * np.pi * ((wave1 * lon2) % NLON) / NLON
    twiddle = np.stack([np.cos(turn), np.sin(turn)]).astype(np.float32)
    angle = 2.0 * np.pi * ((np.arange(N2)[:, None] * np.arange(64)[None, :]) % N2) / N2
    cos, sin = np.cos(angle) * scale, np.sin(angle) * scale
    zero = np.zeros_like(cos)
    forward = np.concatenate(
        [
            np.concatenate([cos, zero, -sin, zero], 1),
            np.concatenate([sin, zero, cos, zero], 1),
            np.concatenate([zero, cos, zero, -sin], 1),
            np.concatenate([zero, sin, zero, cos], 1),
        ],
        0,
    ).astype(np.float32)
    backward = np.concatenate(
        [
            np.concatenate([cos.T, sin.T, zero.T, zero.T], 1),
            np.concatenate([zero.T, zero.T, cos.T, sin.T], 1),
            np.concatenate([-sin.T, cos.T, zero.T, zero.T], 1),
            np.concatenate([zero.T, zero.T, -sin.T, cos.T], 1),
        ],
        0,
    ).astype(np.float32)

    def parts(table):
        high = table.astype(jnp.bfloat16)
        return high, (table - high.astype(np.float32)).astype(jnp.bfloat16)

    return twiddle, parts(forward), parts(backward)


def lane_waves():
    lane = lax.broadcasted_iota(jnp.int32, (1, NM), 1)
    return 2 * (lane // N2) + (lane % N2) // 64 + N1 * (lane % 64)


def one_hot(owner_ref, block, rows):
    column = owner_ref[pl.ds(pl.multiple_of(block * rows, rows), rows), 0:1]
    waves = lane_waves()
    second = jnp.where(NM - 1 - column == waves, 1.0, 0.0).astype(BF)
    first = jnp.where(column == waves, 1.0, 0.0).astype(BF)
    return jnp.concatenate([second, first], axis=0)


def fourier_kernel(grid_ref, owner_ref, twiddle_ref, high_ref, low_ref, send_ref, stage_ref, wide_ref):
    for r in range(ROWS):
        tiles = [grid_ref[:, r, N2 * x1 : N2 * (x1 + 1)] for x1 in range(N1)]
        sums = [tiles[x1] + tiles[x1 + 10] for x1 in range(10)]
        differences = [tiles[x1] - tiles[x1 + 10] for x1 in range(10)]
        for m1 in range(11):
            source = sums if m1 % 2 == 0 else differences
            real, imag = source[0], None
            for x1 in range(1, 10):
                turn = 2.0 * math.pi * ((m1 * x1) % N1) / N1
                cos, sin = math.cos(turn), math.sin(turn)
                real = real + source[x1] * cos
                if m1 % 10:
                    term = source[x1] * (-sin)
                    imag = term if imag is None else imag + term
            if imag is None:
                imag = jnp.zeros_like(real)
            for wave, sign in ((m1, 1.0), (N1 - m1, -1.0)):
                if wave in (m1, N1) and sign < 0:
                    continue
                cos = twiddle_ref[0, wave : wave + 1, :]
                sin = twiddle_ref[1, wave : wave + 1, :]
                rotated_real = real * cos + (sign * imag) * sin
                rotated_imag = (sign * imag) * cos - real * sin
                base = (wave % 2) * 256
                stage_ref[wave // 2, r * 24 : r * 24 + FL, base : base + N2] = rotated_real
                stage_ref[wave // 2, r * 24 : r * 24 + FL, base + N2 : base + 256] = rotated_imag
    wide_ref[...] = jnp.zeros_like(wide_ref)
    for t in range(N1 // 2):
        out = dot3(stage_ref[t], high_ref[...], low_ref[...], NN)
        for r in range(ROWS):
            rows = out[r * 24 : r * 24 + FL]
            both = jnp.concatenate([rows[:, :N2], rows[:, N2:]], axis=0)
            wide_ref[r * 40 : r * 40 + 36, t * N2 : (t + 1) * N2] = both
    high, low = split(wide_ref[...])

    def block_step(block, carry):
        picks = one_hot(owner_ref, block, 160)
        out = lax.dot_general(picks, high, NT, preferred_element_type=F32)
        out += lax.dot_general(picks, low, NT, preferred_element_type=F32)
        for r in range(ROWS):
            lanes = out[:, r * 40 : (r + 1) * 40]
            tile = jnp.concatenate([lanes[:160], lanes[160:], jnp.zeros((160, 48), F32)], axis=1)
            for w in range(2):
                for c in range(2):
                    start = w * 80 + c * 40
                    send_ref[c * 8 + block * 2 + w, r] = tile[start : start + 40]
        return carry

    lax.fori_loop(0, 4, block_step, 0)


def inverse_kernel(got_ref, owner_ref, weight_ref, place_ref, twiddle_ref, high_ref, low_ref, out_ref, stage_ref, wide_ref):
    wide_ref[...] = jnp.zeros_like(wide_ref)
    wave = place_ref[1]

    def block_step(block, carry):
        picks = one_hot(owner_ref, block, 160)
        seconds, firsts = [], []
        for r in range(ROWS):
            pieces = [got_ref[c * 8 + block * 2 + w, r] for w in range(2) for c in range(2)]
            tile = jnp.concatenate(pieces, axis=0) * weight_ref[wave * ROWS + r]
            seconds.append(tile[:, 0:40])
            firsts.append(tile[:, 40:80])
        pad = [jnp.zeros((160, 56), F32)]
        both = jnp.concatenate(
            [jnp.concatenate(seconds + pad, axis=1), jnp.concatenate(firsts + pad, axis=1)], axis=0
        )
        high, low = split(both.T)
        out = lax.dot_general(high, picks, NN, preferred_element_type=F32)
        out += lax.dot_general(low, picks, NN, preferred_element_type=F32)
        wide_ref[...] += out
        return carry

    lax.fori_loop(0, 4, block_step, 0)
    for t in range(N1 // 2):
        rows = []
        for r in range(ROWS):
            block = wide_ref[r * 40 : (r + 1) * 40, t * N2 : (t + 1) * N2]
            real = jnp.concatenate([block[:FL], jnp.zeros((6, N2), F32)], axis=0)
            imag = jnp.concatenate([block[FL : 2 * FL], jnp.zeros((6, N2), F32)], axis=0)
            rows.append(jnp.concatenate([real, imag], axis=1))
        out = dot3(jnp.concatenate(rows, axis=0), high_ref[...], low_ref[...], NN)
        for odd in range(2):
            m1 = 2 * t + odd
            real = out[:, odd * 256 : odd * 256 + N2]
            imag = out[:, odd * 256 + N2 : odd * 256 + 256]
            cos = twiddle_ref[0, m1 : m1 + 1, :]
            sin = twiddle_ref[1, m1 : m1 + 1, :]
            stage_ref[m1, :, :N2] = real * cos - imag * sin
            stage_ref[m1, :, N2:] = real * sin + imag * cos
    for r in range(ROWS):
        rows = slice(r * 24, (r + 1) * 24)
        zero, ten = stage_ref[0, rows, :N2], stage_ref[10, rows, :N2]
        sums, gaps = [None], [None]
        for m in range(1, 10):
            sums.append(stage_ref[m, rows, :N2] + stage_ref[N1 - m, rows, :N2])
            gaps.append(stage_ref[m, rows, N2:] - stage_ref[N1 - m, rows, N2:])
        for x1 in range(10):
            even = zero + ten if x1 % 2 == 0 else zero - ten
            odd = jnp.zeros_like(zero)
            for m in range(1, 10):
                turn = 2.0 * math.pi * ((m * x1) % N1) / N1
                term = sums[m] * math.cos(turn) - gaps[m] * math.sin(turn)
                if m % 2 == 0:
                    even = even + term
                else:
                    odd = odd + term
            out_ref[:, r, x1 * N2 : (x1 + 1) * N2] = (even + odd)[:FL]
            out_ref[:, r, (x1 + 10) * N2 : (x1 + 11) * N2] = (even - odd)[:FL]


def spectra_kernel(start, count, place_ref, owner_ref, own_ref, other_ref, four_ref, out_ref):
    target, step = pl.program_id(0), pl.program_id(1)
    core, wave = place_ref[0], place_ref[1]
    extra = count * 36

    @pl.when(step == 0)
    def _():
        out_ref[0, extra : extra + 8, :] = jnp.zeros((8, NM), F32)

    lane = lax.broadcasted_iota(jnp.int32, (1, NM), 1)
    narrow = lax.broadcasted_iota(jnp.int32, (1, N2), 1)
    kept = []
    for i in range(2):
        pair = target * 10 + start + 2 * step + i
        first_wave = owner_ref[wave * 80 + core * HALF + pair]
        mine = four_ref[pl.ds(core * 1600 + pair, HALF, stride=HALF), :]
        theirs = four_ref[pl.ds((1 - core) * 1600 + pair, HALF, stride=HALF), :]
        four = jnp.concatenate([mine, theirs], axis=0)
        four_high = four.astype(BF).astype(F32)
        left = jnp.concatenate([four_high, four_high, four - four_high], axis=0).T
        table = jnp.concatenate([own_ref[i], other_ref[i]], axis=0)
        main = table[:, :NM]
        main_high = main.astype(BF).astype(F32)
        right = jnp.concatenate([main_high, main - main_high, main_high], axis=0)
        both = lax.dot_general(left[:80].astype(BF), right.astype(BF), NN, preferred_element_type=F32)
        kept.append(jnp.where(lane < NM - first_wave, both[40:80], both[0:40])[:36])
        last = jnp.sum(table[:, NM : NM + 1] * four, axis=0, keepdims=True)
        spot = pl.multiple_of((2 * step + i) * N2, N2)
        out_ref[0, extra : extra + 1, pl.ds(spot, N2)] = jnp.where(narrow < 36, last, 0.0)
    out_ref[0, pl.ds(pl.multiple_of(step * 72, 8), 72), :] = jnp.concatenate(kept, axis=0)


def implicit_rows(load, degree, modes_e, modes_f, rates, height, heating):
    q = degree * (degree + 1.0) / float(NM * (NM + 1))
    rotation = 1.0 / (1.0 + 4.0 * q * q)
    damping = [1.0 / (1.0 + 4.0 * q * rates[i]) for i in range(6)]
    out = []
    for part in range(2):
        base = part * FL
        d = [load(base + 6 + l) for l in range(6)]
        t = [load(base + 12 + l) for l in range(6)]
        forced = []
        for l in range(6):
            total = d[l]
            for h in range(6):
                total = total - heating[h * 6 + l] * t[h]
            forced.append(total)
        modal = []
        for i in range(6):
            total = modes_e[i] * forced[0]
            for h in range(1, 6):
                total = total + modes_e[h * 6 + i] * forced[h]
            modal.append(total * damping[i])
        spread = []
        for l in range(6):
            total = modes_f[l] * modal[0]
            for i in range(1, 6):
                total = total + modes_f[i * 6 + l] * modal[i]
            spread.append(total)
        out += [load(base + l) * rotation for l in range(6)]
        out += spread
        for l in range(6):
            total = height[l] * spread[0]
            for h in range(1, 6):
                total = total + height[h * 6 + l] * spread[h]
            out.append(t[l] - q * total)
    return out


def implicit_kernel(start, count, place_ref, owner_ref, e_ref, f_ref, rate_ref, height_ref, heat_ref, x_ref, y_ref, out_ref):
    core, wave, z = place_ref[0], place_ref[1], place_ref[2]
    matrices = [[ref[i] for i in range(36)] for ref in (e_ref, f_ref)]
    rates = [rate_ref[i] for i in range(6)]
    heights = [[ref[i] for i in range(36)] for ref in (height_ref, heat_ref)]
    arguments = (matrices[0], matrices[1], rates, heights[0], heights[1])
    row = lax.broadcasted_iota(jnp.int32, (count, 1), 0)
    first_wave = jnp.zeros((count, 1), jnp.int32)
    for i in range(count):
        value = owner_ref[wave * 80 + core * HALF + z * 10 + start + i]
        first_wave = jnp.where(row == i, value, first_wave)

    tile = pl.program_id(0)
    packed = tile * N2 + lax.broadcasted_iota(jnp.int32, (count, N2), 1)
    degree = jnp.where(packed < NM - first_wave, first_wave + packed, packed - 1).astype(F32)

    def load(j):
        spot = pl.ds(j, count, stride=36)
        return x_ref[spot, :] + y_ref[spot, :]

    for j, value in enumerate(implicit_rows(load, degree, *arguments)):
        out_ref[pl.ds(j, count, stride=36), :] = value
    extra = count * 36
    line = x_ref[extra : extra + 1, :] + y_ref[extra : extra + 1, :]
    flipped = jnp.broadcast_to(line, (8, N2)).T
    degree = jnp.full((1, 8), NM - 1.0, F32)
    values = implicit_rows(lambda j: flipped[j : j + 1], degree, *arguments)
    values.append(jnp.zeros((N2 - 36, 8), F32))
    out_ref[extra : extra + 8, :] = jnp.concatenate(values, axis=0).T


def grid_rows_kernel(start, count, place_ref, owner_ref, own_ref, other_ref, spec_ref, out_ref):
    target, step = pl.program_id(0), pl.program_id(1)
    core, wave = place_ref[0], place_ref[1]
    extra = count * 36
    lane = lax.broadcasted_iota(jnp.int32, (1, NM), 1)
    block = spec_ref[0, pl.ds(pl.multiple_of(step * 72, 8), 72), :]
    pad = jnp.zeros((4, NM), F32)
    for i in range(2):
        pair = target * 10 + start + 2 * step + i
        first_wave = owner_ref[wave * 80 + core * HALF + pair]
        values = jnp.concatenate([block[i * 36 : i * 36 + 36], pad], axis=0)
        is_first = lane < NM - first_wave
        both = jnp.concatenate(
            [jnp.where(is_first, 0.0, values), jnp.where(is_first, values, 0.0)], axis=0
        )
        high, low = split(both)
        table = jnp.concatenate([own_ref[i], other_ref[i]], axis=0)
        back = dot3(table[:, :NM], high, low, NT)
        back = jnp.concatenate([back, jnp.zeros((80, 48), F32)], axis=1)
        spot = pl.multiple_of((2 * step + i) * N2, N2)
        last = spec_ref[0, extra : extra + 1, pl.ds(spot, N2)]
        back = back + table[:, NM : NM + 1] * last
        out_ref[pl.ds(core * 1600 + pair, HALF, stride=HALF), :] = back[:HALF]
        out_ref[pl.ds((1 - core) * 1600 + pair, HALF, stride=HALF), :] = back[HALF:]


def parameters():
    return pltpu.CompilerParams(vmem_limit_bytes=VMEM_BYTES)


def whole(space=pltpu.VMEM):
    return pl.BlockSpec(memory_space=space)


def cost(flops, size):
    return pl.CostEstimate(flops=int(flops), bytes_accessed=int(size), transcendentals=0)


def per_device(
    grad_grid, owner, legendre, lat_weights, modes_e, modes_f, rates, height_matrix, heating_matrix
):
    core, wave, z = lax.axis_index("core"), lax.axis_index("wave"), lax.axis_index("z")
    twiddle, forward, backward = constant_tables()
    smem = whole(pltpu.SMEM)
    place = jnp.stack([core, wave, z]).astype(jnp.int32)
    owner_column = jnp.broadcast_to(owner[:, None], (PAIRS, N2))

    away = lax.dynamic_slice(legendre, ((1 - core) * HALF, 0, 0), (HALF, HALF, PACK))
    other = lax.ppermute(away, "core", [(0, 1), (1, 0)])

    four = pl.pallas_call(
        fourier_kernel,
        out_shape=jax.ShapeDtypeStruct((16, ROWS, HALF, N2), F32),
        in_specs=[whole()] * 5,
        out_specs=whole(),
        scratch_shapes=[pltpu.VMEM((10, 120, 512), F32), pltpu.VMEM((208, NM), F32)],
        compiler_params=parameters(),
        cost_estimate=cost(4e9, 8e6),
        name="fourier",
    )(grad_grid.reshape(FL, ROWS, NLON), owner_column, twiddle, *forward)
    four = lax.all_to_all(four, ("core", "wave"), 0, 0, tiled=True).reshape(3200, N2)

    def table_specs(start):
        return [
            pl.BlockSpec(
                (2, HALF, PACK),
                lambda t, s, place, owner: (place[0] * 20 + t * 5 + start // 2 + s, 0, 0),
            ),
            pl.BlockSpec((2, HALF, PACK), lambda t, s, place, owner: (t * 5 + start // 2 + s, 0, 0)),
        ]

    results = []
    for start, count in CHUNKS:
        height = count * 36 + 8
        spectra = pl.pallas_call(
            lambda *refs: spectra_kernel(start, count, *refs),
            out_shape=jax.ShapeDtypeStruct((4, height, NM), F32),
            grid_spec=pltpu.PrefetchScalarGridSpec(
                num_scalar_prefetch=2,
                grid=(4, count // 2),
                in_specs=table_specs(start)
                + [pl.BlockSpec((3200, N2), lambda t, s, place, owner: (0, 0))],
                out_specs=pl.BlockSpec((1, height, NM), lambda t, s, place, owner: (t, 0, 0)),
            ),
            compiler_params=parameters(),
            cost_estimate=cost(2e9, 2e7),
            name="spectra",
        )(place, owner, legendre, other, four)
        mine = lax.psum_scatter(spectra, "z", scatter_dimension=0, tiled=True).reshape(height, NM)
        theirs = lax.ppermute(mine, "yh", [(0, 1), (1, 0)])
        updated = pl.pallas_call(
            lambda *refs: implicit_kernel(start, count, *refs),
            out_shape=jax.ShapeDtypeStruct((height, NM), F32),
            grid=(10,),
            in_specs=[smem] * 7 + [pl.BlockSpec((height, N2), lambda t: (0, t))] * 2,
            out_specs=pl.BlockSpec((height, N2), lambda t: (0, t)),
            compiler_params=parameters(),
            cost_estimate=cost(1e8, 6e6),
            name="implicit",
        )(
            place,
            owner,
            modes_e.reshape(36),
            modes_f.reshape(36),
            rates,
            height_matrix.reshape(36),
            heating_matrix.reshape(36),
            mine,
            theirs,
        )
        gathered = lax.all_gather(updated[None], "z", axis=0, tiled=True)
        results.append(
            pl.pallas_call(
                lambda *refs: grid_rows_kernel(start, count, *refs),
                out_shape=jax.ShapeDtypeStruct((3200, N2), F32),
                grid_spec=pltpu.PrefetchScalarGridSpec(
                    num_scalar_prefetch=2,
                    grid=(4, count // 2),
                    in_specs=table_specs(start)
                    + [pl.BlockSpec((1, height, NM), lambda t, s, place, owner: (t, 0, 0))],
                    out_specs=pl.BlockSpec((3200, N2), lambda t, s, place, owner: (0, 0)),
                ),
                compiler_params=parameters(),
                cost_estimate=cost(3e9, 2e7),
                name="grid_rows",
            )(place, owner, legendre, other, gathered)
        )
    rows = results[0].reshape(16, ROWS, HALF, N2)
    rows = lax.all_to_all(rows, ("core", "wave"), 0, 0, tiled=True)
    out = pl.pallas_call(
        inverse_kernel,
        out_shape=jax.ShapeDtypeStruct((FL, ROWS, NLON), F32),
        in_specs=[whole()] * 2 + [smem] * 2 + [whole()] * 3,
        out_specs=whole(),
        scratch_shapes=[pltpu.VMEM((N1, 120, 256), F32), pltpu.VMEM((256, NM), F32)],
        compiler_params=parameters(),
        cost_estimate=cost(4e9, 8e6),
        name="inverse",
    )(rows, owner_column, lat_weights, place, twiddle, *backward)
    return out.reshape(3, 6, ROWS, NLON)


def solution(mesh):
    fine = Mesh(mesh.devices.reshape(2, 4, 2, 8), ("yh", "z", "core", "wave"))
    lat = ("yh", "z", "core")
    rows = P(None, None, lat + ("wave",), None)
    in_specs = (rows, P(), P("wave", lat, None), P(lat), P(), P(), P(), P(), P())
    return jax.shard_map(
        per_device, mesh=fine, in_specs=in_specs, out_specs=rows, check_vma=False
    )
```

time: 979 us -> 348 us (0.36); the launches traced: 966 us -> 347 us
  local copies, waits for them, and re-layouts: 331 us -> 18 us
  matrix products: 163 us -> 0 us
  waiting for transfers between devices: 360 us -> 216 us
  other arithmetic: 68.6 us -> 0.08 us
  Pallas kernels: 0 us -> 61.6 us
    unnamed x3 -> x2, waiting for transfers between devices: 194 us -> 0.03 us
    dot_general x10 -> x0, matrix products: 163 us -> none  [the longest x1 34.2 us: per_device(): lax.dot_general(spectral.reshape(width * lat_rows, 2 * truncation), dft_t...]
    scatter x3 -> x0, local copies, waits for them, and re-layouts: 161 us -> none  [the longest x1 81 us: per_device(): spectral = spectral.at[..., owner].set(returned[:, :, 0:2, :])]
    all_gather x1, waiting for transfers between devices: 153 us -> 76.8 us  [per_device(): gathered = lax.all_gather(updated[None], 'z', axis=0, tiled=True)]
    reduce_scatter x0 -> x1, waiting for transfers between devices: none -> 74.9 us  [per_device(): lax.psum_scatter(spectra, 'z', scatter_dimension=0, tiled=True)]
    pallas_call x0 -> x5, Pallas kernels: none -> 61.6 us  [the longest x1 18.6 us: per_device(): pl.pallas_call(lambda *refs: grid_rows_kernel(start, count, *refs), out_s...]
    mul x2 -> x0, other arithmetic: 55.4 us -> none  [the longest x1 55.2 us: fourier_table(): -jnp.sin(phases) * factor]
    ppermute x0 -> x2, waiting for transfers between devices: none -> 40.7 us  [the longest x1 40.7 us: per_device(): theirs = lax.ppermute(mine, 'yh', [(0, 1), (1, 0)])]
  transfers between devices with their start and end apart: 3 -> 5, of which waited for: 3 -> 4; matrix products, arithmetic and copies ran while one was open for 0% -> 0% of each run, Pallas kernels for 0% -> 3%
where the time goes in v1:
time: 348 us; the launch traced here: 347 us
  waiting for transfers between devices  216 us (62%)
  Pallas kernels  61.6 us (18%)
  blocking collectives  28.2 us (8%)
  local copies, waits for them, and re-layouts  18 us (5%)
  between operations  13.5 us (4%)
  starting transfers between devices  9.95 us (3%)
    all_gather x1, waiting for transfers between devices, per_device(): gathered = lax.all_gather(updated[None], 'z', axis=0, tiled=True)  76.8 us
    reduce_scatter x1, waiting for transfers between devices, per_device(): lax.psum_scatter(spectra, 'z', scatter_dimension=0, tiled=True)  74.9 us
    ppermute x1, waiting for transfers between devices, per_device(): theirs = lax.ppermute(mine, 'yh', [(0, 1), (1, 0)])  40.7 us
    all_to_all x1, blocking collectives, per_device(): rows = lax.all_to_all(rows, ('core', 'wave'), 0, 0, tiled=True)  28.2 us
    all_to_all x1, waiting for transfers between devices, per_device(): lax.all_to_all(four, ('core', 'wave'), 0, 0, tiled=True).reshape(3200, N2)  23.8 us
    pallas_call x1, Pallas kernels, per_device(): pl.pallas_call(lambda *refs: grid_rows_kernel(start, count, *refs), out_s...  18.6 us
    pallas_call x1, Pallas kernels, per_device(): pl.pallas_call(lambda *refs: spectra_kernel(start, count, *refs), out_sha...  17.2 us
    pallas_call x1, Pallas kernels, per_device(): pl.pallas_call(fourier_kernel, out_shape=jax.ShapeDtypeStruct((16, ROWS,...  11.3 us
  transfers between devices with their start and end apart: 5, of which 4 were waited for; matrix products, arithmetic and copies ran while one was open for 0% of the time, Pallas kernels for 3%

profile of v1, /device:TPU:1, one launch (start us, length us, event | category | flops | bytes accessed | tf_op | source)
XLA Modules:
  0.0 347.5 jit_solution(9254774169867217556)
XLA Ops:
  6.5 7.8 %constant_dynamic-slice_fusion = f32[40,40,1408]{2,1,0:T(8,128)} fusion(f32[80,40,1408]{2,1,0:T(8,128)} %refs_2_.3, s32[]{:T(128)S(6)} %select_n.3), kind=kLoop, calls=%fused_computation.1 | loop fusion | bytes 18022404 | tf_op jit(solution)/shard_map/dynamic_slice | solution.py:350
  14.3 1.5 collective-permute-start
  15.8 0.0 copy-done.11
  15.8 0.5 copy.15
  16.4 0.0 copy-done.3
  16.4 0.1 broadcast_in_dim.4.owner_ref
  16.5 0.0 copy-done.8
  16.5 0.0 copy-done.9
  16.5 0.0 copy-done.10
  16.5 11.3 %fourier.1 = f32[16,5,40,128]{3,2,1,0:T(8,128)} custom-call(f32[18,5,2560]{2,1,0:T(8,128)S(1)} %bitcast.15, s32[640,128]{1,0:T(8,128)S(1)} %broadcast_in_dim.4.owner_ref, f32[2,20,128]{2,1,0:T(8,128)S(1)} %copy-done.10, bf16[512,256]{1,0:T(8,128)(2,1)S(1)} %copy-done.8, bf16[512,256]{1,0:T(8,128)(2,1)S(1)} %copy-done.9), custom_call_target="tpu_custom_call" | custom-call | flops 4000000000 | bytes 8000000 | tf_op jit(solution)/shard_map/fourier/pallas_call | solution.py:353
  27.8 5.6 %all-to-all-start = ((f32[16,5,40,128]{3,2,1,0:T(8,128)}), f32[16,5,40,128]{3,2,1,0:T(8,128)S(1)}, u32[]{:S(2)}, u32[]{:S(2)}) async-start(f32[16,5,40,128]{3,2,1,0:T(8,128)} %fourier.1), calls=%async_computation | async-start | bytes 3276800 | tf_op jit(solution)/shard_map/all_to_all | solution.py:363
  33.4 0.0 reduce-scatter.2.cloned.1.call-start
  33.5 0.1 pad_add_fusion.refs_0_.place_ref
  33.6 23.8 %all-to-all-done = f32[16,5,40,128]{3,2,1,0:T(8,128)S(1)} async-done(((f32[16,5,40,128]{3,2,1,0:T(8,128)}), f32[16,5,40,128]{3,2,1,0:T(8,128)S(1)}, u32[]{:S(2)}, u32[]{:S(2)}) %all-to-all-start) | async-done | bytes 1638432 | tf_op jit(solution)/shard_map/all_to_all | solution.py:363
  57.4 0.0 collective-permute-done.refs_3_
  57.4 17.2 %spectra.1 = f32[4,368,1280]{2,1,0:T(8,128)S(1)} custom-call(s32[3]{0:T(128)S(1)} %pad_add_fusion.refs_0_.place_ref, s32[640]{0:T(1024)S(1)} %copy-done.3, f32[80,40,1408]{2,1,0:T(8,128)} %refs_2_.3, f32[40,40,1408]{2,1,0:T(8,128)} %collective-permute-done.refs_3_, f32[3200,128]{1,0:T(8,128)S(1)} %bitcast.10), custom_call_target="tpu_custom_call" | custom-call | flops 2000000000 | bytes 20000000 | tf_op jit(solution)/shard_map/spectra/pallas_call | solution.py:377
  74.5 0.0 copy-start
  74.6 3.0 copy-done
  77.5 0.0 copy-start.4
  77.5 0.0 reduce-scatter.2.cloned.1.call-update
  77.6 0.0 all-gather.3.cloned.1.call-start
  77.6 74.9 %reduce-scatter.2.cloned.1.call-done = f32[1,368,1280]{2,1,0:T(8,128)} async-done(((f32[4,368,1280]{2,1,0:T(8,128)}), f32[1,368,1280]{2,1,0:T(8,128)}) %reduce-scatter.2.cloned.1.call-update) | async-done | bytes 1884176 | tf_op jit(solution)/shard_map/reduce_scatter | solution.py:391
  152.5 2.7 collective-permute-start.1
  155.3 0.0 copy-done.12
  155.3 0.1 reshape.28.refs_2_
  155.3 0.0 copy-done.13
  155.3 0.1 reshape.29.refs_3_
  155.4 0.0 copy-done.14
  155.4 0.1 reshape.30.refs_5_
  155.5 0.0 copy-done.15
  155.5 0.1 reshape.31.refs_6_
  155.6 40.7 %collective-permute-done.1.refs_8_ = f32[368,1280]{1,0:T(8,128)S(1)} collective-permute-done((f32[368,1280]{1,0:T(8,128)}, f32[368,1280]{1,0:T(8,128)S(1)}, u32[]{:S(2)}, u32[]{:S(2)}) %collective-permute-start.1) | collective-permute-done | bytes 1884192 | tf_op jit(solution)/shard_map/ppermute | solution.py:392
  196.2 0.0 copy-done.4
  196.3 1.5 copy-done.2
  197.8 6.8 %implicit.1 = f32[368,1280]{1,0:T(8,128)} custom-call(s32[3]{0:T(128)S(1)} %pad_add_fusion.refs_0_.place_ref, s32[640]{0:T(1024)S(1)} %copy-done.3, f32[36]{0:T(128)S(1)} %reshape.28.refs_2_, f32[36]{0:T(128)S(1)} %reshape.29.refs_3_, f32[6]{0:T(128)S(1)} %copy-done.4, f32[36]{0:T(128)S(1)} %reshape.30.refs_5_, f32[36]{0:T(128)S(1)} %reshape.31.refs_6_, ...), custom_call_target="tpu_custom_call" | custom-call | flops 100000000 | bytes 6000000 | tf_op jit(solution)/shard_map/implicit/pallas_call | solution.py:393
  204.6 0.0 all-gather.3.cloned.1.call-update
  204.6 76.8 %all-gather.3.cloned.1.call-done = f32[1472,1280]{1,0:T(8,128)} async-done(((f32[368,1280]{1,0:T(8,128)}), f32[1472,1280]{1,0:T(8,128)}) %all-gather.3.cloned.1.call-update) | async-done | bytes 7536656 | tf_op jit(solution)/shard_map/all_gather | solution.py:413
  281.4 3.1 copy-done.1
  284.5 18.6 %grid_rows.1 = f32[3200,128]{1,0:T(8,128)S(1)} custom-call(s32[3]{0:T(128)S(1)} %pad_add_fusion.refs_0_.place_ref, s32[640]{0:T(1024)S(1)} %copy-done.3, f32[80,40,1408]{2,1,0:T(8,128)} %refs_2_.3, f32[40,40,1408]{2,1,0:T(8,128)} %collective-permute-done.refs_3_, f32[4,368,1280]{2,1,0:T(8,128)S(1)} %bitcast.9), custom_call_target="tpu_custom_call" | custom-call | flops 3000000000 | bytes 20000000 | tf_op jit(solution)/shard_map/grid_rows/pallas_call | solution.py:415
  303.1 0.0 copy-start.5
  303.1 0.0 copy-start.6
  303.2 0.0 copy-start.7
  303.2 28.2 %all_to_all.10.got_ref = f32[16,5,40,128]{3,2,1,0:T(8,128)S(1)} all-to-all(f32[16,5,40,128]{3,2,1,0:T(8,128)S(1)} %bitcast.11), channel_id=1, replica_groups=mesh['yh'=2,'z'=4,'core'=2,'wave'=8] {'core','wave'}, dimensions={0} | all-to-all | bytes 3276800 | tf_op jit(solution)/shard_map/all_to_all | solution.py:431
  331.4 0.0 copy-done.5
  331.4 0.0 copy-done.6
  331.4 0.0 copy-done.7
  331.4 7.7 %inverse.1 = f32[18,5,2560]{2,1,0:T(8,128)S(1)} custom-call(f32[16,5,40,128]{3,2,1,0:T(8,128)S(1)} %all_to_all.10.got_ref, s32[640,128]{1,0:T(8,128)S(1)} %broadcast_in_dim.4.owner_ref, f32[40]{0:T(128)S(1)} %copy-done.5, s32[3]{0:T(128)S(1)} %pad_add_fusion.refs_0_.place_ref, f32[2,20,128]{2,1,0:T(8,128)S(1)} %copy-done.10, bf16[256,512]{1,0:T(8,128)(2,1)S(1)} %copy-done.6, ...), custom_call_target="tpu_custom_call" | custom-call | flops 4000000000 | bytes 8000000 | tf_op jit(solution)/shard_map/inverse/pallas_call | solution.py:432
  339.1 1.6 copy.16
  (11 shorter events, 0.0 us)
Async XLA Ops:
  6.5 9.3 %copy-start.11 = (f32[3,6,5,2560]{3,1,2,0:T(8,128)S(1)}, f32[3,6,5,2560]{3,1,2,0:T(8,128)}, u32[]{:S(2)}) copy-start(f32[3,6,5,2560]{3,1,2,0:T(8,128)} %param.14) | copy-start | bytes 2764804
  14.3 2.1 copy-start.3
  14.3 2.2 copy-start.8
  14.3 2.2 copy-start.9
  14.3 2.2 copy-start.10
  14.3 43.1 %collective-permute-start = (f32[40,40,1408]{2,1,0:T(8,128)}, f32[40,40,1408]{2,1,0:T(8,128)}, u32[]{:S(2)}, u32[]{:S(2)}) collective-permute-start(f32[40,40,1408]{2,1,0:T(8,128)} %constant_dynamic-slice_fusion), channel_id=1, source_target_pairs={{0,8},{8,0},{1,9},{9,1},{2,10},{10,2},{3,11},{11,3},{4,12},{12,4},... | collective-permute-start | bytes 27033608 | tf_op jit(solution)/shard_map/ppermute | solution.py:351
  27.8 29.6 %all-to-all-start = ((f32[16,5,40,128]{3,2,1,0:T(8,128)}), f32[16,5,40,128]{3,2,1,0:T(8,128)S(1)}, u32[]{:S(2)}, u32[]{:S(2)}) async-start(f32[16,5,40,128]{3,2,1,0:T(8,128)} %fourier.1), calls=%async_computation | async-start | bytes 3276800 | tf_op jit(solution)/shard_map/all_to_all | solution.py:363
  33.4 119.1 %reduce-scatter.2.cloned.1.call-start = ((), (), s32[]{:S(2)}) async-start(), calls=%async_computation.3 | async-start | bytes 9420800 | tf_op jit(solution)/shard_map/reduce_scatter | solution.py:391
  74.5 3.0 copy-start
  77.5 77.7 %copy-start.12 = (f32[6,6]{1,0:T(8,128)S(1)}, f32[6,6]{1,0:T(8,128)}, u32[]{:S(2)}) copy-start(f32[6,6]{1,0:T(8,128)} %param.18) | copy-start | bytes 436
  77.5 77.8 %copy-start.13 = (f32[6,6]{1,0:T(8,128)S(1)}, f32[6,6]{1,0:T(8,128)}, u32[]{:S(2)}) copy-start(f32[6,6]{1,0:T(8,128)} %param.19) | copy-start | bytes 436
  77.5 77.9 %copy-start.14 = (f32[6,6]{1,0:T(8,128)S(1)}, f32[6,6]{1,0:T(8,128)}, u32[]{:S(2)}) copy-start(f32[6,6]{1,0:T(8,128)} %param.21) | copy-start | bytes 436
  77.5 78.0 %copy-start.15 = (f32[6,6]{1,0:T(8,128)S(1)}, f32[6,6]{1,0:T(8,128)}, u32[]{:S(2)}) copy-start(f32[6,6]{1,0:T(8,128)} %param.22) | copy-start | bytes 436
  77.5 118.7 %copy-start.4 = (f32[6]{0:T(128)S(1)}, f32[6]{0:T(128)}, u32[]{:S(2)}) copy-start(f32[6]{0:T(128)} %refs_4_.1) | copy-start | bytes 76
  77.6 203.8 %all-gather.3.cloned.1.call-start = ((), (), s32[]{:S(2)}) async-start(), calls=%async_computation.4 | async-start | bytes 9420800 | tf_op jit(solution)/shard_map/all_gather | solution.py:413
  152.5 43.7 %collective-permute-start.1 = (f32[368,1280]{1,0:T(8,128)}, f32[368,1280]{1,0:T(8,128)S(1)}, u32[]{:S(2)}, u32[]{:S(2)}) collective-permute-start(f32[368,1280]{1,0:T(8,128)} %bitcast.12), channel_id=1, source_target_pairs={{0,64},{64,0},{1,65},{65,1},{2,66},{66,2},{3,67},{67,3},{4,68},{68... | collective-permute-start | bytes 5652488 | tf_op jit(solution)/shard_map/ppermute | solution.py:392
  196.3 1.5 copy-start.2
  281.4 3.1 copy-start.1
  303.1 28.2 %copy-start.5 = (f32[40]{0:T(128)S(1)}, f32[40]{0:T(128)}, u32[]{:S(2)}) copy-start(f32[40]{0:T(128)} %weight_ref.1) | copy-start | bytes 484
  303.1 28.2 %copy-start.6 = (bf16[256,512]{1,0:T(8,128)(2,1)S(1)}, bf16[256,512]{1,0:T(8,128)(2,1)}, u32[]{:S(2)}) copy-start(bf16[256,512]{1,0:T(8,128)(2,1)} %constant.35.clone.high_ref) | copy-start | bytes 786436
  303.2 28.2 %copy-start.7 = (bf16[256,512]{1,0:T(8,128)(2,1)S(1)}, bf16[256,512]{1,0:T(8,128)(2,1)}, u32[]{:S(2)}) copy-start(bf16[256,512]{1,0:T(8,128)(2,1)} %constant.36.clone.low_ref) | copy-start | bytes 786436
Sparse Core Ops, SparseCore 0:
  77.7 74.7 reduce-scatter.1
  204.7 76.5 all-gather.2

commit v2 on v1

--- a/solution.py
+++ b/solution.py
@@ -20,7 +20,10 @@
 HALF = 40
 BF = jnp.bfloat16
 F32 = jnp.float32
-CHUNKS = ((0, 10),)
+CHUNKS = ((0, 6), (6, 4))
+UP = [(i, (i + 1) % 4) for i in range(4)]
+DOWN = [(i, (i + 3) % 4) for i in range(4)]
+SWAP = [(0, 1), (1, 0)]
 VMEM_BYTES = 40 * 1024 * 1024
 
 
@@ -80,17 +83,40 @@
     return 2 * (lane // N2) + (lane % N2) // 64 + N1 * (lane % 64)
 
 
-def one_hot(owner_ref, block, rows):
-    column = owner_ref[pl.ds(pl.multiple_of(block * rows, rows), rows), 0:1]
+def one_hot(owner_ref, start, rows):
+    column = owner_ref[start : start + rows, 0:1]
     waves = lane_waves()
     second = jnp.where(NM - 1 - column == waves, 1.0, 0.0).astype(BF)
     first = jnp.where(column == waves, 1.0, 0.0).astype(BF)
     return jnp.concatenate([second, first], axis=0)
 
 
-def fourier_kernel(grid_ref, owner_ref, twiddle_ref, high_ref, low_ref, send_ref, stage_ref, wide_ref):
+def fourier_kernel(place_ref, grid_ref, owner_ref, twiddle_ref, high_ref, low_ref, table_ref, *refs):
+    parts = len(CHUNKS)
+    send_refs, away_refs = refs[:parts], refs[parts : 2 * parts]
+    stage_ref, wide_ref, half_ref, sem = refs[2 * parts :]
+    source = (1 - place_ref[0]) * HALF
+    fetches, copies = [], []
+    for k, (start, count) in enumerate(CHUNKS):
+        for z in range(4):
+            rows = pl.ds(4 * start + z * count, count)
+            fetches.append(
+                pltpu.make_async_copy(
+                    table_ref.at[pl.ds(source + z * 10 + start, count)],
+                    half_ref.at[rows],
+                    sem.at[4 * k + z],
+                )
+            )
+            fetches[-1].start()
+            copies.append(
+                pltpu.make_async_copy(
+                    half_ref.at[rows],
+                    away_refs[k].at[pl.ds(z * count, count)],
+                    sem.at[4 * parts + 4 * k + z],
+                )
+            )
     for r in range(ROWS):
-        tiles = [grid_ref[:, r, N2 * x1 : N2 * (x1 + 1)] for x1 in range(N1)]
+        tiles = [grid_ref[:, r, :, N2 * x1 : N2 * (x1 + 1)] for x1 in range(N1)]
         sums = [tiles[x1] + tiles[x1 + 10] for x1 in range(10)]
         differences = [tiles[x1] - tiles[x1 + 10] for x1 in range(10)]
         for m1 in range(11):
@@ -113,63 +139,76 @@
                 rotated_real = real * cos + (sign * imag) * sin
                 rotated_imag = (sign * imag) * cos - real * sin
                 base = (wave % 2) * 256
-                stage_ref[wave // 2, r * 24 : r * 24 + FL, base : base + N2] = rotated_real
-                stage_ref[wave // 2, r * 24 : r * 24 + FL, base + N2 : base + 256] = rotated_imag
+                rows = slice(3 * r, 3 * r + 3)
+                stage_ref[wave // 2, rows, 0:6, base : base + N2] = rotated_real
+                stage_ref[wave // 2, rows, 0:6, base + N2 : base + 256] = rotated_imag
+    for fetch, copy in zip(fetches, copies):
+        fetch.wait()
+        copy.start()
     wide_ref[...] = jnp.zeros_like(wide_ref)
     for t in range(N1 // 2):
-        out = dot3(stage_ref[t], high_ref[...], low_ref[...], NN)
+        out = dot3(stage_ref[t].reshape(120, 512), high_ref[...], low_ref[...], NN)
         for r in range(ROWS):
-            rows = out[r * 24 : r * 24 + FL]
-            both = jnp.concatenate([rows[:, :N2], rows[:, N2:]], axis=0)
+            rows = [out[r * 24 + f * 8 : r * 24 + f * 8 + 6] for f in range(3)]
+            both = [row[:, :N2] for row in rows] + [row[:, N2:] for row in rows]
+            both = jnp.concatenate(both, axis=0)
             wide_ref[r * 40 : r * 40 + 36, t * N2 : (t + 1) * N2] = both
     high, low = split(wide_ref[...])
 
-    def block_step(block, carry):
-        picks = one_hot(owner_ref, block, 160)
-        out = lax.dot_general(picks, high, NT, preferred_element_type=F32)
-        out += lax.dot_general(picks, low, NT, preferred_element_type=F32)
-        for r in range(ROWS):
-            lanes = out[:, r * 40 : (r + 1) * 40]
-            tile = jnp.concatenate([lanes[:160], lanes[160:], jnp.zeros((160, 48), F32)], axis=1)
-            for w in range(2):
-                for c in range(2):
-                    start = w * 80 + c * 40
-                    send_ref[c * 8 + block * 2 + w, r] = tile[start : start + 40]
-        return carry
-
-    lax.fori_loop(0, 4, block_step, 0)
-
-
-def inverse_kernel(got_ref, owner_ref, weight_ref, place_ref, twiddle_ref, high_ref, low_ref, out_ref, stage_ref, wide_ref):
-    wide_ref[...] = jnp.zeros_like(wide_ref)
+    for k, (start, count) in enumerate(CHUNKS):
+        group = 4 * count
+        for c in range(2):
+            picks = one_hot(owner_ref, 64 * start + c * 8 * group, 8 * group)
+            out = lax.dot_general(picks, high, NT, preferred_element_type=F32)
+            out += lax.dot_general(picks, low, NT, preferred_element_type=F32)
+            for r in range(ROWS):
+                lanes = out[:, r * 40 : (r + 1) * 40]
+                half = 8 * group
+                tile = [lanes[:half], lanes[half:], jnp.zeros((half, 48), F32)]
+                tile = jnp.concatenate(tile, axis=1)
+                for w in range(8):
+                    send_refs[k][c * 8 + w, r] = tile[w * group : (w + 1) * group]
+    for copy in copies:
+        copy.wait()
+
+
+def inverse_kernel(owner_ref, weight_ref, place_ref, twiddle_ref, high_ref, low_ref, *refs):
+    got_refs = refs[: len(CHUNKS)]
+    out_ref, stage_ref, wide_ref = refs[len(CHUNKS) :]
     wave = place_ref[1]
 
-    def block_step(block, carry):
-        picks = one_hot(owner_ref, block, 160)
-        seconds, firsts = [], []
-        for r in range(ROWS):
-            pieces = [got_ref[c * 8 + block * 2 + w, r] for w in range(2) for c in range(2)]
-            tile = jnp.concatenate(pieces, axis=0) * weight_ref[wave * ROWS + r]
-            seconds.append(tile[:, 0:40])
-            firsts.append(tile[:, 40:80])
-        pad = [jnp.zeros((160, 56), F32)]
-        both = jnp.concatenate(
-            [jnp.concatenate(seconds + pad, axis=1), jnp.concatenate(firsts + pad, axis=1)], axis=0
-        )
-        high, low = split(both.T)
-        out = lax.dot_general(high, picks, NN, preferred_element_type=F32)
-        out += lax.dot_general(low, picks, NN, preferred_element_type=F32)
-        wide_ref[...] += out
-        return carry
-
-    lax.fori_loop(0, 4, block_step, 0)
+    fresh = True
+    for k, (start, count) in enumerate(CHUNKS):
+        group = 4 * count
+        for c in range(2):
+            picks = one_hot(owner_ref, 64 * start + c * 8 * group, 8 * group)
+            seconds, firsts = [], []
+            for r in range(ROWS):
+                pieces = [got_refs[k][c * 8 + w, r] for w in range(8)]
+                tile = jnp.concatenate(pieces, axis=0) * weight_ref[wave * ROWS + r]
+                seconds.append(tile[:, 0:40])
+                firsts.append(tile[:, 40:80])
+            pad = [jnp.zeros((8 * group, 56), F32)]
+            both = [jnp.concatenate(part + pad, axis=1) for part in (seconds, firsts)]
+            high, low = split(jnp.concatenate(both, axis=0).T)
+            out = lax.dot_general(high, picks, NN, preferred_element_type=F32)
+            out += lax.dot_general(low, picks, NN, preferred_element_type=F32)
+            if fresh:
+                wide_ref[...] = out
+            else:
+                wide_ref[...] += out
+            fresh = False
     for t in range(N1 // 2):
         rows = []
         for r in range(ROWS):
             block = wide_ref[r * 40 : (r + 1) * 40, t * N2 : (t + 1) * N2]
-            real = jnp.concatenate([block[:FL], jnp.zeros((6, N2), F32)], axis=0)
-            imag = jnp.concatenate([block[FL : 2 * FL], jnp.zeros((6, N2), F32)], axis=0)
-            rows.append(jnp.concatenate([real, imag], axis=1))
+            gap = jnp.zeros((2, N2), F32)
+            real, imag = [], []
+            for f in range(3):
+                real += [block[f * 6 : f * 6 + 6], gap]
+                imag += [block[FL + f * 6 : FL + f * 6 + 6], gap]
+            both = [jnp.concatenate(real, axis=0), jnp.concatenate(imag, axis=0)]
+            rows.append(jnp.concatenate(both, axis=1))
         out = dot3(jnp.concatenate(rows, axis=0), high_ref[...], low_ref[...], NN)
         for odd in range(2):
             m1 = 2 * t + odd
@@ -196,27 +235,40 @@
                     even = even + term
                 else:
                     odd = odd + term
-            out_ref[:, r, x1 * N2 : (x1 + 1) * N2] = (even + odd)[:FL]
-            out_ref[:, r, (x1 + 10) * N2 : (x1 + 11) * N2] = (even - odd)[:FL]
-
-
-def spectra_kernel(start, count, place_ref, owner_ref, own_ref, other_ref, four_ref, out_ref):
+            for f in range(3):
+                rows6 = slice(f * 8, f * 8 + 6)
+                out_ref[f, r, :, x1 * N2 : (x1 + 1) * N2] = (even + odd)[rows6]
+                out_ref[f, r, :, (x1 + 10) * N2 : (x1 + 11) * N2] = (even - odd)[rows6]
+
+
+def relative(rels, step):
+    value = jnp.int32(rels[-1])
+    for k, rel in enumerate(rels[:-1]):
+        value = jnp.where(step == k, rel, value)
+    return value
+
+
+def spectra_kernel(start, count, rels, place_ref, owner_ref, own_ref, other_ref, four_ref, *refs):
     target, step = pl.program_id(0), pl.program_id(1)
     core, wave = place_ref[0], place_ref[1]
+    z = lax.rem(place_ref[2] + relative(rels, target), 4)
+    out_refs, work_ref = refs[:-1], refs[-1]
     extra = count * 36
+    group = 4 * count
+    side = 40 * group
 
     @pl.when(step == 0)
     def _():
-        out_ref[0, extra : extra + 8, :] = jnp.zeros((8, NM), F32)
+        work_ref[extra : extra + 8, :] = jnp.zeros((8, NM), F32)
 
     lane = lax.broadcasted_iota(jnp.int32, (1, NM), 1)
     narrow = lax.broadcasted_iota(jnp.int32, (1, N2), 1)
     kept = []
     for i in range(2):
-        pair = target * 10 + start + 2 * step + i
-        first_wave = owner_ref[wave * 80 + core * HALF + pair]
-        mine = four_ref[pl.ds(core * 1600 + pair, HALF, stride=HALF), :]
-        theirs = four_ref[pl.ds((1 - core) * 1600 + pair, HALF, stride=HALF), :]
+        first_wave = owner_ref[wave * 80 + core * HALF + z * 10 + start + 2 * step + i]
+        pair = z * count + 2 * step + i
+        mine = four_ref[pl.ds(core * side + pair, HALF, stride=group), :]
+        theirs = four_ref[pl.ds((1 - core) * side + pair, HALF, stride=group), :]
         four = jnp.concatenate([mine, theirs], axis=0)
         four_high = four.astype(BF).astype(F32)
         left = jnp.concatenate([four_high, four_high, four - four_high], axis=0).T
@@ -228,8 +280,25 @@
         kept.append(jnp.where(lane < NM - first_wave, both[40:80], both[0:40])[:36])
         last = jnp.sum(table[:, NM : NM + 1] * four, axis=0, keepdims=True)
         spot = pl.multiple_of((2 * step + i) * N2, N2)
-        out_ref[0, extra : extra + 1, pl.ds(spot, N2)] = jnp.where(narrow < 36, last, 0.0)
-    out_ref[0, pl.ds(pl.multiple_of(step * 72, 8), 72), :] = jnp.concatenate(kept, axis=0)
+        work_ref[extra : extra + 1, pl.ds(spot, N2)] = jnp.where(narrow < 36, last, 0.0)
+    work_ref[pl.ds(pl.multiple_of(step * 72, 8), 72), :] = jnp.concatenate(kept, axis=0)
+
+    @pl.when(step == count // 2 - 1)
+    def _():
+        if len(rels) == 1:
+            cut = halves(count)
+            out_refs[0][...] = work_ref[:cut]
+            out_refs[1][...] = work_ref[cut:]
+        else:
+            for k, out_ref in enumerate(out_refs):
+
+                @pl.when(target == k)
+                def _(out_ref=out_ref):
+                    out_ref[...] = work_ref[...]
+
+
+def halves(count):
+    return (count * 36 + 8) // 16 * 8
 
 
 def implicit_rows(load, degree, modes_e, modes_f, rates, height, heating):
@@ -300,16 +369,32 @@
     out_ref[extra : extra + 8, :] = jnp.concatenate(values, axis=0).T
 
 
-def grid_rows_kernel(start, count, place_ref, owner_ref, own_ref, other_ref, spec_ref, out_ref):
+def grid_rows_kernel(start, count, rels, place_ref, owner_ref, own_ref, other_ref, *refs):
     target, step = pl.program_id(0), pl.program_id(1)
     core, wave = place_ref[0], place_ref[1]
+    z = lax.rem(place_ref[2] + relative(rels, target), 4)
+    spec_refs, (out_ref, work_ref) = refs[:-2], refs[-2:]
     extra = count * 36
+    group = 4 * count
+    side = 40 * group
+    cut = halves(count)
+
+    for k in range(4):
+
+        @pl.when((target == k) & (step == 0))
+        def _(k=k):
+            if k < 3:
+                work_ref[...] = spec_refs[k][...]
+            else:
+                work_ref[:cut] = spec_refs[3][...]
+                work_ref[cut:] = spec_refs[4][...]
+
     lane = lax.broadcasted_iota(jnp.int32, (1, NM), 1)
-    block = spec_ref[0, pl.ds(pl.multiple_of(step * 72, 8), 72), :]
+    block = work_ref[pl.ds(pl.multiple_of(step * 72, 8), 72), :]
     pad = jnp.zeros((4, NM), F32)
     for i in range(2):
-        pair = target * 10 + start + 2 * step + i
-        first_wave = owner_ref[wave * 80 + core * HALF + pair]
+        first_wave = owner_ref[wave * 80 + core * HALF + z * 10 + start + 2 * step + i]
+        pair = z * count + 2 * step + i
         values = jnp.concatenate([block[i * 36 : i * 36 + 36], pad], axis=0)
         is_first = lane < NM - first_wave
         both = jnp.concatenate(
@@ -320,10 +405,10 @@
         back = dot3(table[:, :NM], high, low, NT)
         back = jnp.concatenate([back, jnp.zeros((80, 48), F32)], axis=1)
         spot = pl.multiple_of((2 * step + i) * N2, N2)
-        last = spec_ref[0, extra : extra + 1, pl.ds(spot, N2)]
+        last = work_ref[extra : extra + 1, pl.ds(spot, N2)]
         back = back + table[:, NM : NM + 1] * last
-        out_ref[pl.ds(core * 1600 + pair, HALF, stride=HALF), :] = back[:HALF]
-        out_ref[pl.ds((1 - core) * 1600 + pair, HALF, stride=HALF), :] = back[HALF:]
+        out_ref[pl.ds(core * side + pair, HALF, stride=group), :] = back[:HALF]
+        out_ref[pl.ds((1 - core) * side + pair, HALF, stride=group), :] = back[HALF:]
 
 
 def parameters():
@@ -345,101 +430,159 @@
     twiddle, forward, backward = constant_tables()
     smem = whole(pltpu.SMEM)
     place = jnp.stack([core, wave, z]).astype(jnp.int32)
-    owner_column = jnp.broadcast_to(owner[:, None], (PAIRS, N2))
-
-    away = lax.dynamic_slice(legendre, ((1 - core) * HALF, 0, 0), (HALF, HALF, PACK))
-    other = lax.ppermute(away, "core", [(0, 1), (1, 0)])
-
-    four = pl.pallas_call(
+    by_group = owner.reshape(8, 2, 4, 10)
+    order = [by_group[..., a : a + n].transpose(1, 0, 2, 3).reshape(-1) for a, n in CHUNKS]
+    owner_column = jnp.broadcast_to(jnp.concatenate(order)[:, None], (PAIRS, N2))
+    matrices = [m.reshape(36) for m in (modes_e, modes_f)] + [rates]
+    matrices += [m.reshape(36) for m in (height_matrix, heating_matrix)]
+
+    made = pl.pallas_call(
         fourier_kernel,
-        out_shape=jax.ShapeDtypeStruct((16, ROWS, HALF, N2), F32),
-        in_specs=[whole()] * 5,
-        out_specs=whole(),
-        scratch_shapes=[pltpu.VMEM((10, 120, 512), F32), pltpu.VMEM((208, NM), F32)],
+        out_shape=[jax.ShapeDtypeStruct((16, ROWS, 4 * n, N2), F32) for _, n in CHUNKS]
+        + [jax.ShapeDtypeStruct((4 * n, HALF, PACK), F32) for _, n in CHUNKS],
+        in_specs=[smem] + [whole()] * 5 + [whole(pl.ANY)],
+        out_specs=[whole()] * len(CHUNKS) + [whole(pl.ANY)] * len(CHUNKS),
+        scratch_shapes=[
+            pltpu.VMEM((10, 15, 8, 512), F32),
+            pltpu.VMEM((208, NM), F32),
+            pltpu.VMEM((HALF, HALF, PACK), F32),
+            pltpu.SemaphoreType.DMA((8 * len(CHUNKS),)),
+        ],
         compiler_params=parameters(),
-        cost_estimate=cost(4e9, 8e6),
+        cost_estimate=cost(4e9, 2.6e7),
         name="fourier",
-    )(grad_grid.reshape(FL, ROWS, NLON), owner_column, twiddle, *forward)
-    four = lax.all_to_all(four, ("core", "wave"), 0, 0, tiled=True).reshape(3200, N2)
-
-    def table_specs(start):
+    )(place, grad_grid.transpose(0, 2, 1, 3), owner_column, twiddle, *forward, legendre)
+    fours, aways = made[: len(CHUNKS)], made[len(CHUNKS) :]
+
+    def zone(rels, t, place):
+        return lax.rem(place[2] + relative(rels, t), 4)
+
+    def table_specs(start, count, rels):
         return [
             pl.BlockSpec(
                 (2, HALF, PACK),
-                lambda t, s, place, owner: (place[0] * 20 + t * 5 + start // 2 + s, 0, 0),
+                lambda t, s, place, owner: (
+                    place[0] * 20 + zone(rels, t, place) * 5 + start // 2 + s,
+                    0,
+                    0,
+                ),
             ),
-            pl.BlockSpec((2, HALF, PACK), lambda t, s, place, owner: (t * 5 + start // 2 + s, 0, 0)),
+            pl.BlockSpec(
+                (2, HALF, PACK),
+                lambda t, s, place, owner: (zone(rels, t, place) * (count // 2) + s, 0, 0),
+            ),
         ]
 
-    results = []
-    for start, count in CHUNKS:
+    def kept(rows, lanes):
+        return pl.BlockSpec((rows, lanes), lambda t, s, place, owner: (0, 0))
+
+    def spectra(start, count, rels, four, other):
         height = count * 36 + 8
-        spectra = pl.pallas_call(
-            lambda *refs: spectra_kernel(start, count, *refs),
-            out_shape=jax.ShapeDtypeStruct((4, height, NM), F32),
+        cut = halves(count)
+        rows = [cut, height - cut] if len(rels) == 1 else [height] * len(rels)
+        return pl.pallas_call(
+            lambda *refs: spectra_kernel(start, count, rels, *refs),
+            out_shape=[jax.ShapeDtypeStruct((n, NM), F32) for n in rows],
             grid_spec=pltpu.PrefetchScalarGridSpec(
                 num_scalar_prefetch=2,
-                grid=(4, count // 2),
-                in_specs=table_specs(start)
-                + [pl.BlockSpec((3200, N2), lambda t, s, place, owner: (0, 0))],
-                out_specs=pl.BlockSpec((1, height, NM), lambda t, s, place, owner: (t, 0, 0)),
+                grid=(len(rels), count // 2),
+                in_specs=table_specs(start, count, rels) + [kept(320 * count, N2)],
+                out_specs=[kept(n, NM) for n in rows],
+                scratch_shapes=[pltpu.VMEM((height, NM), F32)],
             ),
             compiler_params=parameters(),
-            cost_estimate=cost(2e9, 2e7),
+            cost_estimate=cost(5e7 * count * len(rels), 5e5 * count * len(rels)),
             name="spectra",
         )(place, owner, legendre, other, four)
-        mine = lax.psum_scatter(spectra, "z", scatter_dimension=0, tiled=True).reshape(height, NM)
-        theirs = lax.ppermute(mine, "yh", [(0, 1), (1, 0)])
-        updated = pl.pallas_call(
+
+    def implicit(start, count, mine, theirs):
+        height = count * 36 + 8
+        return pl.pallas_call(
             lambda *refs: implicit_kernel(start, count, *refs),
             out_shape=jax.ShapeDtypeStruct((height, NM), F32),
             grid=(10,),
             in_specs=[smem] * 7 + [pl.BlockSpec((height, N2), lambda t: (0, t))] * 2,
             out_specs=pl.BlockSpec((height, N2), lambda t: (0, t)),
             compiler_params=parameters(),
-            cost_estimate=cost(1e8, 6e6),
+            cost_estimate=cost(1e7 * count, 6e5 * count),
             name="implicit",
-        )(
-            place,
-            owner,
-            modes_e.reshape(36),
-            modes_f.reshape(36),
-            rates,
-            height_matrix.reshape(36),
-            heating_matrix.reshape(36),
-            mine,
-            theirs,
-        )
-        gathered = lax.all_gather(updated[None], "z", axis=0, tiled=True)
-        results.append(
-            pl.pallas_call(
-                lambda *refs: grid_rows_kernel(start, count, *refs),
-                out_shape=jax.ShapeDtypeStruct((3200, N2), F32),
-                grid_spec=pltpu.PrefetchScalarGridSpec(
-                    num_scalar_prefetch=2,
-                    grid=(4, count // 2),
-                    in_specs=table_specs(start)
-                    + [pl.BlockSpec((1, height, NM), lambda t, s, place, owner: (t, 0, 0))],
-                    out_specs=pl.BlockSpec((3200, N2), lambda t, s, place, owner: (0, 0)),
-                ),
-                compiler_params=parameters(),
-                cost_estimate=cost(3e9, 2e7),
-                name="grid_rows",
-            )(place, owner, legendre, other, gathered)
-        )
-    rows = results[0].reshape(16, ROWS, HALF, N2)
-    rows = lax.all_to_all(rows, ("core", "wave"), 0, 0, tiled=True)
+        )(place, owner, *matrices, mine, theirs)
+
+    def grid_rows(start, count, other, blocks):
+        height = count * 36 + 8
+        cut = halves(count)
+        rels = (0, 1, 3, 2)
+        rows = pl.pallas_call(
+            lambda *refs: grid_rows_kernel(start, count, rels, *refs),
+            out_shape=jax.ShapeDtypeStruct((320 * count, N2), F32),
+            grid_spec=pltpu.PrefetchScalarGridSpec(
+                num_scalar_prefetch=2,
+                grid=(4, count // 2),
+                in_specs=table_specs(start, count, rels)
+                + [kept(n, NM) for n in (height, height, height, cut, height - cut)],
+                out_specs=kept(320 * count, N2),
+                scratch_shapes=[pltpu.VMEM((height, NM), F32)],
+            ),
+            compiler_params=parameters(),
+            cost_estimate=cost(3e8 * count, 2e6 * count),
+            name="grid_rows",
+        )(place, owner, legendre, other, *blocks)
+        return rows.reshape(16, ROWS, 4 * count, N2)
+
+    def after(value, *earlier):
+        return lax.optimization_barrier((value,) + earlier)[0]
+
+    def exchange(value):
+        return lax.all_to_all(value, ("core", "wave"), 0, 0, tiled=True)
+
+    steps = [{} for _ in CHUNKS]
+    for k, (start, count) in enumerate(CHUNKS):
+        now, before = steps[k], steps[k - 1] if k else None
+        now["cut"] = cut = halves(count)
+        now["other"] = lax.ppermute(aways[k], "core", SWAP)
+        four = fours[k] if k == 0 else after(fours[k], before["opposite"][0])
+        four = exchange(four).reshape(320 * count, N2)
+        if k:
+            four = after(four, before["right"], before["left"])
+        now["opposite"] = top, bottom = spectra(start, count, (2,), four, now["other"])
+        top = lax.ppermute(top, "z", UP)
+        bottom = lax.ppermute(bottom, "z", DOWN)
+        right, left, mine = spectra(start, count, (1, 3, 0), four, now["other"])
+        if k:
+            top = after(top, before["sum"])
+        now["right"] = right = right.at[:cut].add(top)
+        now["left"] = left = left.at[cut:].add(bottom)
+        now["sum"] = mine + lax.ppermute(right, "z", UP) + lax.ppermute(left, "z", DOWN)
+        now["theirs"] = lax.ppermute(now["sum"], "yh", SWAP)
+    for k, (start, count) in enumerate(CHUNKS):
+        now, before = steps[k], steps[k - 1] if k else None
+        theirs = after(now["theirs"], *before["ends"]) if k else now["theirs"]
+        now["new"] = new = implicit(start, count, now["sum"], theirs)
+        left = lax.ppermute(new, "z", UP)
+        right = lax.ppermute(new, "z", DOWN)
+        now["left"], now["right"] = left, right
+        now["ends"] = left[: now["cut"]], right[now["cut"] :]
+        now["top"] = lax.ppermute(now["ends"][0], "z", UP)
+        now["bottom"] = lax.ppermute(now["ends"][1], "z", DOWN)
+    results = []
+    for k, (start, count) in enumerate(CHUNKS):
+        now = steps[k]
+        top = now["top"]
+        if k + 1 < len(CHUNKS):
+            top = after(top, steps[k + 1]["new"])
+        blocks = (now["new"], now["right"], now["left"], top, now["bottom"])
+        results.append(exchange(grid_rows(start, count, now["other"], blocks)))
     out = pl.pallas_call(
         inverse_kernel,
-        out_shape=jax.ShapeDtypeStruct((FL, ROWS, NLON), F32),
-        in_specs=[whole()] * 2 + [smem] * 2 + [whole()] * 3,
+        out_shape=jax.ShapeDtypeStruct((3, ROWS, 6, NLON), F32),
+        in_specs=[whole()] + [smem] * 2 + [whole()] * (3 + len(CHUNKS)),
         out_specs=whole(),
         scratch_shapes=[pltpu.VMEM((N1, 120, 256), F32), pltpu.VMEM((256, NM), F32)],
         compiler_params=parameters(),
         cost_estimate=cost(4e9, 8e6),
         name="inverse",
-    )(rows, owner_column, lat_weights, place, twiddle, *backward)
-    return out.reshape(3, 6, ROWS, NLON)
+    )(owner_column, lat_weights, place, twiddle, *backward, *results)
+    return out.transpose(0, 2, 1, 3)
 
 
 def solution(mesh):

time: 348 us -> 237 us (0.68)
  waiting for transfers between devices: 216 us -> 69.9 us
  starting transfers between devices: 9.95 us -> 46.3 us
  between operations: 13.5 us -> 0.33 us
  local copies, waits for them, and re-layouts: 18 us -> 8.15 us
  Pallas kernels: 61.6 us -> 69.6 us
  blocking collectives: 28.2 us -> 35.7 us
  other arithmetic: 0.08 us -> 5.75 us
    all_gather x1 -> x0, waiting for transfers between devices: 76.8 us -> none  [per_device(): gathered = lax.all_gather(updated[None], 'z', axis=0, tiled=True)]
    reduce_scatter x1 -> x0, waiting for transfers between devices: 74.9 us -> none  [per_device(): lax.psum_scatter(spectra, 'z', scatter_dimension=0, tiled=True)]
    ppermute x2 -> x20, starting transfers between devices: 4.24 us -> 28.7 us  [the longest x2 5.86 us: per_device(): now['bottom'] = lax.ppermute(now['ends'][1], 'z', DOWN)]
    ppermute x2 -> x20, waiting for transfers between devices: 40.7 us -> 54.5 us  [the longest x2 18.6 us: per_device(): left = lax.ppermute(new, 'z', UP)]
    all_to_all x1 -> x2, starting transfers between devices: 5.63 us -> 17.6 us  [exchange(): return lax.all_to_all(value, ('core', 'wave'), 0, 0, tiled=True)]
    all_to_all x1 -> x2, waiting for transfers between devices: 23.8 us -> 15.3 us  [exchange(): return lax.all_to_all(value, ('core', 'wave'), 0, 0, tiled=True)]
    pallas_call x5 -> x10, Pallas kernels: 61.6 us -> 69.6 us  [the longest x4 22.5 us: spectra(): pl.pallas_call(lambda *refs: spectra_kernel(start, count, rels, *refs), o...]
    dynamic_slice x1 -> x0, local copies, waits for them, and re-layouts: 7.76 us -> none  [per_device(): lax.dynamic_slice(legendre, ((1 - core) * HALF, 0, 0), (HALF, HALF, PACK))]
  transfers between devices with their start and end apart: 5 -> 22, of which waited for: 4 -> 6; matrix products, arithmetic and copies ran while one was open for 0% -> 3% of each run, Pallas kernels for 3% -> 22%
where the time goes in v2:
time: 237 us; the launch traced here: 236 us
  waiting for transfers between devices  69.9 us (29%)
  Pallas kernels  69.6 us (29%)
  starting transfers between devices  46.3 us (20%)
  blocking collectives  35.7 us (15%)
  local copies, waits for them, and re-layouts  8.15 us (3%)
  other arithmetic  5.75 us (2%)
    all_to_all x2, blocking collectives, exchange(): return lax.all_to_all(value, ('core', 'wave'), 0, 0, tiled=True)  35.7 us
    pallas_call x4, Pallas kernels, spectra(): pl.pallas_call(lambda *refs: spectra_kernel(start, count, rels, *refs), o...  22.5 us
    pallas_call x2, Pallas kernels, grid_rows(): pl.pallas_call(lambda *refs: grid_rows_kernel(start, count, rels, *refs),...  21 us
    ppermute x2, waiting for transfers between devices, per_device(): left = lax.ppermute(new, 'z', UP)  18.6 us
    ppermute x2, waiting for transfers between devices, per_device(): now['theirs'] = lax.ppermute(now['sum'], 'yh', SWAP)  18.3 us
    all_to_all x2, starting transfers between devices, exchange(): return lax.all_to_all(value, ('core', 'wave'), 0, 0, tiled=True)  17.6 us
    all_to_all x2, waiting for transfers between devices, exchange(): return lax.all_to_all(value, ('core', 'wave'), 0, 0, tiled=True)  15.3 us
    ppermute x2, waiting for transfers between devices, per_device(): now['top'] = lax.ppermute(now['ends'][0], 'z', UP)  14.8 us
  transfers between devices with their start and end apart: 22, of which 6 were waited for; matrix products, arithmetic and copies ran while one was open for 3% of the time, Pallas kernels for 22%

profile of v2, /device:TPU:1, one launch (start us, length us, event | category | flops | bytes accessed | tf_op | source)
XLA Modules:
  0.0 235.7 jit_solution(9256268642073083886)
XLA Ops:
  0.0 0.8 reshape.129
  0.9 0.1 reshape.130
  1.3 0.1 broadcast_in_dim.2.owner_ref
  1.5 1.3 copy-done
  2.8 0.9 copy-done.4
  3.7 0.9 copy-done.5
  4.7 0.7 copy-done.6
  5.4 10.7 %fourier.1 = (f32[16,5,24,128]{3,2,1,0:T(8,128)}, f32[16,5,16,128]{3,2,1,0:T(8,128)S(1)}, f32[24,40,1408]{2,1,0:T(8,128)}, f32[16,40,1408]{2,1,0:T(8,128)S(1)}) custom-call(s32[3]{0:T(128)S(1)} %pad_add_fusion.1.place_ref.refs_0_, f32[3,5,6,2560]{3,2,1,0:T(8,128)S(1)} %bitcast.18, s32[640,128]{1,0:T(8,128)S(1)} %broadcast_in_dim.2.owner_ref, ...), custom_call_target="tpu_custom_call" | custom-call | flops 4000000000 | bytes 26000000 | tf_op jit(solution)/shard_map/fourier/pallas_call | solution.py:439
  16.1 1.8 copy-done.9
  17.8 1.4 collective-permute-start
  19.3 5.6 %all-to-all-start = ((f32[16,5,24,128]{3,2,1,0:T(8,128)}), f32[16,5,24,128]{3,2,1,0:T(8,128)S(1)}, u32[]{:S(2)}, u32[]{:S(2)}) async-start(f32[16,5,24,128]{3,2,1,0:T(8,128)} %get-tuple-element.73), calls=%async_computation | async-start | bytes 1966080 | tf_op jit(solution)/shard_map/all_to_all | solution.py:536
  24.8 0.2 collective-permute-start.9
  25.0 15.3 %all-to-all-done = f32[16,5,24,128]{3,2,1,0:T(8,128)S(1)} async-done(((f32[16,5,24,128]{3,2,1,0:T(8,128)}), f32[16,5,24,128]{3,2,1,0:T(8,128)S(1)}, u32[]{:S(2)}, u32[]{:S(2)}) %all-to-all-start) | async-done | bytes 983072 | tf_op jit(solution)/shard_map/all_to_all | solution.py:536
  40.3 3.8 %spectra.5 = (f32[112,1280]{1,0:T(8,128)S(1)}, f32[112,1280]{1,0:T(8,128)S(1)}) custom-call(s32[3]{0:T(128)S(1)} %pad_add_fusion.1.place_ref.refs_0_, s32[640]{0:T(1024)S(1)} %copy-done.3, f32[80,40,1408]{2,1,0:T(8,128)} %refs_2_.11, f32[24,40,1408]{2,1,0:T(8,128)} %collective-permute-done.refs_3_, f32[1920,128]{1,0:T(8,128)S(1)} %bitcast.13), custom_call_target="tpu_custom_call" | custom-call | flops 300000000 | bytes 3000000 | tf_op jit(solution)/shard_map/spectra/pallas_call | solution.py:483
  44.1 1.7 collective-permute-start.1
  45.8 2.2 collective-permute-start.3
  48.0 8.7 %spectra.4 = (f32[224,1280]{1,0:T(8,128)S(1)}, f32[224,1280]{1,0:T(8,128)S(1)}, f32[224,1280]{1,0:T(8,128)S(1)}) custom-call(s32[3]{0:T(128)S(1)} %pad_add_fusion.1.place_ref.refs_0_, s32[640]{0:T(1024)S(1)} %copy-done.3, f32[80,40,1408]{2,1,0:T(8,128)} %refs_2_.11, f32[24,40,1408]{2,1,0:T(8,128)} %collective-permute-done.refs_3_, f32[1920,128]{1,0:T(8,128)S(1)} %bitcast.14), custom_call_target="tpu_custom_call" | custom-call | flops 900000000 | bytes 9000000 | tf_op jit(solution)/shard_map/spectra/pallas_call | solution.py:483
  56.7 2.8 %collective-permute-done.1 = f32[112,1280]{1,0:T(8,128)S(1)} collective-permute-done((f32[112,1280]{1,0:T(8,128)S(1)}, f32[112,1280]{1,0:T(8,128)S(1)}, u32[]{:S(2)}, u32[]{:S(2)}) %collective-permute-start.1) | collective-permute-done | bytes 573472 | tf_op jit(solution)/shard_map/ppermute | solution.py:548
  59.7 0.1 add_dynamic-update-slice_fusion
  59.9 2.7 %collective-permute-start.4 = (f32[224,1280]{1,0:T(8,128)S(1)}, f32[224,1280]{1,0:T(8,128)S(1)}, u32[]{:S(2)}, u32[]{:S(2)}) collective-permute-start(f32[224,1280]{1,0:T(8,128)S(1)} %add_dynamic-update-slice_fusion), channel_id=1, source_target_pairs={{0,48},{16,0},{32,16},{48,32},{1,49},{17,1},{33,17},{49,33},{2,50}... | collective-permute-start | bytes 3440648 | tf_op jit(solution)/shard_map/ppermute | solution.py:555
  62.6 17.5 %all_to_all.20 = f32[16,5,16,128]{3,2,1,0:T(8,128)S(1)} all-to-all(f32[16,5,16,128]{3,2,1,0:T(8,128)S(1)} %get-tuple-element.81), channel_id=1, replica_groups=mesh['yh'=2,'z'=4,'core'=2,'wave'=8] {'core','wave'}, dimensions={0} | all-to-all | bytes 1310720 | tf_op jit(solution)/shard_map/all_to_all | solution.py:536
  80.1 2.7 %spectra.7 = (f32[72,1280]{1,0:T(8,128)S(1)}, f32[80,1280]{1,0:T(8,128)S(1)}) custom-call(s32[3]{0:T(128)S(1)} %pad_add_fusion.1.place_ref.refs_0_, s32[640]{0:T(1024)S(1)} %copy-done.3, f32[80,40,1408]{2,1,0:T(8,128)} %refs_2_.11, f32[16,40,1408]{2,1,0:T(8,128)} %collective-permute-done.9.refs_3_, f32[1280,128]{1,0:T(8,128)S(1)} %bitcast.15), custom_call_target="tpu_custom_call" | custom-call | flops 200000000 | bytes 2000000 | tf_op jit(solution)/shard_map/spectra/pallas_call | solution.py:483
  82.9 2.7 %collective-permute-start.12 = (f32[80,1280]{1,0:T(8,128)S(1)}, f32[80,1280]{1,0:T(8,128)S(1)}, u32[]{:S(2)}, u32[]{:S(2)}) collective-permute-start(f32[80,1280]{1,0:T(8,128)S(1)} %get-tuple-element.88), channel_id=1, source_target_pairs={{0,48},{16,0},{32,16},{48,32},{1,49},{17,1},{33,17},{49,33},{2,50}... | collective-permute-start | bytes 1228808 | tf_op jit(solution)/shard_map/ppermute | solution.py:549
  85.5 7.3 %spectra.6 = (f32[152,1280]{1,0:T(8,128)}, f32[152,1280]{1,0:T(8,128)}, f32[152,1280]{1,0:T(8,128)S(1)}) custom-call(s32[3]{0:T(128)S(1)} %pad_add_fusion.1.place_ref.refs_0_, s32[640]{0:T(1024)S(1)} %copy-done.3, f32[80,40,1408]{2,1,0:T(8,128)} %refs_2_.11, f32[16,40,1408]{2,1,0:T(8,128)} %collective-permute-done.9.refs_3_, f32[1280,128]{1,0:T(8,128)S(1)} %bitcast.16), custom_call_target="tpu_custom_call" | custom-call | flops 600000000 | bytes 6000000 | tf_op jit(solution)/shard_map/spectra/pallas_call | solution.py:483
  92.9 0.2 add_add_fusion.refs_7_
  93.1 0.6 copy-done.1
  93.7 2.6 %collective-permute-start.5 = (f32[224,1280]{1,0:T(8,128)S(1)}, f32[224,1280]{1,0:T(8,128)S(1)}, u32[]{:S(2)}, u32[]{:S(2)}) collective-permute-start(f32[224,1280]{1,0:T(8,128)S(1)} %add_add_fusion.refs_7_), channel_id=1, source_target_pairs={{0,64},{64,0},{1,65},{65,1},{2,66},{66,2},{3,67},{67,3},{4,68},{68... | collective-permute-start | bytes 3440648 | tf_op jit(solution)/shard_map/ppermute | solution.py:556
  96.4 1.9 add_dynamic-update-slice_fusion.2
  98.3 1.9 collective-permute-start.13
  100.2 1.8 add_dynamic-update-slice_fusion.3
  102.3 18.3 %collective-permute-done.5.refs_8_ = f32[224,1280]{1,0:T(8,128)S(1)} collective-permute-done((f32[224,1280]{1,0:T(8,128)S(1)}, f32[224,1280]{1,0:T(8,128)S(1)}, u32[]{:S(2)}, u32[]{:S(2)}) %collective-permute-start.5) | collective-permute-done | bytes 1146912 | tf_op jit(solution)/shard_map/ppermute | solution.py:556
  120.6 4.2 %implicit.2.refs_4_ = f32[224,1280]{1,0:T(8,128)S(1)} custom-call(s32[3]{0:T(128)S(1)} %pad_add_fusion.1.place_ref.refs_0_, s32[640]{0:T(1024)S(1)} %copy-done.3, f32[36]{0:T(128)S(1)} %reshape.132.refs_2_, f32[36]{0:T(128)S(1)} %reshape.133.refs_3_, f32[6]{0:T(128)S(1)} %copy-done.8, f32[36]{0:T(128)S(1)} %reshape.134.refs_5_, f32[36]{0:T(128)S(1)} %reshape.135.refs_6_, ...), custom_call_target="tpu_custom_call" | custom-call | flops 60000000 | bytes 3600000 | tf_op jit(solution)/shard_map/implicit/pallas_call | solution.py:500
  124.9 2.7 %collective-permute-start.6 = (f32[224,1280]{1,0:T(8,128)S(1)}, f32[224,1280]{1,0:T(8,128)S(1)}, u32[]{:S(2)}, u32[]{:S(2)}) collective-permute-start(f32[224,1280]{1,0:T(8,128)S(1)} %implicit.2.refs_4_), channel_id=1, source_target_pairs={{0,48},{16,0},{32,16},{48,32},{1,49},{17,1},{33,17},{49,33},{2,50}... | collective-permute-start | bytes 3440648 | tf_op jit(solution)/shard_map/ppermute | solution.py:562
  127.6 1.5 add_add_fusion.1.refs_7_
  129.1 2.8 %collective-permute-start.14 = (f32[152,1280]{1,0:T(8,128)S(1)}, f32[152,1280]{1,0:T(8,128)S(1)}, u32[]{:S(2)}, u32[]{:S(2)}) collective-permute-start(f32[152,1280]{1,0:T(8,128)S(1)} %add_add_fusion.1.refs_7_), channel_id=1, source_target_pairs={{0,64},{64,0},{1,65},{65,1},{2,66},{66,2},{3,67},{67,3},{4,68},{68... | collective-permute-start | bytes 2334728 | tf_op jit(solution)/shard_map/ppermute | solution.py:556
  131.9 18.6 %collective-permute-done.7.refs_6_ = f32[224,1280]{1,0:T(8,128)S(1)} collective-permute-done((f32[224,1280]{1,0:T(8,128)S(1)}, f32[224,1280]{1,0:T(8,128)S(1)}, u32[]{:S(2)}, u32[]{:S(2)}) %collective-permute-start.7) | collective-permute-done | bytes 1146912 | tf_op jit(solution)/shard_map/ppermute | solution.py:561
  150.7 2.7 %collective-permute-start.15 = (f32[112,1280]{1,0:T(8,128)S(1)}, f32[112,1280]{1,0:T(8,128)S(1)}, u32[]{:S(2)}, u32[]{:S(2)}) collective-permute-start(f32[112,1280]{1,0:T(8,128)S(1)} %slice.107), channel_id=1, source_target_pairs={{0,48},{16,0},{32,16},{48,32},{1,49},{17,1},{33,17},{49,33},{2,50}... | collective-permute-start | bytes 1720328 | tf_op jit(solution)/shard_map/ppermute | solution.py:566
  153.4 4.2 %implicit.3.refs_4_ = f32[152,1280]{1,0:T(8,128)S(1)} custom-call(s32[3]{0:T(128)S(1)} %pad_add_fusion.1.place_ref.refs_0_, s32[640]{0:T(1024)S(1)} %copy-done.3, f32[36]{0:T(128)S(1)} %reshape.132.refs_2_, f32[36]{0:T(128)S(1)} %reshape.133.refs_3_, f32[6]{0:T(128)S(1)} %copy-done.8, f32[36]{0:T(128)S(1)} %reshape.134.refs_5_, f32[36]{0:T(128)S(1)} %reshape.135.refs_6_, ...), custom_call_target="tpu_custom_call" | custom-call | flops 40000000 | bytes 2400000 | tf_op jit(solution)/shard_map/implicit/pallas_call | solution.py:500
  157.6 0.1 collective-permute-start.16
  157.8 1.4 collective-permute-start.17
  159.2 3.9 %collective-permute-done.8.refs_7_ = f32[112,1280]{1,0:T(8,128)S(1)} collective-permute-done((f32[112,1280]{1,0:T(8,128)S(1)}, f32[112,1280]{1,0:T(8,128)S(1)}, u32[]{:S(2)}, u32[]{:S(2)}) %collective-permute-start.8) | collective-permute-done | bytes 573472 | tf_op jit(solution)/shard_map/ppermute | solution.py:565
  163.1 12.8 %grid_rows.2 = f32[1920,128]{1,0:T(8,128)} custom-call(s32[3]{0:T(128)S(1)} %pad_add_fusion.1.place_ref.refs_0_, s32[640]{0:T(1024)S(1)} %copy-done.3, f32[80,40,1408]{2,1,0:T(8,128)} %refs_2_.11, f32[24,40,1408]{2,1,0:T(8,128)} %collective-permute-done.refs_3_, f32[224,1280]{1,0:T(8,128)S(1)} %implicit.2.refs_4_, ...), custom_call_target="tpu_custom_call" | custom-call | flops 1800000000 | bytes 12000000 | tf_op jit(solution)/shard_map/grid_rows/pallas_call | solution.py:515
  175.8 12.1 %all-to-all-start.2 = ((f32[16,5,24,128]{3,2,1,0:T(8,128)}), f32[16,5,24,128]{3,2,1,0:T(8,128)}, u32[]{:S(2)}, u32[]{:S(2)}) async-start(f32[16,5,24,128]{3,2,1,0:T(8,128)} %bitcast.8), calls=%async_computation.2 | async-start | bytes 1966080 | tf_op jit(solution)/shard_map/all_to_all | solution.py:536
  187.9 3.1 %collective-permute-start.19 = (f32[80,1280]{1,0:T(8,128)S(1)}, f32[80,1280]{1,0:T(8,128)S(1)}, u32[]{:S(2)}, u32[]{:S(2)}) collective-permute-start(f32[80,1280]{1,0:T(8,128)S(1)} %slice.109), channel_id=1, source_target_pairs={{0,48},{16,0},{32,16},{48,32},{1,49},{17,1},{33,17},{49,33},{2,50}... | collective-permute-start | bytes 1228808 | tf_op jit(solution)/shard_map/ppermute | solution.py:566
  191.2 10.9 %collective-permute-done.18.refs_7_ = f32[72,1280]{1,0:T(8,128)S(1)} collective-permute-done((f32[72,1280]{1,0:T(8,128)S(1)}, f32[72,1280]{1,0:T(8,128)S(1)}, u32[]{:S(2)}, u32[]{:S(2)}) %collective-permute-start.18) | collective-permute-done | bytes 368672 | tf_op jit(solution)/shard_map/ppermute | solution.py:565
  202.1 8.3 %grid_rows.3 = f32[1280,128]{1,0:T(8,128)S(1)} custom-call(s32[3]{0:T(128)S(1)} %pad_add_fusion.1.place_ref.refs_0_, s32[640]{0:T(1024)S(1)} %copy-done.3, f32[80,40,1408]{2,1,0:T(8,128)} %refs_2_.11, f32[16,40,1408]{2,1,0:T(8,128)} %collective-permute-done.9.refs_3_, f32[152,1280]{1,0:T(8,128)S(1)} %implicit.3.refs_4_, ...), custom_call_target="tpu_custom_call" | custom-call | flops 1200000000 | bytes 8000000 | tf_op jit(solution)/shard_map/grid_rows/pallas_call | solution.py:515
  210.5 18.2 %all_to_all.21.refs_1_ = f32[16,5,16,128]{3,2,1,0:T(8,128)S(1)} all-to-all(f32[16,5,16,128]{3,2,1,0:T(8,128)S(1)} %bitcast.17), channel_id=1, replica_groups=mesh['yh'=2,'z'=4,'core'=2,'wave'=8] {'core','wave'}, dimensions={0} | all-to-all | bytes 1310720 | tf_op jit(solution)/shard_map/all_to_all | solution.py:536
  228.7 7.0 %inverse.1 = f32[3,5,6,2560]{3,2,1,0:T(8,128)} custom-call(s32[640,128]{1,0:T(8,128)S(1)} %broadcast_in_dim.2.owner_ref, f32[40]{0:T(128)S(1)} %copy-done.10, s32[3]{0:T(128)S(1)} %pad_add_fusion.1.place_ref.refs_0_, f32[2,20,128]{2,1,0:T(8,128)S(1)} %copy-done.7, bf16[256,512]{1,0:T(8,128)(2,1)S(1)} %copy-done.11, bf16[256,512]{1,0:T(8,128)(2,1)S(1)} %copy-done.12, ...), custom_call_target="tpu_custom_call" | custom-call | flops 4000000000 | bytes 8000000 | tf_op jit(solution)/shard_map/inverse/pallas_call | solution.py:575
  (66 shorter events, 1.3 us)
Async XLA Ops:
  1.5 1.3 copy-start
  2.8 0.9 copy-start.4
  3.7 0.9 copy-start.5
  4.7 0.7 copy-start.6
  16.1 1.8 copy-start.9
  17.8 22.5 %copy-start.3 = (s32[640]{0:T(1024)S(1)}, s32[640]{0:T(1024)}, u32[]{:S(2)}) copy-start(s32[640]{0:T(1024)} %refs_1_.15) | copy-start | bytes 7684
  17.8 22.5 %collective-permute-start = (f32[24,40,1408]{2,1,0:T(8,128)}, f32[24,40,1408]{2,1,0:T(8,128)}, u32[]{:S(2)}, u32[]{:S(2)}) collective-permute-start(f32[24,40,1408]{2,1,0:T(8,128)} %get-tuple-element.72), channel_id=1, source_target_pairs={{0,8},{8,0},{1,9},{9,1},{2,10},{10,2},{3,11},{11,3},{4,12},{12,4},... | collective-permute-start | bytes 16220168 | tf_op jit(solution)/shard_map/ppermute | solution.py:542
  19.3 21.0 %all-to-all-start = ((f32[16,5,24,128]{3,2,1,0:T(8,128)}), f32[16,5,24,128]{3,2,1,0:T(8,128)S(1)}, u32[]{:S(2)}, u32[]{:S(2)}) async-start(f32[16,5,24,128]{3,2,1,0:T(8,128)} %get-tuple-element.73), calls=%async_computation | async-start | bytes 1966080 | tf_op jit(solution)/shard_map/all_to_all | solution.py:536
  24.8 55.2 %collective-permute-start.9 = (f32[16,40,1408]{2,1,0:T(8,128)}, f32[16,40,1408]{2,1,0:T(8,128)}, u32[]{:S(2)}, u32[]{:S(2)}) collective-permute-start(f32[16,40,1408]{2,1,0:T(8,128)} %copy-done.9), channel_id=1, source_target_pairs={{0,8},{8,0},{1,9},{9,1},{2,10},{10,2},{3,11},{11,3},{4,12},{12,4},... | collective-permute-start | bytes 10813448 | tf_op jit(solution)/shard_map/ppermute | solution.py:542
  44.1 15.4 %collective-permute-start.1 = (f32[112,1280]{1,0:T(8,128)S(1)}, f32[112,1280]{1,0:T(8,128)S(1)}, u32[]{:S(2)}, u32[]{:S(2)}) collective-permute-start(f32[112,1280]{1,0:T(8,128)S(1)} %get-tuple-element.76), channel_id=1, source_target_pairs={{0,16},{16,32},{32,48},{48,0},{1,17},{17,33},{33,49},{49,1},{2,18}... | collective-permute-start | bytes 1720328 | tf_op jit(solution)/shard_map/ppermute | solution.py:548
  45.8 13.9 %collective-permute-start.3 = (f32[112,1280]{1,0:T(8,128)S(1)}, f32[112,1280]{1,0:T(8,128)S(1)}, u32[]{:S(2)}, u32[]{:S(2)}) collective-permute-start(f32[112,1280]{1,0:T(8,128)S(1)} %get-tuple-element.78), channel_id=1, source_target_pairs={{0,48},{16,0},{32,16},{48,32},{1,49},{17,1},{33,17},{49,33},{2,50}... | collective-permute-start | bytes 1720328 | tf_op jit(solution)/shard_map/ppermute | solution.py:549
  59.6 33.2 %collective-permute-start.2 = (f32[224,1280]{1,0:T(8,128)S(1)}, f32[224,1280]{1,0:T(8,128)S(1)}, u32[]{:S(2)}, u32[]{:S(2)}) collective-permute-start(f32[224,1280]{1,0:T(8,128)S(1)} %add_dynamic-update-slice_fusion.1), channel_id=1, source_target_pairs={{0,16},{16,32},{32,48},{48,0},{1,17},{17,33},{33,49},{49,1},{2,18}... | collective-permute-start | bytes 3440648 | tf_op jit(solution)/shard_map/ppermute | solution.py:555
  59.9 33.0 %collective-permute-start.4 = (f32[224,1280]{1,0:T(8,128)S(1)}, f32[224,1280]{1,0:T(8,128)S(1)}, u32[]{:S(2)}, u32[]{:S(2)}) collective-permute-start(f32[224,1280]{1,0:T(8,128)S(1)} %add_dynamic-update-slice_fusion), channel_id=1, source_target_pairs={{0,48},{16,0},{32,16},{48,32},{1,49},{17,1},{33,17},{49,33},{2,50}... | collective-permute-start | bytes 3440648 | tf_op jit(solution)/shard_map/ppermute | solution.py:555
  82.8 17.4 %collective-permute-start.10 = (f32[72,1280]{1,0:T(8,128)S(1)}, f32[72,1280]{1,0:T(8,128)S(1)}, u32[]{:S(2)}, u32[]{:S(2)}) collective-permute-start(f32[72,1280]{1,0:T(8,128)S(1)} %get-tuple-element.85), channel_id=1, source_target_pairs={{0,16},{16,32},{32,48},{48,0},{1,17},{17,33},{33,49},{49,1},{2,18}... | collective-permute-start | bytes 1105928 | tf_op jit(solution)/shard_map/ppermute | solution.py:548
  82.9 13.5 %collective-permute-start.12 = (f32[80,1280]{1,0:T(8,128)S(1)}, f32[80,1280]{1,0:T(8,128)S(1)}, u32[]{:S(2)}, u32[]{:S(2)}) collective-permute-start(f32[80,1280]{1,0:T(8,128)S(1)} %get-tuple-element.88), channel_id=1, source_target_pairs={{0,48},{16,0},{32,16},{48,32},{1,49},{17,1},{33,17},{49,33},{2,50}... | collective-permute-start | bytes 1228808 | tf_op jit(solution)/shard_map/ppermute | solution.py:549
  92.9 0.9 copy-start.1
  93.7 26.8 %collective-permute-start.5 = (f32[224,1280]{1,0:T(8,128)S(1)}, f32[224,1280]{1,0:T(8,128)S(1)}, u32[]{:S(2)}, u32[]{:S(2)}) collective-permute-start(f32[224,1280]{1,0:T(8,128)S(1)} %add_add_fusion.refs_7_), channel_id=1, source_target_pairs={{0,64},{64,0},{1,65},{65,1},{2,66},{66,2},{3,67},{67,3},{4,68},{68... | collective-permute-start | bytes 3440648 | tf_op jit(solution)/shard_map/ppermute | solution.py:556
  96.4 5.6 %copy-start.13 = (f32[6,6]{1,0:T(8,128)S(1)}, f32[6,6]{1,0:T(8,128)}, u32[]{:S(2)}) copy-start(f32[6,6]{1,0:T(8,128)} %param.26) | copy-start | bytes 436
  96.4 5.7 %copy-start.14 = (f32[6,6]{1,0:T(8,128)S(1)}, f32[6,6]{1,0:T(8,128)}, u32[]{:S(2)}) copy-start(f32[6,6]{1,0:T(8,128)} %param.27) | copy-start | bytes 436
  96.4 5.8 %copy-start.15 = (f32[6,6]{1,0:T(8,128)S(1)}, f32[6,6]{1,0:T(8,128)}, u32[]{:S(2)}) copy-start(f32[6,6]{1,0:T(8,128)} %param.29) | copy-start | bytes 436
  96.4 5.9 %copy-start.16 = (f32[6,6]{1,0:T(8,128)S(1)}, f32[6,6]{1,0:T(8,128)}, u32[]{:S(2)}) copy-start(f32[6,6]{1,0:T(8,128)} %param.30) | copy-start | bytes 436
  96.4 24.2 %copy-start.8 = (f32[6]{0:T(128)S(1)}, f32[6]{0:T(128)}, u32[]{:S(2)}) copy-start(f32[6]{0:T(128)} %refs_4_.3) | copy-start | bytes 76
  98.3 29.3 %collective-permute-start.13 = (f32[152,1280]{1,0:T(8,128)}, f32[152,1280]{1,0:T(8,128)}, u32[]{:S(2)}, u32[]{:S(2)}) collective-permute-start(f32[152,1280]{1,0:T(8,128)} %add_dynamic-update-slice_fusion.2), channel_id=1, source_target_pairs={{0,48},{16,0},{32,16},{48,32},{1,49},{17,1},{33,17},{49,33},{2,50}... | collective-permute-start | bytes 2334728 | tf_op jit(solution)/shard_map/ppermute | solution.py:555
  102.0 25.6 %collective-permute-start.11 = (f32[152,1280]{1,0:T(8,128)}, f32[152,1280]{1,0:T(8,128)}, u32[]{:S(2)}, u32[]{:S(2)}) collective-permute-start(f32[152,1280]{1,0:T(8,128)} %add_dynamic-update-slice_fusion.3), channel_id=1, source_target_pairs={{0,16},{16,32},{32,48},{48,0},{1,17},{17,33},{33,49},{49,1},{2,18}... | collective-permute-start | bytes 2334728 | tf_op jit(solution)/shard_map/ppermute | solution.py:555
  102.3 25.3 %copy-start.2 = (f32[152,1280]{1,0:T(8,128)S(1)}, f32[152,1280]{1,0:T(8,128)}, u32[]{:S(2)}) copy-start(f32[152,1280]{1,0:T(8,128)} %copy-done.1) | copy-start | bytes 2334724
  124.8 25.7 %collective-permute-start.7 = (f32[224,1280]{1,0:T(8,128)S(1)}, f32[224,1280]{1,0:T(8,128)S(1)}, u32[]{:S(2)}, u32[]{:S(2)}) collective-permute-start(f32[224,1280]{1,0:T(8,128)S(1)} %implicit.2.refs_4_), channel_id=1, source_target_pairs={{0,16},{16,32},{32,48},{48,0},{1,17},{17,33},{33,49},{49,1},{2,18}... | collective-permute-start | bytes 3440648 | tf_op jit(solution)/shard_map/ppermute | solution.py:561
  124.9 25.7 %collective-permute-start.6 = (f32[224,1280]{1,0:T(8,128)S(1)}, f32[224,1280]{1,0:T(8,128)S(1)}, u32[]{:S(2)}, u32[]{:S(2)}) collective-permute-start(f32[224,1280]{1,0:T(8,128)S(1)} %implicit.2.refs_4_), channel_id=1, source_target_pairs={{0,48},{16,0},{32,16},{48,32},{1,49},{17,1},{33,17},{49,33},{2,50}... | collective-permute-start | bytes 3440648 | tf_op jit(solution)/shard_map/ppermute | solution.py:562
  129.1 24.3 %collective-permute-start.14 = (f32[152,1280]{1,0:T(8,128)S(1)}, f32[152,1280]{1,0:T(8,128)S(1)}, u32[]{:S(2)}, u32[]{:S(2)}) collective-permute-start(f32[152,1280]{1,0:T(8,128)S(1)} %add_add_fusion.1.refs_7_), channel_id=1, source_target_pairs={{0,64},{64,0},{1,65},{65,1},{2,66},{66,2},{3,67},{67,3},{4,68},{68... | collective-permute-start | bytes 2334728 | tf_op jit(solution)/shard_map/ppermute | solution.py:556
  150.6 12.5 %collective-permute-start.8 = (f32[112,1280]{1,0:T(8,128)S(1)}, f32[112,1280]{1,0:T(8,128)S(1)}, u32[]{:S(2)}, u32[]{:S(2)}) collective-permute-start(f32[112,1280]{1,0:T(8,128)S(1)} %slice.106), channel_id=1, source_target_pairs={{0,16},{16,32},{32,48},{48,0},{1,17},{17,33},{33,49},{49,1},{2,18}... | collective-permute-start | bytes 1720328 | tf_op jit(solution)/shard_map/ppermute | solution.py:565
  150.7 12.3 %collective-permute-start.15 = (f32[112,1280]{1,0:T(8,128)S(1)}, f32[112,1280]{1,0:T(8,128)S(1)}, u32[]{:S(2)}, u32[]{:S(2)}) collective-permute-start(f32[112,1280]{1,0:T(8,128)S(1)} %slice.107), channel_id=1, source_target_pairs={{0,48},{16,0},{32,16},{48,32},{1,49},{17,1},{33,17},{49,33},{2,50}... | collective-permute-start | bytes 1720328 | tf_op jit(solution)/shard_map/ppermute | solution.py:566
  157.6 30.2 %collective-permute-start.16 = (f32[152,1280]{1,0:T(8,128)S(1)}, f32[152,1280]{1,0:T(8,128)S(1)}, u32[]{:S(2)}, u32[]{:S(2)}) collective-permute-start(f32[152,1280]{1,0:T(8,128)S(1)} %implicit.3.refs_4_), channel_id=1, source_target_pairs={{0,48},{16,0},{32,16},{48,32},{1,49},{17,1},{33,17},{49,33},{2,50}... | collective-permute-start | bytes 2334728 | tf_op jit(solution)/shard_map/ppermute | solution.py:562
  157.8 33.3 %collective-permute-start.17 = (f32[152,1280]{1,0:T(8,128)S(1)}, f32[152,1280]{1,0:T(8,128)S(1)}, u32[]{:S(2)}, u32[]{:S(2)}) collective-permute-start(f32[152,1280]{1,0:T(8,128)S(1)} %implicit.3.refs_4_), channel_id=1, source_target_pairs={{0,16},{16,32},{32,48},{48,0},{1,17},{17,33},{33,49},{49,1},{2,18}... | collective-permute-start | bytes 2334728 | tf_op jit(solution)/shard_map/ppermute | solution.py:561
  175.8 34.6 %all-to-all-start.2 = ((f32[16,5,24,128]{3,2,1,0:T(8,128)}), f32[16,5,24,128]{3,2,1,0:T(8,128)}, u32[]{:S(2)}, u32[]{:S(2)}) async-start(f32[16,5,24,128]{3,2,1,0:T(8,128)} %bitcast.8), calls=%async_computation.2 | async-start | bytes 1966080 | tf_op jit(solution)/shard_map/all_to_all | solution.py:536
  187.9 14.2 %collective-permute-start.19 = (f32[80,1280]{1,0:T(8,128)S(1)}, f32[80,1280]{1,0:T(8,128)S(1)}, u32[]{:S(2)}, u32[]{:S(2)}) collective-permute-start(f32[80,1280]{1,0:T(8,128)S(1)} %slice.109), channel_id=1, source_target_pairs={{0,48},{16,0},{32,16},{48,32},{1,49},{17,1},{33,17},{49,33},{2,50}... | collective-permute-start | bytes 1228808 | tf_op jit(solution)/shard_map/ppermute | solution.py:566
  191.1 11.0 %collective-permute-start.18 = (f32[72,1280]{1,0:T(8,128)S(1)}, f32[72,1280]{1,0:T(8,128)S(1)}, u32[]{:S(2)}, u32[]{:S(2)}) collective-permute-start(f32[72,1280]{1,0:T(8,128)S(1)} %slice.108), channel_id=1, source_target_pairs={{0,16},{16,32},{32,48},{48,0},{1,17},{17,33},{33,49},{49,1},{2,18}... | collective-permute-start | bytes 1105928 | tf_op jit(solution)/shard_map/ppermute | solution.py:565
  210.4 18.3 %copy-start.7 = (f32[2,20,128]{2,1,0:T(8,128)S(1)}, f32[2,20,128]{2,1,0:T(8,128)}, u32[]{:S(2)}) copy-start(f32[2,20,128]{2,1,0:T(8,128)} %constant.131.clone.twiddle_ref) | copy-start | bytes 61444
  210.4 18.3 %copy-start.10 = (f32[40]{0:T(128)S(1)}, f32[40]{0:T(128)}, u32[]{:S(2)}) copy-start(f32[40]{0:T(128)} %weight_ref.1) | copy-start | bytes 484
  210.4 18.3 %copy-start.11 = (bf16[256,512]{1,0:T(8,128)(2,1)S(1)}, bf16[256,512]{1,0:T(8,128)(2,1)}, u32[]{:S(2)}) copy-start(bf16[256,512]{1,0:T(8,128)(2,1)} %constant.134.clone.high_ref) | copy-start | bytes 786436
  210.4 18.3 %copy-start.12 = (bf16[256,512]{1,0:T(8,128)(2,1)S(1)}, bf16[256,512]{1,0:T(8,128)(2,1)}, u32[]{:S(2)}) copy-start(bf16[256,512]{1,0:T(8,128)(2,1)} %constant.135.clone.low_ref) | copy-start | bytes 786436

commit v3 on v2

--- a/solution.py
+++ b/solution.py
@@ -88,13 +88,20 @@
     waves = lane_waves()
     second = jnp.where(NM - 1 - column == waves, 1.0, 0.0).astype(BF)
     first = jnp.where(column == waves, 1.0, 0.0).astype(BF)
-    return jnp.concatenate([second, first], axis=0)
-
-
-def fourier_kernel(place_ref, grid_ref, owner_ref, twiddle_ref, high_ref, low_ref, table_ref, *refs):
+    return second, first
+
+
+def fourier_kernel(place_ref, owner_ref, *refs):
     parts = len(CHUNKS)
+    sources, table_ref, refs = refs[:4], refs[4], refs[5:]
     send_refs, away_refs = refs[:parts], refs[parts : 2 * parts]
-    stage_ref, wide_ref, half_ref, sem = refs[2 * parts :]
+    stage_ref, wide_ref, half_ref, sem = refs[2 * parts : 2 * parts + 4]
+    locals_ = refs[2 * parts + 4 :]
+    grid_ref, twiddle_ref, high_ref, low_ref = locals_
+    loads = []
+    for k in range(4):
+        loads.append(pltpu.make_async_copy(sources[k], locals_[k], sem.at[8 * parts + k]))
+        loads[-1].start()
     source = (1 - place_ref[0]) * HALF
     fetches, copies = [], []
     for k, (start, count) in enumerate(CHUNKS):
@@ -115,6 +122,8 @@
                     sem.at[4 * parts + 4 * k + z],
                 )
             )
+    loads[0].wait()
+    loads[1].wait()
     for r in range(ROWS):
         tiles = [grid_ref[:, r, :, N2 * x1 : N2 * (x1 + 1)] for x1 in range(N1)]
         sums = [tiles[x1] + tiles[x1 + 10] for x1 in range(10)]
@@ -142,6 +151,8 @@
                 rows = slice(3 * r, 3 * r + 3)
                 stage_ref[wave // 2, rows, 0:6, base : base + N2] = rotated_real
                 stage_ref[wave // 2, rows, 0:6, base + N2 : base + 256] = rotated_imag
+    loads[2].wait()
+    loads[3].wait()
     for fetch, copy in zip(fetches, copies):
         fetch.wait()
         copy.start()
@@ -152,22 +163,22 @@
             rows = [out[r * 24 + f * 8 : r * 24 + f * 8 + 6] for f in range(3)]
             both = [row[:, :N2] for row in rows] + [row[:, N2:] for row in rows]
             both = jnp.concatenate(both, axis=0)
-            wide_ref[r * 40 : r * 40 + 36, t * N2 : (t + 1) * N2] = both
+            wide_ref[r * 36 : r * 36 + 36, t * N2 : (t + 1) * N2] = both
     high, low = split(wide_ref[...])
 
     for k, (start, count) in enumerate(CHUNKS):
         group = 4 * count
         for c in range(2):
-            picks = one_hot(owner_ref, 64 * start + c * 8 * group, 8 * group)
+            half = 8 * group
+            picks = jnp.concatenate(one_hot(owner_ref, 64 * start + c * half, half), axis=0)
             out = lax.dot_general(picks, high, NT, preferred_element_type=F32)
             out += lax.dot_general(picks, low, NT, preferred_element_type=F32)
-            for r in range(ROWS):
-                lanes = out[:, r * 40 : (r + 1) * 40]
-                half = 8 * group
-                tile = [lanes[:half], lanes[half:], jnp.zeros((half, 48), F32)]
-                tile = jnp.concatenate(tile, axis=1)
-                for w in range(8):
-                    send_refs[k][c * 8 + w, r] = tile[w * group : (w + 1) * group]
+            tile = [out[:half, :180], out[half:, :180], jnp.zeros((half, 24), F32)]
+            tile = jnp.concatenate(tile, axis=1)
+            for w in range(8):
+                for t in range(3):
+                    rows = slice(w * group, (w + 1) * group)
+                    send_refs[k][c * 8 + w, t] = tile[rows, t * N2 : (t + 1) * N2]
     for copy in copies:
         copy.wait()
 
@@ -181,18 +192,18 @@
     for k, (start, count) in enumerate(CHUNKS):
         group = 4 * count
         for c in range(2):
-            picks = one_hot(owner_ref, 64 * start + c * 8 * group, 8 * group)
-            seconds, firsts = [], []
-            for r in range(ROWS):
-                pieces = [got_refs[k][c * 8 + w, r] for w in range(8)]
-                tile = jnp.concatenate(pieces, axis=0) * weight_ref[wave * ROWS + r]
-                seconds.append(tile[:, 0:40])
-                firsts.append(tile[:, 40:80])
-            pad = [jnp.zeros((8 * group, 56), F32)]
-            both = [jnp.concatenate(part + pad, axis=1) for part in (seconds, firsts)]
-            high, low = split(jnp.concatenate(both, axis=0).T)
-            out = lax.dot_general(high, picks, NN, preferred_element_type=F32)
-            out += lax.dot_general(low, picks, NN, preferred_element_type=F32)
+            half = 8 * group
+            second, first = one_hot(owner_ref, 64 * start + c * half, half)
+            tiles = [
+                jnp.concatenate([got_refs[k][c * 8 + w, t] for w in range(8)], axis=0)
+                for t in range(3)
+            ]
+            flipped = jnp.concatenate(tiles, axis=1).T
+            out = jnp.zeros((184, NM), F32)
+            for rows, picks in ((flipped[0:184], second), (flipped[180:364], first)):
+                high, low = split(rows)
+                out += lax.dot_general(high, picks, NN, preferred_element_type=F32)
+                out += lax.dot_general(low, picks, NN, preferred_element_type=F32)
             if fresh:
                 wide_ref[...] = out
             else:
@@ -201,7 +212,8 @@
     for t in range(N1 // 2):
         rows = []
         for r in range(ROWS):
-            block = wide_ref[r * 40 : (r + 1) * 40, t * N2 : (t + 1) * N2]
+            block = wide_ref[r * 36 : (r + 1) * 36, t * N2 : (t + 1) * N2]
+            block = block * weight_ref[wave * ROWS + r]
             gap = jnp.zeros((2, N2), F32)
             real, imag = [], []
             for f in range(3):
@@ -252,10 +264,9 @@
     target, step = pl.program_id(0), pl.program_id(1)
     core, wave = place_ref[0], place_ref[1]
     z = lax.rem(place_ref[2] + relative(rels, target), 4)
-    out_refs, work_ref = refs[:-1], refs[-1]
+    out_refs, work_ref, four_work = refs[:-2], refs[-2], refs[-1]
     extra = count * 36
     group = 4 * count
-    side = 40 * group
 
     @pl.when(step == 0)
     def _():
@@ -267,9 +278,18 @@
     for i in range(2):
         first_wave = owner_ref[wave * 80 + core * HALF + z * 10 + start + 2 * step + i]
         pair = z * count + 2 * step + i
-        mine = four_ref[pl.ds(core * side + pair, HALF, stride=group), :]
-        theirs = four_ref[pl.ds((1 - core) * side + pair, HALF, stride=group), :]
-        four = jnp.concatenate([mine, theirs], axis=0)
+        for b, band in enumerate((core, 1 - core)):
+            base = band * (24 * group) + pair
+            tiles = [
+                four_ref[pl.ds(base + t * group, 8, stride=3 * group), :] for t in range(3)
+            ]
+            line = jnp.concatenate(tiles, axis=1)
+            for r in range(ROWS):
+                pieces = [line[:, r * 36 : r * 36 + 36], jnp.zeros((8, 4), F32)]
+                pieces += [line[:, 180 + r * 36 : 216 + r * 36], jnp.zeros((8, 52), F32)]
+                piece = jnp.concatenate(pieces, axis=1)
+                four_work[pl.ds(i * 80 + b * HALF + r, 8, stride=ROWS), :] = piece
+        four = four_work[i * 80 : (i + 1) * 80, :]
         four_high = four.astype(BF).astype(F32)
         left = jnp.concatenate([four_high, four_high, four - four_high], axis=0).T
         table = jnp.concatenate([own_ref[i], other_ref[i]], axis=0)
@@ -373,21 +393,25 @@
     target, step = pl.program_id(0), pl.program_id(1)
     core, wave = place_ref[0], place_ref[1]
     z = lax.rem(place_ref[2] + relative(rels, target), 4)
-    spec_refs, (out_ref, work_ref) = refs[:-2], refs[-2:]
+    out_ref, work_ref, back_work = refs[-3:]
+    if len(rels) == 1:
+        top_ref, bottom_ref, before_ref = refs[:-3]
+    else:
+        spec_refs = refs[:-3]
     extra = count * 36
     group = 4 * count
-    side = 40 * group
     cut = halves(count)
 
-    for k in range(4):
+    for k in range(len(rels)):
 
         @pl.when((target == k) & (step == 0))
         def _(k=k):
-            if k < 3:
+            if len(rels) == 1:
+                work_ref[:cut] = top_ref[...]
+                work_ref[cut:] = bottom_ref[...]
+                out_ref[...] = before_ref[...]
+            else:
                 work_ref[...] = spec_refs[k][...]
-            else:
-                work_ref[:cut] = spec_refs[3][...]
-                work_ref[cut:] = spec_refs[4][...]
 
     lane = lax.broadcasted_iota(jnp.int32, (1, NM), 1)
     block = work_ref[pl.ds(pl.multiple_of(step * 72, 8), 72), :]
@@ -407,8 +431,17 @@
         spot = pl.multiple_of((2 * step + i) * N2, N2)
         last = work_ref[extra : extra + 1, pl.ds(spot, N2)]
         back = back + table[:, NM : NM + 1] * last
-        out_ref[pl.ds(core * side + pair, HALF, stride=group), :] = back[:HALF]
-        out_ref[pl.ds((1 - core) * side + pair, HALF, stride=group), :] = back[HALF:]
+        back_work[i * 80 : (i + 1) * 80, :] = back
+        for b, band in enumerate((core, 1 - core)):
+            rows = [
+                back_work[pl.ds(i * 80 + b * HALF + r, 8, stride=ROWS), :] for r in range(ROWS)
+            ]
+            line = [row[:, 0:36] for row in rows] + [row[:, 40:76] for row in rows]
+            line = jnp.concatenate(line + [jnp.zeros((8, 24), F32)], axis=1)
+            base = band * (24 * group) + pair
+            for t in range(3):
+                spot = pl.ds(base + t * group, 8, stride=3 * group)
+                out_ref[spot, :] = line[:, t * N2 : (t + 1) * N2]
 
 
 def parameters():
@@ -438,20 +471,24 @@
 
     made = pl.pallas_call(
         fourier_kernel,
-        out_shape=[jax.ShapeDtypeStruct((16, ROWS, 4 * n, N2), F32) for _, n in CHUNKS]
+        out_shape=[jax.ShapeDtypeStruct((16, 3, 4 * n, N2), F32) for _, n in CHUNKS]
         + [jax.ShapeDtypeStruct((4 * n, HALF, PACK), F32) for _, n in CHUNKS],
-        in_specs=[smem] + [whole()] * 5 + [whole(pl.ANY)],
-        out_specs=[whole()] * len(CHUNKS) + [whole(pl.ANY)] * len(CHUNKS),
+        in_specs=[smem, whole()] + [whole(pltpu.HBM)] * 5,
+        out_specs=[whole()] * len(CHUNKS) + [whole(pltpu.HBM)] * len(CHUNKS),
         scratch_shapes=[
             pltpu.VMEM((10, 15, 8, 512), F32),
-            pltpu.VMEM((208, NM), F32),
+            pltpu.VMEM((184, NM), F32),
             pltpu.VMEM((HALF, HALF, PACK), F32),
-            pltpu.SemaphoreType.DMA((8 * len(CHUNKS),)),
+            pltpu.SemaphoreType.DMA((8 * len(CHUNKS) + 4,)),
+            pltpu.VMEM((3, ROWS, 6, NLON), F32),
+            pltpu.VMEM((2, N1, N2), F32),
+            pltpu.VMEM((512, 256), BF),
+            pltpu.VMEM((512, 256), BF),
         ],
         compiler_params=parameters(),
         cost_estimate=cost(4e9, 2.6e7),
         name="fourier",
-    )(place, grad_grid.transpose(0, 2, 1, 3), owner_column, twiddle, *forward, legendre)
+    )(place, owner_column, grad_grid.transpose(0, 2, 1, 3), twiddle, *forward, legendre)
     fours, aways = made[: len(CHUNKS)], made[len(CHUNKS) :]
 
     def zone(rels, t, place):
@@ -486,9 +523,9 @@
             grid_spec=pltpu.PrefetchScalarGridSpec(
                 num_scalar_prefetch=2,
                 grid=(len(rels), count // 2),
-                in_specs=table_specs(start, count, rels) + [kept(320 * count, N2)],
+                in_specs=table_specs(start, count, rels) + [kept(192 * count, N2)],
                 out_specs=[kept(n, NM) for n in rows],
-                scratch_shapes=[pltpu.VMEM((height, NM), F32)],
+                scratch_shapes=[pltpu.VMEM((height, NM), F32), pltpu.VMEM((160, N2), F32)],
             ),
             compiler_params=parameters(),
             cost_estimate=cost(5e7 * count * len(rels), 5e5 * count * len(rels)),
@@ -508,26 +545,22 @@
             name="implicit",
         )(place, owner, *matrices, mine, theirs)
 
-    def grid_rows(start, count, other, blocks):
+    def grid_rows(start, count, rels, other, blocks):
         height = count * 36 + 8
-        cut = halves(count)
-        rels = (0, 1, 3, 2)
-        rows = pl.pallas_call(
+        return pl.pallas_call(
             lambda *refs: grid_rows_kernel(start, count, rels, *refs),
-            out_shape=jax.ShapeDtypeStruct((320 * count, N2), F32),
+            out_shape=jax.ShapeDtypeStruct((192 * count, N2), F32),
             grid_spec=pltpu.PrefetchScalarGridSpec(
                 num_scalar_prefetch=2,
-                grid=(4, count // 2),
-                in_specs=table_specs(start, count, rels)
-                + [kept(n, NM) for n in (height, height, height, cut, height - cut)],
-                out_specs=kept(320 * count, N2),
-                scratch_shapes=[pltpu.VMEM((height, NM), F32)],
+                grid=(len(rels), count // 2),
+                in_specs=table_specs(start, count, rels) + [kept(*b.shape) for b in blocks],
+                out_specs=kept(192 * count, N2),
+                scratch_shapes=[pltpu.VMEM((height, NM), F32), pltpu.VMEM((160, N2), F32)],
             ),
             compiler_params=parameters(),
-            cost_estimate=cost(3e8 * count, 2e6 * count),
+            cost_estimate=cost(7e7 * count * len(rels), 5e5 * count * len(rels)),
             name="grid_rows",
         )(place, owner, legendre, other, *blocks)
-        return rows.reshape(16, ROWS, 4 * count, N2)
 
     def after(value, *earlier):
         return lax.optimization_barrier((value,) + earlier)[0]
@@ -536,28 +569,40 @@
         return lax.all_to_all(value, ("core", "wave"), 0, 0, tiled=True)
 
     steps = [{} for _ in CHUNKS]
+
+    def finish(now, *earlier):
+        up, down = now["moving"]
+        if earlier:
+            up = after(up, *earlier)
+        now["sum"] = now["mine"] + up + down
+        now["theirs"] = lax.ppermute(now["sum"], "yh", SWAP)
+
     for k, (start, count) in enumerate(CHUNKS):
         now, before = steps[k], steps[k - 1] if k else None
         now["cut"] = cut = halves(count)
-        now["other"] = lax.ppermute(aways[k], "core", SWAP)
-        four = fours[k] if k == 0 else after(fours[k], before["opposite"][0])
-        four = exchange(four).reshape(320 * count, N2)
+        away, source = aways[k], fours[k]
         if k:
-            four = after(four, before["right"], before["left"])
-        now["opposite"] = top, bottom = spectra(start, count, (2,), four, now["other"])
+            away = after(away, before["four"])
+            source = after(source, before["right"], before["left"])
+        now["other"] = lax.ppermute(away, "core", SWAP)
+        now["four"] = four = exchange(source).reshape(192 * count, N2)
+        top, bottom = spectra(start, count, (2,), four, now["other"])
+        right, left, now["mine"] = spectra(start, count, (1, 3, 0), four, now["other"])
+        if k:
+            finish(before, now["mine"])
+            top, bottom, _ = lax.optimization_barrier((top, bottom, before["sum"]))
         top = lax.ppermute(top, "z", UP)
         bottom = lax.ppermute(bottom, "z", DOWN)
-        right, left, mine = spectra(start, count, (1, 3, 0), four, now["other"])
-        if k:
-            top = after(top, before["sum"])
         now["right"] = right = right.at[:cut].add(top)
         now["left"] = left = left.at[cut:].add(bottom)
-        now["sum"] = mine + lax.ppermute(right, "z", UP) + lax.ppermute(left, "z", DOWN)
-        now["theirs"] = lax.ppermute(now["sum"], "yh", SWAP)
+        now["moving"] = lax.ppermute(right, "z", UP), lax.ppermute(left, "z", DOWN)
+    finish(steps[-1])
     for k, (start, count) in enumerate(CHUNKS):
         now, before = steps[k], steps[k - 1] if k else None
         theirs = after(now["theirs"], *before["ends"]) if k else now["theirs"]
         now["new"] = new = implicit(start, count, now["sum"], theirs)
+        if k:
+            new = after(new, before["top"], before["bottom"])
         left = lax.ppermute(new, "z", UP)
         right = lax.ppermute(new, "z", DOWN)
         now["left"], now["right"] = left, right
@@ -567,17 +612,19 @@
     results = []
     for k, (start, count) in enumerate(CHUNKS):
         now = steps[k]
-        top = now["top"]
-        if k + 1 < len(CHUNKS):
-            top = after(top, steps[k + 1]["new"])
-        blocks = (now["new"], now["right"], now["left"], top, now["bottom"])
-        results.append(exchange(grid_rows(start, count, now["other"], blocks)))
+        later = steps[k + 1] if k + 1 < len(CHUNKS) else None
+        right, top = now["right"], now["top"]
+        if later:
+            right = after(right, later["new"])
+        rows = grid_rows(start, count, (0, 1, 3), now["other"], (now["new"], right, now["left"]))
+        rows = grid_rows(start, count, (2,), now["other"], (top, now["bottom"], rows))
+        results.append(exchange(rows.reshape(16, 3, 4 * count, N2)))
     out = pl.pallas_call(
         inverse_kernel,
         out_shape=jax.ShapeDtypeStruct((3, ROWS, 6, NLON), F32),
         in_specs=[whole()] + [smem] * 2 + [whole()] * (3 + len(CHUNKS)),
         out_specs=whole(),
-        scratch_shapes=[pltpu.VMEM((N1, 120, 256), F32), pltpu.VMEM((256, NM), F32)],
+        scratch_shapes=[pltpu.VMEM((N1, 120, 256), F32), pltpu.VMEM((184, NM), F32)],
         compiler_params=parameters(),
         cost_estimate=cost(4e9, 8e6),
         name="inverse",

time: 237 us -> 221 us (0.932)
  waiting for transfers between devices: 69.9 us -> 55 us
  other arithmetic: 5.75 us -> 10.9 us
  blocking collectives: 35.7 us -> 31.4 us
  local copies, waits for them, and re-layouts: 8.15 us -> 5.75 us
    ppermute x2, waiting for transfers between devices: 0.01 us -> 18.7 us  [per_device(): right = lax.ppermute(new, 'z', DOWN)]
    ppermute x2, waiting for transfers between devices: 18.6 us -> 0.01 us  [per_device(): left = lax.ppermute(new, 'z', UP)]
    ppermute x4, waiting for transfers between devices: 18.3 us -> 7.73 us  [the longest x2 7.73 us: finish(): now['theirs'] = lax.ppermute(now['sum'], 'yh', SWAP)]
    ppermute x2, waiting for transfers between devices: 14.8 us -> 6.9 us  [per_device(): now['top'] = lax.ppermute(now['ends'][0], 'z', UP)]
    all_to_all x2, waiting for transfers between devices: 15.3 us -> 8.54 us  [exchange(): return lax.all_to_all(value, ('core', 'wave'), 0, 0, tiled=True)]
    all_to_all x2, starting transfers between devices: 17.6 us -> 12.7 us  [exchange(): return lax.all_to_all(value, ('core', 'wave'), 0, 0, tiled=True)]
    ppermute x2, waiting for transfers between devices: 0.01 us -> 4.88 us  [per_device(): now['bottom'] = lax.ppermute(now['ends'][1], 'z', DOWN)]
    ppermute x2, waiting for transfers between devices: 2.82 us -> 7.6 us  [per_device(): top = lax.ppermute(top, 'z', UP)]
  transfers between devices with their start and end apart: 22 -> 22, of which waited for: 6 -> 10; matrix products, arithmetic and copies ran while one was open for 3% -> 4% of each run, Pallas kernels for 22% -> 26%
where the time goes in v3:
time: 221 us; the launch traced here: 220 us
  Pallas kernels  71.8 us (32%)
  waiting for transfers between devices  55 us (25%)
  starting transfers between devices  44.6 us (20%)
  blocking collectives  31.4 us (14%)
  other arithmetic  10.9 us (5%)
  local copies, waits for them, and re-layouts  5.75 us (3%)
    all_to_all x2, blocking collectives, exchange(): return lax.all_to_all(value, ('core', 'wave'), 0, 0, tiled=True)  31.4 us
    pallas_call x4, Pallas kernels, spectra(): pl.pallas_call(lambda *refs: spectra_kernel(start, count, rels, *refs), o...  25 us
    pallas_call x4, Pallas kernels, grid_rows(): pl.pallas_call(lambda *refs: grid_rows_kernel(start, count, rels, *refs),...  23.7 us
    ppermute x2, waiting for transfers between devices, per_device(): right = lax.ppermute(new, 'z', DOWN)  18.7 us
    all_to_all x2, starting transfers between devices, exchange(): return lax.all_to_all(value, ('core', 'wave'), 0, 0, tiled=True)  12.7 us
    all_to_all x2, waiting for transfers between devices, exchange(): return lax.all_to_all(value, ('core', 'wave'), 0, 0, tiled=True)  8.54 us
    pallas_call x2, Pallas kernels, implicit(): pl.pallas_call(lambda *refs: implicit_kernel(start, count, *refs), out_sh...  8.48 us
    pallas_call x1, Pallas kernels, per_device(): pl.pallas_call(fourier_kernel, out_shape=[jax.ShapeDtypeStruct((16, 3, 4...  8.47 us
  transfers between devices with their start and end apart: 22, of which 10 were waited for; matrix products, arithmetic and copies ran while one was open for 4% of the time, Pallas kernels for 26%

profile of v3, /device:TPU:1, one launch (start us, length us, event | category | flops | bytes accessed | tf_op | source)
XLA Modules:
  0.0 219.8 jit_solution(6629031989791573312)
XLA Ops:
  0.0 0.8 reshape.129
  1.5 1.3 copy-done.1
  2.8 0.9 copy-done.3
  3.7 0.9 copy-done.4
  4.7 0.7 copy-done.5
  5.4 8.5 %fourier.1 = (f32[16,3,24,128]{3,2,1,0:T(8,128)S(1)}, f32[16,3,16,128]{3,2,1,0:T(8,128)}, f32[24,40,1408]{2,1,0:T(8,128)S(1)}, f32[16,40,1408]{2,1,0:T(8,128)}) custom-call(s32[3]{0:T(128)S(1)} %pad_add_fusion.1.place_ref.refs_0_, s32[640,128]{1,0:T(8,128)S(1)} %broadcast_in_dim.2.owner_ref, f32[3,5,6,2560]{3,2,1,0:T(8,128)S(1)} %bitcast.20, ...), custom_call_target="tpu_custom_call" | custom-call | flops 4000000000 | bytes 26000000 | tf_op jit(solution)/shard_map/fourier/pallas_call | solution.py:472
  13.9 1.5 collective-permute-start
  15.4 16.4 %all_to_all.20 = f32[16,3,24,128]{3,2,1,0:T(8,128)S(1)} all-to-all(f32[16,3,24,128]{3,2,1,0:T(8,128)S(1)} %get-tuple-element.76), channel_id=1, replica_groups=mesh['yh'=2,'z'=4,'core'=2,'wave'=8] {'core','wave'}, dimensions={0} | all-to-all | bytes 1179648 | tf_op jit(solution)/shard_map/all_to_all | solution.py:569
  31.8 0.8 collective-permute-start.3
  32.6 4.2 %spectra.5 = (f32[112,1280]{1,0:T(8,128)S(1)}, f32[112,1280]{1,0:T(8,128)S(1)}) custom-call(s32[3]{0:T(128)S(1)} %pad_add_fusion.1.place_ref.refs_0_, s32[640]{0:T(1024)S(1)} %copy-done.2, f32[80,40,1408]{2,1,0:T(8,128)} %refs_2_.16, f32[24,40,1408]{2,1,0:T(8,128)S(1)} %collective-permute-done.refs_3_, f32[1152,128]{1,0:T(8,128)S(1)} %bitcast.15), custom_call_target="tpu_custom_call" | custom-call | flops 300000000 | bytes 3000000 | tf_op jit(solution)/shard_map/spectra/pallas_call | solution.py:520
  36.8 1.7 collective-permute-start.1
  38.5 2.2 %collective-permute-start.4 = (f32[112,1280]{1,0:T(8,128)S(1)}, f32[112,1280]{1,0:T(8,128)S(1)}, u32[]{:S(2)}, u32[]{:S(2)}) collective-permute-start(f32[112,1280]{1,0:T(8,128)S(1)} %get-tuple-element.84), channel_id=1, source_target_pairs={{0,48},{16,0},{32,16},{48,32},{1,49},{17,1},{33,17},{49,33},{2,50}... | collective-permute-start | bytes 1720328 | tf_op jit(solution)/shard_map/ppermute | solution.py:595
  40.7 10.1 %spectra.4 = (f32[224,1280]{1,0:T(8,128)}, f32[224,1280]{1,0:T(8,128)}, f32[224,1280]{1,0:T(8,128)S(1)}) custom-call(s32[3]{0:T(128)S(1)} %pad_add_fusion.1.place_ref.refs_0_, s32[640]{0:T(1024)S(1)} %copy-done.2, f32[80,40,1408]{2,1,0:T(8,128)} %refs_2_.16, f32[24,40,1408]{2,1,0:T(8,128)S(1)} %collective-permute-done.refs_3_, f32[1152,128]{1,0:T(8,128)S(1)} %bitcast.16), custom_call_target="tpu_custom_call" | custom-call | flops 900000000 | bytes 9000000 | tf_op jit(solution)/shard_map/spectra/pallas_call | solution.py:520
  50.8 3.2 %collective-permute-done.1 = f32[112,1280]{1,0:T(8,128)S(1)} collective-permute-done((f32[112,1280]{1,0:T(8,128)S(1)}, f32[112,1280]{1,0:T(8,128)S(1)}, u32[]{:S(2)}, u32[]{:S(2)}) %collective-permute-start.1) | collective-permute-done | bytes 573472 | tf_op jit(solution)/shard_map/ppermute | solution.py:594
  54.0 1.9 add_dynamic-update-slice_fusion.1
  55.9 2.0 add_dynamic-update-slice_fusion
  57.9 2.7 %collective-permute-start.5 = (f32[224,1280]{1,0:T(8,128)}, f32[224,1280]{1,0:T(8,128)}, u32[]{:S(2)}, u32[]{:S(2)}) collective-permute-start(f32[224,1280]{1,0:T(8,128)} %add_dynamic-update-slice_fusion), channel_id=1, source_target_pairs={{0,48},{16,0},{32,16},{48,32},{1,49},{17,1},{33,17},{49,33},{2,50}... | collective-permute-start | bytes 3440648 | tf_op jit(solution)/shard_map/ppermute | solution.py:598
  60.5 4.5 %all-to-all-start.1 = ((f32[16,3,16,128]{3,2,1,0:T(8,128)}), f32[16,3,16,128]{3,2,1,0:T(8,128)S(1)}, u32[]{:S(2)}, u32[]{:S(2)}) async-start(f32[16,3,16,128]{3,2,1,0:T(8,128)} %get-tuple-element.85), calls=%async_computation.1 | async-start | bytes 786432 | tf_op jit(solution)/shard_map/all_to_all | solution.py:569
  65.1 8.5 %all-to-all-done.1 = f32[16,3,16,128]{3,2,1,0:T(8,128)S(1)} async-done(((f32[16,3,16,128]{3,2,1,0:T(8,128)}), f32[16,3,16,128]{3,2,1,0:T(8,128)S(1)}, u32[]{:S(2)}, u32[]{:S(2)}) %all-to-all-start.1) | async-done | bytes 393248 | tf_op jit(solution)/shard_map/all_to_all | solution.py:569
  73.6 3.0 %spectra.7 = (f32[72,1280]{1,0:T(8,128)S(1)}, f32[80,1280]{1,0:T(8,128)S(1)}) custom-call(s32[3]{0:T(128)S(1)} %pad_add_fusion.1.place_ref.refs_0_, s32[640]{0:T(1024)S(1)} %copy-done.2, f32[80,40,1408]{2,1,0:T(8,128)} %refs_2_.16, f32[16,40,1408]{2,1,0:T(8,128)} %collective-permute-done.3.refs_3_, f32[768,128]{1,0:T(8,128)S(1)} %bitcast.17), custom_call_target="tpu_custom_call" | custom-call | flops 200000000 | bytes 2000000 | tf_op jit(solution)/shard_map/spectra/pallas_call | solution.py:520
  76.6 7.8 %spectra.6 = (f32[152,1280]{1,0:T(8,128)}, f32[152,1280]{1,0:T(8,128)}, f32[152,1280]{1,0:T(8,128)S(1)}) custom-call(s32[3]{0:T(128)S(1)} %pad_add_fusion.1.place_ref.refs_0_, s32[640]{0:T(1024)S(1)} %copy-done.2, f32[80,40,1408]{2,1,0:T(8,128)} %refs_2_.16, f32[16,40,1408]{2,1,0:T(8,128)} %collective-permute-done.3.refs_3_, f32[768,128]{1,0:T(8,128)S(1)} %bitcast.18), custom_call_target="tpu_custom_call" | custom-call | flops 600000000 | bytes 6000000 | tf_op jit(solution)/shard_map/spectra/pallas_call | solution.py:520
  84.6 1.8 add_add_fusion.refs_7_
  86.5 2.6 %collective-permute-start.6 = (f32[224,1280]{1,0:T(8,128)S(1)}, f32[224,1280]{1,0:T(8,128)S(1)}, u32[]{:S(2)}, u32[]{:S(2)}) collective-permute-start(f32[224,1280]{1,0:T(8,128)S(1)} %add_add_fusion.refs_7_), channel_id=1, source_target_pairs={{0,64},{64,0},{1,65},{65,1},{2,66},{66,2},{3,67},{67,3},{4,68},{68... | collective-permute-start | bytes 3440648 | tf_op jit(solution)/shard_map/ppermute | solution.py:578
  89.2 3.4 %collective-permute-start.13 = (f32[80,1280]{1,0:T(8,128)S(1)}, f32[80,1280]{1,0:T(8,128)S(1)}, u32[]{:S(2)}, u32[]{:S(2)}) collective-permute-start(f32[80,1280]{1,0:T(8,128)S(1)} %get-tuple-element.93), channel_id=1, source_target_pairs={{0,48},{16,0},{32,16},{48,32},{1,49},{17,1},{33,17},{49,33},{2,50}... | collective-permute-start | bytes 1228808 | tf_op jit(solution)/shard_map/ppermute | solution.py:595
  92.6 4.4 %collective-permute-done.11 = f32[72,1280]{1,0:T(8,128)S(1)} collective-permute-done((f32[72,1280]{1,0:T(8,128)S(1)}, f32[72,1280]{1,0:T(8,128)S(1)}, u32[]{:S(2)}, u32[]{:S(2)}) %collective-permute-start.11) | collective-permute-done | bytes 368672 | tf_op jit(solution)/shard_map/ppermute | solution.py:594
  97.0 1.8 add_dynamic-update-slice_fusion.3
  99.3 1.8 add_dynamic-update-slice_fusion.2
  101.1 3.4 %collective-permute-start.14 = (f32[152,1280]{1,0:T(8,128)}, f32[152,1280]{1,0:T(8,128)}, u32[]{:S(2)}, u32[]{:S(2)}) collective-permute-start(f32[152,1280]{1,0:T(8,128)} %add_dynamic-update-slice_fusion.2), channel_id=1, source_target_pairs={{0,48},{16,0},{32,16},{48,32},{1,49},{17,1},{33,17},{49,33},{2,50}... | collective-permute-start | bytes 2334728 | tf_op jit(solution)/shard_map/ppermute | solution.py:598
  104.8 7.7 %collective-permute-done.6.refs_8_ = f32[224,1280]{1,0:T(8,128)S(1)} collective-permute-done((f32[224,1280]{1,0:T(8,128)S(1)}, f32[224,1280]{1,0:T(8,128)S(1)}, u32[]{:S(2)}, u32[]{:S(2)}) %collective-permute-start.6) | collective-permute-done | bytes 1146912 | tf_op jit(solution)/shard_map/ppermute | solution.py:578
  112.5 4.2 %implicit.2.refs_4_ = f32[224,1280]{1,0:T(8,128)S(1)} custom-call(s32[3]{0:T(128)S(1)} %pad_add_fusion.1.place_ref.refs_0_, s32[640]{0:T(1024)S(1)} %copy-done.2, f32[36]{0:T(128)S(1)} %reshape.132.refs_2_, f32[36]{0:T(128)S(1)} %reshape.133.refs_3_, f32[6]{0:T(128)S(1)} %copy-done.7, f32[36]{0:T(128)S(1)} %reshape.134.refs_5_, f32[36]{0:T(128)S(1)} %reshape.135.refs_6_, ...), custom_call_target="tpu_custom_call" | custom-call | flops 60000000 | bytes 3600000 | tf_op jit(solution)/shard_map/implicit/pallas_call | solution.py:537
  116.8 4.0 %collective-permute-start.9 = (f32[224,1280]{1,0:T(8,128)S(1)}, f32[224,1280]{1,0:T(8,128)S(1)}, u32[]{:S(2)}, u32[]{:S(2)}) collective-permute-start(f32[224,1280]{1,0:T(8,128)S(1)} %implicit.2.refs_4_), channel_id=1, source_target_pairs={{0,48},{16,0},{32,16},{48,32},{1,49},{17,1},{33,17},{49,33},{2,50}... | collective-permute-start | bytes 3440648 | tf_op jit(solution)/shard_map/ppermute | solution.py:607
  120.8 1.5 add_add_fusion.1.refs_7_
  122.3 2.8 %collective-permute-start.15 = (f32[152,1280]{1,0:T(8,128)S(1)}, f32[152,1280]{1,0:T(8,128)S(1)}, u32[]{:S(2)}, u32[]{:S(2)}) collective-permute-start(f32[152,1280]{1,0:T(8,128)S(1)} %add_add_fusion.1.refs_7_), channel_id=1, source_target_pairs={{0,64},{64,0},{1,65},{65,1},{2,66},{66,2},{3,67},{67,3},{4,68},{68... | collective-permute-start | bytes 2334728 | tf_op jit(solution)/shard_map/ppermute | solution.py:578
  125.1 18.7 %collective-permute-done.9.refs_5_ = f32[224,1280]{1,0:T(8,128)S(1)} collective-permute-done((f32[224,1280]{1,0:T(8,128)S(1)}, f32[224,1280]{1,0:T(8,128)S(1)}, u32[]{:S(2)}, u32[]{:S(2)}) %collective-permute-start.9) | collective-permute-done | bytes 1146912 | tf_op jit(solution)/shard_map/ppermute | solution.py:607
  143.9 3.5 %collective-permute-start.10 = (f32[112,1280]{1,0:T(8,128)S(1)}, f32[112,1280]{1,0:T(8,128)S(1)}, u32[]{:S(2)}, u32[]{:S(2)}) collective-permute-start(f32[112,1280]{1,0:T(8,128)S(1)} %slice.107), channel_id=1, source_target_pairs={{0,48},{16,0},{32,16},{48,32},{1,49},{17,1},{33,17},{49,33},{2,50}... | collective-permute-start | bytes 1720328 | tf_op jit(solution)/shard_map/ppermute | solution.py:611
  147.5 4.2 %implicit.3.refs_4_ = f32[152,1280]{1,0:T(8,128)S(1)} custom-call(s32[3]{0:T(128)S(1)} %pad_add_fusion.1.place_ref.refs_0_, s32[640]{0:T(1024)S(1)} %copy-done.2, f32[36]{0:T(128)S(1)} %reshape.132.refs_2_, f32[36]{0:T(128)S(1)} %reshape.133.refs_3_, f32[6]{0:T(128)S(1)} %copy-done.7, f32[36]{0:T(128)S(1)} %reshape.134.refs_5_, f32[36]{0:T(128)S(1)} %reshape.135.refs_6_, ...), custom_call_target="tpu_custom_call" | custom-call | flops 40000000 | bytes 2400000 | tf_op jit(solution)/shard_map/implicit/pallas_call | solution.py:537
  151.8 4.9 %collective-permute-done.10.refs_5_ = f32[112,1280]{1,0:T(8,128)S(1)} collective-permute-done((f32[112,1280]{1,0:T(8,128)S(1)}, f32[112,1280]{1,0:T(8,128)S(1)}, u32[]{:S(2)}, u32[]{:S(2)}) %collective-permute-start.10) | collective-permute-done | bytes 573472 | tf_op jit(solution)/shard_map/ppermute | solution.py:611
  156.6 3.2 %collective-permute-done.8.refs_4_ = f32[112,1280]{1,0:T(8,128)S(1)} collective-permute-done((f32[112,1280]{1,0:T(8,128)S(1)}, f32[112,1280]{1,0:T(8,128)S(1)}, u32[]{:S(2)}, u32[]{:S(2)}) %collective-permute-start.8) | collective-permute-done | bytes 573472 | tf_op jit(solution)/shard_map/ppermute | solution.py:610
  160.0 1.3 collective-permute-start.16
  161.4 9.0 %grid_rows.4.refs_6_ = f32[1152,128]{1,0:T(8,128)S(1)} custom-call(s32[3]{0:T(128)S(1)} %pad_add_fusion.1.place_ref.refs_0_, s32[640]{0:T(1024)S(1)} %copy-done.2, f32[80,40,1408]{2,1,0:T(8,128)} %refs_2_.16, f32[24,40,1408]{2,1,0:T(8,128)S(1)} %bitcast.14, f32[224,1280]{1,0:T(8,128)S(1)} %implicit.2.refs_4_, ...), custom_call_target="tpu_custom_call" | custom-call | flops 1260000000 | bytes 9000000 | tf_op jit(solution)/shard_map/grid_rows/pallas_call | solution.py:550
  170.4 4.8 %grid_rows.5 = f32[1152,128]{1,0:T(8,128)} custom-call(s32[3]{0:T(128)S(1)} %pad_add_fusion.1.place_ref.refs_0_, s32[640]{0:T(1024)S(1)} %copy-done.2, f32[80,40,1408]{2,1,0:T(8,128)} %refs_2_.16, f32[24,40,1408]{2,1,0:T(8,128)S(1)} %bitcast.14, f32[112,1280]{1,0:T(8,128)S(1)} %collective-permute-done.8.refs_4_, ...), custom_call_target="tpu_custom_call" | custom-call | flops 420000000 | bytes 3000000 | tf_op jit(solution)/shard_map/grid_rows/pallas_call | solution.py:550
  175.1 8.2 %all-to-all-start.2 = ((f32[16,3,24,128]{3,2,1,0:T(8,128)}), f32[16,3,24,128]{3,2,1,0:T(8,128)S(1)}, u32[]{:S(2)}, u32[]{:S(2)}) async-start(f32[16,3,24,128]{3,2,1,0:T(8,128)} %bitcast.8), calls=%async_computation.2 | async-start | bytes 1179648 | tf_op jit(solution)/shard_map/all_to_all | solution.py:569
  183.4 1.2 collective-permute-start.19
  185.0 6.8 %grid_rows.6.refs_6_ = f32[768,128]{1,0:T(8,128)S(1)} custom-call(s32[3]{0:T(128)S(1)} %pad_add_fusion.1.place_ref.refs_0_, s32[640]{0:T(1024)S(1)} %copy-done.2, f32[80,40,1408]{2,1,0:T(8,128)} %refs_2_.16, f32[16,40,1408]{2,1,0:T(8,128)} %collective-permute-done.3.refs_3_, f32[152,1280]{1,0:T(8,128)S(1)} %implicit.3.refs_4_, ...), custom_call_target="tpu_custom_call" | custom-call | flops 840000000 | bytes 6000000 | tf_op jit(solution)/shard_map/grid_rows/pallas_call | solution.py:550
  191.9 3.7 %collective-permute-done.17.refs_4_ = f32[72,1280]{1,0:T(8,128)S(1)} collective-permute-done((f32[72,1280]{1,0:T(8,128)S(1)}, f32[72,1280]{1,0:T(8,128)S(1)}, u32[]{:S(2)}, u32[]{:S(2)}) %collective-permute-start.17) | collective-permute-done | bytes 368672 | tf_op jit(solution)/shard_map/ppermute | solution.py:610
  195.5 3.1 %grid_rows.7 = f32[768,128]{1,0:T(8,128)S(1)} custom-call(s32[3]{0:T(128)S(1)} %pad_add_fusion.1.place_ref.refs_0_, s32[640]{0:T(1024)S(1)} %copy-done.2, f32[80,40,1408]{2,1,0:T(8,128)} %refs_2_.16, f32[16,40,1408]{2,1,0:T(8,128)} %collective-permute-done.3.refs_3_, f32[72,1280]{1,0:T(8,128)S(1)} %collective-permute-done.17.refs_4_, ...), custom_call_target="tpu_custom_call" | custom-call | flops 280000000 | bytes 2000000 | tf_op jit(solution)/shard_map/grid_rows/pallas_call | solution.py:550
  198.7 15.0 %all_to_all.21.refs_1_ = f32[16,3,16,128]{3,2,1,0:T(8,128)S(1)} all-to-all(f32[16,3,16,128]{3,2,1,0:T(8,128)S(1)} %bitcast.19), channel_id=1, replica_groups=mesh['yh'=2,'z'=4,'core'=2,'wave'=8] {'core','wave'}, dimensions={0} | all-to-all | bytes 786432 | tf_op jit(solution)/shard_map/all_to_all | solution.py:569
  213.7 6.1 %inverse.1 = f32[3,5,6,2560]{3,2,1,0:T(8,128)} custom-call(s32[640,128]{1,0:T(8,128)S(1)} %broadcast_in_dim.2.owner_ref, f32[40]{0:T(128)S(1)} %copy-done.8, s32[3]{0:T(128)S(1)} %pad_add_fusion.1.place_ref.refs_0_, f32[2,20,128]{2,1,0:T(8,128)S(1)} %copy-done.6, bf16[256,512]{1,0:T(8,128)(2,1)S(1)} %copy-done.10, bf16[256,512]{1,0:T(8,128)(2,1)S(1)} %copy-done.9, ...), custom_call_target="tpu_custom_call" | custom-call | flops 4000000000 | bytes 8000000 | tf_op jit(solution)/shard_map/inverse/pallas_call | solution.py:622
  (69 shorter events, 2.6 us)
Async XLA Ops:
  1.5 1.3 copy-start.1
  2.8 0.9 copy-start.3
  3.7 0.9 copy-start.4
  4.7 0.7 copy-start.5
  13.9 18.7 %copy-start.2 = (s32[640]{0:T(1024)S(1)}, s32[640]{0:T(1024)}, u32[]{:S(2)}) copy-start(s32[640]{0:T(1024)} %refs_1_.20) | copy-start | bytes 7684
  13.9 18.7 %collective-permute-start = (f32[24,40,1408]{2,1,0:T(8,128)S(1)}, f32[24,40,1408]{2,1,0:T(8,128)S(1)}, u32[]{:S(2)}, u32[]{:S(2)}) collective-permute-start(f32[24,40,1408]{2,1,0:T(8,128)S(1)} %get-tuple-element.75), channel_id=1, source_target_pairs={{0,8},{8,0},{1,9},{9,1},{2,10},{10,2},{3,11},{11,3},{4,12},{12,4},... | collective-permute-start | bytes 16220168 | tf_op jit(solution)/shard_map/ppermute | solution.py:587
  31.8 33.2 %collective-permute-start.3 = (f32[16,40,1408]{2,1,0:T(8,128)}, f32[16,40,1408]{2,1,0:T(8,128)}, u32[]{:S(2)}, u32[]{:S(2)}) collective-permute-start(f32[16,40,1408]{2,1,0:T(8,128)} %get-tuple-element.81), channel_id=1, source_target_pairs={{0,8},{8,0},{1,9},{9,1},{2,10},{10,2},{3,11},{11,3},{4,12},{12,4},... | collective-permute-start | bytes 10813448 | tf_op jit(solution)/shard_map/ppermute | solution.py:587
  32.6 8.1 %copy-start = (f32[24,40,1408]{2,1,0:T(8,128)}, f32[24,40,1408]{2,1,0:T(8,128)S(1)}, u32[]{:S(2)}) copy-start(f32[24,40,1408]{2,1,0:T(8,128)S(1)} %collective-permute-done.refs_3_) | copy-start | bytes 16220164
  36.8 17.2 %collective-permute-start.1 = (f32[112,1280]{1,0:T(8,128)S(1)}, f32[112,1280]{1,0:T(8,128)S(1)}, u32[]{:S(2)}, u32[]{:S(2)}) collective-permute-start(f32[112,1280]{1,0:T(8,128)S(1)} %get-tuple-element.79), channel_id=1, source_target_pairs={{0,16},{16,32},{32,48},{48,0},{1,17},{17,33},{33,49},{49,1},{2,18}... | collective-permute-start | bytes 1720328 | tf_op jit(solution)/shard_map/ppermute | solution.py:594
  38.5 17.4 %collective-permute-start.4 = (f32[112,1280]{1,0:T(8,128)S(1)}, f32[112,1280]{1,0:T(8,128)S(1)}, u32[]{:S(2)}, u32[]{:S(2)}) collective-permute-start(f32[112,1280]{1,0:T(8,128)S(1)} %get-tuple-element.84), channel_id=1, source_target_pairs={{0,48},{16,0},{32,16},{48,32},{1,49},{17,1},{33,17},{49,33},{2,50}... | collective-permute-start | bytes 1720328 | tf_op jit(solution)/shard_map/ppermute | solution.py:595
  55.9 28.5 %collective-permute-start.2 = (f32[224,1280]{1,0:T(8,128)}, f32[224,1280]{1,0:T(8,128)}, u32[]{:S(2)}, u32[]{:S(2)}) collective-permute-start(f32[224,1280]{1,0:T(8,128)} %add_dynamic-update-slice_fusion.1), channel_id=1, source_target_pairs={{0,16},{16,32},{32,48},{48,0},{1,17},{17,33},{33,49},{49,1},{2,18}... | collective-permute-start | bytes 3440648 | tf_op jit(solution)/shard_map/ppermute | solution.py:598
  57.9 26.7 %collective-permute-start.5 = (f32[224,1280]{1,0:T(8,128)}, f32[224,1280]{1,0:T(8,128)}, u32[]{:S(2)}, u32[]{:S(2)}) collective-permute-start(f32[224,1280]{1,0:T(8,128)} %add_dynamic-update-slice_fusion), channel_id=1, source_target_pairs={{0,48},{16,0},{32,16},{48,32},{1,49},{17,1},{33,17},{49,33},{2,50}... | collective-permute-start | bytes 3440648 | tf_op jit(solution)/shard_map/ppermute | solution.py:598
  60.5 13.1 %all-to-all-start.1 = ((f32[16,3,16,128]{3,2,1,0:T(8,128)}), f32[16,3,16,128]{3,2,1,0:T(8,128)S(1)}, u32[]{:S(2)}, u32[]{:S(2)}) async-start(f32[16,3,16,128]{3,2,1,0:T(8,128)} %get-tuple-element.85), calls=%async_computation.1 | async-start | bytes 786432 | tf_op jit(solution)/shard_map/all_to_all | solution.py:569
  86.4 10.6 %collective-permute-start.11 = (f32[72,1280]{1,0:T(8,128)S(1)}, f32[72,1280]{1,0:T(8,128)S(1)}, u32[]{:S(2)}, u32[]{:S(2)}) collective-permute-start(f32[72,1280]{1,0:T(8,128)S(1)} %get-tuple-element.91), channel_id=1, source_target_pairs={{0,16},{16,32},{32,48},{48,0},{1,17},{17,33},{33,49},{49,1},{2,18}... | collective-permute-start | bytes 1105928 | tf_op jit(solution)/shard_map/ppermute | solution.py:594
  86.5 26.0 %collective-permute-start.6 = (f32[224,1280]{1,0:T(8,128)S(1)}, f32[224,1280]{1,0:T(8,128)S(1)}, u32[]{:S(2)}, u32[]{:S(2)}) collective-permute-start(f32[224,1280]{1,0:T(8,128)S(1)} %add_add_fusion.refs_7_), channel_id=1, source_target_pairs={{0,64},{64,0},{1,65},{65,1},{2,66},{66,2},{3,67},{67,3},{4,68},{68... | collective-permute-start | bytes 3440648 | tf_op jit(solution)/shard_map/ppermute | solution.py:578
  89.2 10.1 %collective-permute-start.13 = (f32[80,1280]{1,0:T(8,128)S(1)}, f32[80,1280]{1,0:T(8,128)S(1)}, u32[]{:S(2)}, u32[]{:S(2)}) collective-permute-start(f32[80,1280]{1,0:T(8,128)S(1)} %get-tuple-element.93), channel_id=1, source_target_pairs={{0,48},{16,0},{32,16},{48,32},{1,49},{17,1},{33,17},{49,33},{2,50}... | collective-permute-start | bytes 1228808 | tf_op jit(solution)/shard_map/ppermute | solution.py:595
  97.0 7.5 %copy-start.11 = (f32[6,6]{1,0:T(8,128)S(1)}, f32[6,6]{1,0:T(8,128)}, u32[]{:S(2)}) copy-start(f32[6,6]{1,0:T(8,128)} %param.26) | copy-start | bytes 436
  97.0 7.6 %copy-start.12 = (f32[6,6]{1,0:T(8,128)S(1)}, f32[6,6]{1,0:T(8,128)}, u32[]{:S(2)}) copy-start(f32[6,6]{1,0:T(8,128)} %param.27) | copy-start | bytes 436
  97.0 7.7 %copy-start.13 = (f32[6,6]{1,0:T(8,128)S(1)}, f32[6,6]{1,0:T(8,128)}, u32[]{:S(2)}) copy-start(f32[6,6]{1,0:T(8,128)} %param.29) | copy-start | bytes 436
  97.0 7.7 %copy-start.14 = (f32[6,6]{1,0:T(8,128)S(1)}, f32[6,6]{1,0:T(8,128)}, u32[]{:S(2)}) copy-start(f32[6,6]{1,0:T(8,128)} %param.30) | copy-start | bytes 436
  97.0 15.5 %copy-start.7 = (f32[6]{0:T(128)S(1)}, f32[6]{0:T(128)}, u32[]{:S(2)}) copy-start(f32[6]{0:T(128)} %refs_4_.5) | copy-start | bytes 76
  98.8 21.9 %collective-permute-start.12 = (f32[152,1280]{1,0:T(8,128)}, f32[152,1280]{1,0:T(8,128)}, u32[]{:S(2)}, u32[]{:S(2)}) collective-permute-start(f32[152,1280]{1,0:T(8,128)} %add_dynamic-update-slice_fusion.3), channel_id=1, source_target_pairs={{0,16},{16,32},{32,48},{48,0},{1,17},{17,33},{33,49},{49,1},{2,18}... | collective-permute-start | bytes 2334728 | tf_op jit(solution)/shard_map/ppermute | solution.py:598
  101.1 19.7 %collective-permute-start.14 = (f32[152,1280]{1,0:T(8,128)}, f32[152,1280]{1,0:T(8,128)}, u32[]{:S(2)}, u32[]{:S(2)}) collective-permute-start(f32[152,1280]{1,0:T(8,128)} %add_dynamic-update-slice_fusion.2), channel_id=1, source_target_pairs={{0,48},{16,0},{32,16},{48,32},{1,49},{17,1},{33,17},{49,33},{2,50}... | collective-permute-start | bytes 2334728 | tf_op jit(solution)/shard_map/ppermute | solution.py:598
  112.5 48.8 %slice-start = ((s8[5406720]{0:T(1024)(128)(4,1)}), s8[4194304]{0:T(1024)(128)(4,1)S(1)}, s32[]{:S(2)}) async-start(s8[5406720]{0:T(1024)(128)(4,1)} %bitcast.13), calls=%async_computation.4 | async-start | bytes 8388608
  116.8 44.6 %slice-start.1 = ((s8[5406720]{0:T(1024)(128)(4,1)}), s8[1212416]{0:T(1024)(128)(4,1)S(1)}, s32[]{:S(2)}) async-start(s8[5406720]{0:T(1024)(128)(4,1)} %bitcast.13), calls=%async_computation.5 | async-start | bytes 2424832
  116.8 27.1 %collective-permute-start.9 = (f32[224,1280]{1,0:T(8,128)S(1)}, f32[224,1280]{1,0:T(8,128)S(1)}, u32[]{:S(2)}, u32[]{:S(2)}) collective-permute-start(f32[224,1280]{1,0:T(8,128)S(1)} %implicit.2.refs_4_), channel_id=1, source_target_pairs={{0,48},{16,0},{32,16},{48,32},{1,49},{17,1},{33,17},{49,33},{2,50}... | collective-permute-start | bytes 3440648 | tf_op jit(solution)/shard_map/ppermute | solution.py:607
  120.8 26.6 %collective-permute-start.7 = (f32[224,1280]{1,0:T(8,128)S(1)}, f32[224,1280]{1,0:T(8,128)S(1)}, u32[]{:S(2)}, u32[]{:S(2)}) collective-permute-start(f32[224,1280]{1,0:T(8,128)S(1)} %implicit.2.refs_4_), channel_id=1, source_target_pairs={{0,16},{16,32},{32,48},{48,0},{1,17},{17,33},{33,49},{49,1},{2,18}... | collective-permute-start | bytes 3440648 | tf_op jit(solution)/shard_map/ppermute | solution.py:606
  122.3 25.2 %collective-permute-start.15 = (f32[152,1280]{1,0:T(8,128)S(1)}, f32[152,1280]{1,0:T(8,128)S(1)}, u32[]{:S(2)}, u32[]{:S(2)}) collective-permute-start(f32[152,1280]{1,0:T(8,128)S(1)} %add_add_fusion.1.refs_7_), channel_id=1, source_target_pairs={{0,64},{64,0},{1,65},{65,1},{2,66},{66,2},{3,67},{67,3},{4,68},{68... | collective-permute-start | bytes 2334728 | tf_op jit(solution)/shard_map/ppermute | solution.py:578
  143.9 12.7 %collective-permute-start.10 = (f32[112,1280]{1,0:T(8,128)S(1)}, f32[112,1280]{1,0:T(8,128)S(1)}, u32[]{:S(2)}, u32[]{:S(2)}) collective-permute-start(f32[112,1280]{1,0:T(8,128)S(1)} %slice.107), channel_id=1, source_target_pairs={{0,48},{16,0},{32,16},{48,32},{1,49},{17,1},{33,17},{49,33},{2,50}... | collective-permute-start | bytes 1720328 | tf_op jit(solution)/shard_map/ppermute | solution.py:611
  147.4 12.5 %collective-permute-start.8 = (f32[112,1280]{1,0:T(8,128)S(1)}, f32[112,1280]{1,0:T(8,128)S(1)}, u32[]{:S(2)}, u32[]{:S(2)}) collective-permute-start(f32[112,1280]{1,0:T(8,128)S(1)} %slice.106), channel_id=1, source_target_pairs={{0,16},{16,32},{32,48},{48,0},{1,17},{17,33},{33,49},{49,1},{2,18}... | collective-permute-start | bytes 1720328 | tf_op jit(solution)/shard_map/ppermute | solution.py:610
  159.9 23.4 %collective-permute-start.18 = (f32[152,1280]{1,0:T(8,128)S(1)}, f32[152,1280]{1,0:T(8,128)S(1)}, u32[]{:S(2)}, u32[]{:S(2)}) collective-permute-start(f32[152,1280]{1,0:T(8,128)S(1)} %implicit.3.refs_4_), channel_id=1, source_target_pairs={{0,48},{16,0},{32,16},{48,32},{1,49},{17,1},{33,17},{49,33},{2,50}... | collective-permute-start | bytes 2334728 | tf_op jit(solution)/shard_map/ppermute | solution.py:607
  160.0 24.5 %collective-permute-start.16 = (f32[152,1280]{1,0:T(8,128)S(1)}, f32[152,1280]{1,0:T(8,128)S(1)}, u32[]{:S(2)}, u32[]{:S(2)}) collective-permute-start(f32[152,1280]{1,0:T(8,128)S(1)} %implicit.3.refs_4_), channel_id=1, source_target_pairs={{0,16},{16,32},{32,48},{48,0},{1,17},{17,33},{33,49},{49,1},{2,18}... | collective-permute-start | bytes 2334728 | tf_op jit(solution)/shard_map/ppermute | solution.py:606
  175.1 23.5 %all-to-all-start.2 = ((f32[16,3,24,128]{3,2,1,0:T(8,128)}), f32[16,3,24,128]{3,2,1,0:T(8,128)S(1)}, u32[]{:S(2)}, u32[]{:S(2)}) async-start(f32[16,3,24,128]{3,2,1,0:T(8,128)} %bitcast.8), calls=%async_computation.2 | async-start | bytes 1179648 | tf_op jit(solution)/shard_map/all_to_all | solution.py:569
  183.4 12.2 %collective-permute-start.19 = (f32[80,1280]{1,0:T(8,128)S(1)}, f32[80,1280]{1,0:T(8,128)S(1)}, u32[]{:S(2)}, u32[]{:S(2)}) collective-permute-start(f32[80,1280]{1,0:T(8,128)S(1)} %slice.109), channel_id=1, source_target_pairs={{0,48},{16,0},{32,16},{48,32},{1,49},{17,1},{33,17},{49,33},{2,50}... | collective-permute-start | bytes 1228808 | tf_op jit(solution)/shard_map/ppermute | solution.py:611
  184.6 11.0 %collective-permute-start.17 = (f32[72,1280]{1,0:T(8,128)S(1)}, f32[72,1280]{1,0:T(8,128)S(1)}, u32[]{:S(2)}, u32[]{:S(2)}) collective-permute-start(f32[72,1280]{1,0:T(8,128)S(1)} %slice.108), channel_id=1, source_target_pairs={{0,16},{16,32},{32,48},{48,0},{1,17},{17,33},{33,49},{49,1},{2,18}... | collective-permute-start | bytes 1105928 | tf_op jit(solution)/shard_map/ppermute | solution.py:610
  191.8 21.8 %copy-start.6 = (f32[2,20,128]{2,1,0:T(8,128)S(1)}, f32[2,20,128]{2,1,0:T(8,128)}, u32[]{:S(2)}) copy-start(f32[2,20,128]{2,1,0:T(8,128)} %constant.131.clone.refs_1_.twiddle_ref) | copy-start | bytes 61444
  191.8 21.8 %copy-start.8 = (f32[40]{0:T(128)S(1)}, f32[40]{0:T(128)}, u32[]{:S(2)}) copy-start(f32[40]{0:T(128)} %weight_ref.1) | copy-start | bytes 484
  191.9 21.8 %copy-start.9 = (bf16[256,512]{1,0:T(8,128)(2,1)S(1)}, bf16[256,512]{1,0:T(8,128)(2,1)}, u32[]{:S(2)}) copy-start(bf16[256,512]{1,0:T(8,128)(2,1)} %constant.135.clone.low_ref) | copy-start | bytes 786436
  191.9 21.8 %copy-start.10 = (bf16[256,512]{1,0:T(8,128)(2,1)S(1)}, bf16[256,512]{1,0:T(8,128)(2,1)}, u32[]{:S(2)}) copy-start(bf16[256,512]{1,0:T(8,128)(2,1)} %constant.134.clone.high_ref) | copy-start | bytes 786436

commit v4 on v3

--- a/solution.py
+++ b/solution.py
@@ -73,7 +73,7 @@
 
     def parts(table):
         high = table.astype(jnp.bfloat16)
-        return high, (table - high.astype(np.float32)).astype(jnp.bfloat16)
+        return np.concatenate([high, (table - high.astype(np.float32)).astype(jnp.bfloat16)])
 
     return twiddle, parts(forward), parts(backward)
 
@@ -83,8 +83,10 @@
     return 2 * (lane // N2) + (lane % N2) // 64 + N1 * (lane % 64)
 
 
-def one_hot(owner_ref, start, rows):
-    column = owner_ref[start : start + rows, 0:1]
+def one_hot(owner_ref, core, start, rows):
+    first = core * HALF + 4 * start
+    column = [owner_ref[w * 80 + first : w * 80 + first + rows, :] for w in range(8)]
+    column = jnp.concatenate(column, axis=0)[:, 0:1]
     waves = lane_waves()
     second = jnp.where(NM - 1 - column == waves, 1.0, 0.0).astype(BF)
     first = jnp.where(column == waves, 1.0, 0.0).astype(BF)
@@ -93,35 +95,23 @@
 
 def fourier_kernel(place_ref, owner_ref, *refs):
     parts = len(CHUNKS)
-    sources, table_ref, refs = refs[:4], refs[4], refs[5:]
+    sources, table_ref, refs = refs[:3], refs[3], refs[4:]
     send_refs, away_refs = refs[:parts], refs[parts : 2 * parts]
     stage_ref, wide_ref, half_ref, sem = refs[2 * parts : 2 * parts + 4]
     locals_ = refs[2 * parts + 4 :]
-    grid_ref, twiddle_ref, high_ref, low_ref = locals_
+    grid_ref, twiddle_ref, weight_ref = locals_
     loads = []
-    for k in range(4):
-        loads.append(pltpu.make_async_copy(sources[k], locals_[k], sem.at[8 * parts + k]))
+    for k in range(3):
+        loads.append(pltpu.make_async_copy(sources[k], locals_[k], sem.at[2 * parts + k]))
         loads[-1].start()
     source = (1 - place_ref[0]) * HALF
     fetches, copies = [], []
     for k, (start, count) in enumerate(CHUNKS):
-        for z in range(4):
-            rows = pl.ds(4 * start + z * count, count)
-            fetches.append(
-                pltpu.make_async_copy(
-                    table_ref.at[pl.ds(source + z * 10 + start, count)],
-                    half_ref.at[rows],
-                    sem.at[4 * k + z],
-                )
-            )
-            fetches[-1].start()
-            copies.append(
-                pltpu.make_async_copy(
-                    half_ref.at[rows],
-                    away_refs[k].at[pl.ds(z * count, count)],
-                    sem.at[4 * parts + 4 * k + z],
-                )
-            )
+        rows = pl.ds(4 * start, 4 * count)
+        here = table_ref.at[pl.ds(source + 4 * start, 4 * count)]
+        fetches.append(pltpu.make_async_copy(here, half_ref.at[rows], sem.at[k]))
+        fetches[-1].start()
+        copies.append(pltpu.make_async_copy(half_ref.at[rows], away_refs[k], sem.at[parts + k]))
     loads[0].wait()
     loads[1].wait()
     for r in range(ROWS):
@@ -152,13 +142,12 @@
                 stage_ref[wave // 2, rows, 0:6, base : base + N2] = rotated_real
                 stage_ref[wave // 2, rows, 0:6, base + N2 : base + 256] = rotated_imag
     loads[2].wait()
-    loads[3].wait()
     for fetch, copy in zip(fetches, copies):
         fetch.wait()
         copy.start()
     wide_ref[...] = jnp.zeros_like(wide_ref)
     for t in range(N1 // 2):
-        out = dot3(stage_ref[t].reshape(120, 512), high_ref[...], low_ref[...], NN)
+        out = dot3(stage_ref[t].reshape(120, 512), weight_ref[:512], weight_ref[512:], NN)
         for r in range(ROWS):
             rows = [out[r * 24 + f * 8 : r * 24 + f * 8 + 6] for f in range(3)]
             both = [row[:, :N2] for row in rows] + [row[:, N2:] for row in rows]
@@ -170,7 +159,7 @@
         group = 4 * count
         for c in range(2):
             half = 8 * group
-            picks = jnp.concatenate(one_hot(owner_ref, 64 * start + c * half, half), axis=0)
+            picks = jnp.concatenate(one_hot(owner_ref, c, start, group), axis=0)
             out = lax.dot_general(picks, high, NT, preferred_element_type=F32)
             out += lax.dot_general(picks, low, NT, preferred_element_type=F32)
             tile = [out[:half, :180], out[half:, :180], jnp.zeros((half, 24), F32)]
@@ -183,32 +172,33 @@
         copy.wait()
 
 
-def inverse_kernel(owner_ref, weight_ref, place_ref, twiddle_ref, high_ref, low_ref, *refs):
-    got_refs = refs[: len(CHUNKS)]
-    out_ref, stage_ref, wide_ref = refs[len(CHUNKS) :]
+def scatter(owner_ref, got_ref, start, count):
+    group = 4 * count
+    total = jnp.zeros((184, NM), F32)
+    for c in range(2):
+        second, first = one_hot(owner_ref, c, start, group)
+        tiles = [
+            jnp.concatenate([got_ref[c * 8 + w, t] for w in range(8)], axis=0) for t in range(3)
+        ]
+        flipped = jnp.concatenate(tiles, axis=1).T
+        for rows, picks in ((flipped[0:184], second), (flipped[180:364], first)):
+            high, low = split(rows)
+            total += lax.dot_general(high, picks, NN, preferred_element_type=F32)
+            total += lax.dot_general(low, picks, NN, preferred_element_type=F32)
+    return total
+
+
+def scatter_kernel(owner_ref, *refs):
+    total = jnp.zeros((184, NM), F32)
+    for k, (start, count) in enumerate(CHUNKS[:-1]):
+        total += scatter(owner_ref, refs[k], start, count)
+    refs[-1][...] = total
+
+
+def inverse_kernel(owner_ref, weight_ref, place_ref, twiddle_ref, table_ref, early_ref, got_ref, out_ref, stage_ref, wide_ref):
     wave = place_ref[1]
-
-    fresh = True
-    for k, (start, count) in enumerate(CHUNKS):
-        group = 4 * count
-        for c in range(2):
-            half = 8 * group
-            second, first = one_hot(owner_ref, 64 * start + c * half, half)
-            tiles = [
-                jnp.concatenate([got_refs[k][c * 8 + w, t] for w in range(8)], axis=0)
-                for t in range(3)
-            ]
-            flipped = jnp.concatenate(tiles, axis=1).T
-            out = jnp.zeros((184, NM), F32)
-            for rows, picks in ((flipped[0:184], second), (flipped[180:364], first)):
-                high, low = split(rows)
-                out += lax.dot_general(high, picks, NN, preferred_element_type=F32)
-                out += lax.dot_general(low, picks, NN, preferred_element_type=F32)
-            if fresh:
-                wide_ref[...] = out
-            else:
-                wide_ref[...] += out
-            fresh = False
+    start, count = CHUNKS[-1]
+    wide_ref[...] = early_ref[...] + scatter(owner_ref, got_ref, start, count)
     for t in range(N1 // 2):
         rows = []
         for r in range(ROWS):
@@ -221,7 +211,7 @@
                 imag += [block[FL + f * 6 : FL + f * 6 + 6], gap]
             both = [jnp.concatenate(real, axis=0), jnp.concatenate(imag, axis=0)]
             rows.append(jnp.concatenate(both, axis=1))
-        out = dot3(jnp.concatenate(rows, axis=0), high_ref[...], low_ref[...], NN)
+        out = dot3(jnp.concatenate(rows, axis=0), table_ref[:256], table_ref[256:], NN)
         for odd in range(2):
             m1 = 2 * t + odd
             real = out[:, odd * 256 : odd * 256 + N2]
@@ -276,7 +266,7 @@
     narrow = lax.broadcasted_iota(jnp.int32, (1, N2), 1)
     kept = []
     for i in range(2):
-        first_wave = owner_ref[wave * 80 + core * HALF + z * 10 + start + 2 * step + i]
+        first_wave = owner_ref[wave * 80 + core * HALF + 4 * start + z * count + 2 * step + i]
         pair = z * count + 2 * step + i
         for b, band in enumerate((core, 1 - core)):
             base = band * (24 * group) + pair
@@ -367,7 +357,7 @@
     row = lax.broadcasted_iota(jnp.int32, (count, 1), 0)
     first_wave = jnp.zeros((count, 1), jnp.int32)
     for i in range(count):
-        value = owner_ref[wave * 80 + core * HALF + z * 10 + start + i]
+        value = owner_ref[wave * 80 + core * HALF + 4 * start + z * count + i]
         first_wave = jnp.where(row == i, value, first_wave)
 
     tile = pl.program_id(0)
@@ -417,7 +407,7 @@
     block = work_ref[pl.ds(pl.multiple_of(step * 72, 8), 72), :]
     pad = jnp.zeros((4, NM), F32)
     for i in range(2):
-        first_wave = owner_ref[wave * 80 + core * HALF + z * 10 + start + 2 * step + i]
+        first_wave = owner_ref[wave * 80 + core * HALF + 4 * start + z * count + 2 * step + i]
         pair = z * count + 2 * step + i
         values = jnp.concatenate([block[i * 36 : i * 36 + 36], pad], axis=0)
         is_first = lane < NM - first_wave
@@ -444,6 +434,18 @@
                 out_ref[spot, :] = line[:, t * N2 : (t + 1) * N2]
 
 
+def fold_kernel(right_ref, top_ref, left_ref, bottom_ref, right_out, left_out):
+    cut = top_ref.shape[0]
+    right_out[:cut] = right_ref[:cut] + top_ref[...]
+    right_out[cut:] = right_ref[cut:]
+    left_out[:cut] = left_ref[:cut]
+    left_out[cut:] = left_ref[cut:] + bottom_ref[...]
+
+
+def sum_kernel(x_ref, y_ref, z_ref, out_ref):
+    out_ref[...] = x_ref[...] + y_ref[...] + z_ref[...]
+
+
 def parameters():
     return pltpu.CompilerParams(vmem_limit_bytes=VMEM_BYTES)
 
@@ -463,9 +465,7 @@
     twiddle, forward, backward = constant_tables()
     smem = whole(pltpu.SMEM)
     place = jnp.stack([core, wave, z]).astype(jnp.int32)
-    by_group = owner.reshape(8, 2, 4, 10)
-    order = [by_group[..., a : a + n].transpose(1, 0, 2, 3).reshape(-1) for a, n in CHUNKS]
-    owner_column = jnp.broadcast_to(jnp.concatenate(order)[:, None], (PAIRS, N2))
+    owner_column = jnp.broadcast_to(owner[:, None], (PAIRS, N2))
     matrices = [m.reshape(36) for m in (modes_e, modes_f)] + [rates]
     matrices += [m.reshape(36) for m in (height_matrix, heating_matrix)]
 
@@ -473,22 +473,21 @@
         fourier_kernel,
         out_shape=[jax.ShapeDtypeStruct((16, 3, 4 * n, N2), F32) for _, n in CHUNKS]
         + [jax.ShapeDtypeStruct((4 * n, HALF, PACK), F32) for _, n in CHUNKS],
-        in_specs=[smem, whole()] + [whole(pltpu.HBM)] * 5,
+        in_specs=[smem, whole()] + [whole(pltpu.HBM)] * 4,
         out_specs=[whole()] * len(CHUNKS) + [whole(pltpu.HBM)] * len(CHUNKS),
         scratch_shapes=[
             pltpu.VMEM((10, 15, 8, 512), F32),
             pltpu.VMEM((184, NM), F32),
             pltpu.VMEM((HALF, HALF, PACK), F32),
-            pltpu.SemaphoreType.DMA((8 * len(CHUNKS) + 4,)),
+            pltpu.SemaphoreType.DMA((2 * len(CHUNKS) + 3,)),
             pltpu.VMEM((3, ROWS, 6, NLON), F32),
             pltpu.VMEM((2, N1, N2), F32),
-            pltpu.VMEM((512, 256), BF),
-            pltpu.VMEM((512, 256), BF),
+            pltpu.VMEM((1024, 256), BF),
         ],
         compiler_params=parameters(),
         cost_estimate=cost(4e9, 2.6e7),
         name="fourier",
-    )(place, owner_column, grad_grid.transpose(0, 2, 1, 3), twiddle, *forward, legendre)
+    )(place, owner_column, grad_grid.transpose(0, 2, 1, 3), twiddle, forward, legendre)
     fours, aways = made[: len(CHUNKS)], made[len(CHUNKS) :]
 
     def zone(rels, t, place):
@@ -499,7 +498,7 @@
             pl.BlockSpec(
                 (2, HALF, PACK),
                 lambda t, s, place, owner: (
-                    place[0] * 20 + zone(rels, t, place) * 5 + start // 2 + s,
+                    place[0] * 20 + 2 * start + zone(rels, t, place) * (count // 2) + s,
                     0,
                     0,
                 ),
@@ -593,8 +592,19 @@
             top, bottom, _ = lax.optimization_barrier((top, bottom, before["sum"]))
         top = lax.ppermute(top, "z", UP)
         bottom = lax.ppermute(bottom, "z", DOWN)
-        now["right"] = right = right.at[:cut].add(top)
-        now["left"] = left = left.at[cut:].add(bottom)
+        if k:
+            right, left = right.at[:cut].add(top), left.at[cut:].add(bottom)
+        else:
+            right, left = pl.pallas_call(
+                fold_kernel,
+                out_shape=[jax.ShapeDtypeStruct(right.shape, F32)] * 2,
+                in_specs=[whole()] * 4,
+                out_specs=[whole()] * 2,
+                compiler_params=parameters(),
+                cost_estimate=cost(1e5, 1e6),
+                name="fold",
+            )(right, top, left, bottom)
+        now["right"], now["left"] = right, left
         now["moving"] = lax.ppermute(right, "z", UP), lax.ppermute(left, "z", DOWN)
     finish(steps[-1])
     for k, (start, count) in enumerate(CHUNKS):
@@ -619,16 +629,25 @@
         rows = grid_rows(start, count, (0, 1, 3), now["other"], (now["new"], right, now["left"]))
         rows = grid_rows(start, count, (2,), now["other"], (top, now["bottom"], rows))
         results.append(exchange(rows.reshape(16, 3, 4 * count, N2)))
+    early = pl.pallas_call(
+        scatter_kernel,
+        out_shape=jax.ShapeDtypeStruct((184, NM), F32),
+        in_specs=[whole()] * len(CHUNKS),
+        out_specs=whole(),
+        compiler_params=parameters(),
+        cost_estimate=cost(1e9, 2e6),
+        name="scatter",
+    )(owner_column, *results[:-1])
     out = pl.pallas_call(
         inverse_kernel,
         out_shape=jax.ShapeDtypeStruct((3, ROWS, 6, NLON), F32),
-        in_specs=[whole()] + [smem] * 2 + [whole()] * (3 + len(CHUNKS)),
+        in_specs=[whole()] + [smem] * 2 + [whole()] * 4,
         out_specs=whole(),
         scratch_shapes=[pltpu.VMEM((N1, 120, 256), F32), pltpu.VMEM((184, NM), F32)],
         compiler_params=parameters(),
         cost_estimate=cost(4e9, 8e6),
         name="inverse",
-    )(owner_column, lat_weights, place, twiddle, *backward, *results)
+    )(owner_column, lat_weights, place, twiddle, backward, early, results[-1])
     return out.transpose(0, 2, 1, 3)
 
 

time: 221 us -> 217 us (0.982)
  blocking collectives: 31.4 us -> 16.4 us
  waiting for transfers between devices: 55 us -> 64.8 us
  starting transfers between devices: 44.6 us -> 50.1 us
  other arithmetic: 10.9 us -> 7.05 us
    all_to_all x2 -> x1, blocking collectives: 31.4 us -> 16.4 us  [exchange(): return lax.all_to_all(value, ('core', 'wave'), 0, 0, tiled=True)]
    all_to_all x2 -> x3, waiting for transfers between devices: 8.54 us -> 15.7 us  [exchange(): return lax.all_to_all(value, ('core', 'wave'), 0, 0, tiled=True)]
    all_to_all x2 -> x3, starting transfers between devices: 12.7 us -> 19.5 us  [exchange(): return lax.all_to_all(value, ('core', 'wave'), 0, 0, tiled=True)]
    scatter-add x4 -> x2, other arithmetic: 7.51 us -> 3.63 us  [per_device(): right, left = (right.at[:cut].add(top), left.at[cut:].add(bottom))]
    pallas_call x0 -> x2, Pallas kernels: none -> 2.91 us  [the longest x1 1.59 us: per_device(): pl.pallas_call(fold_kernel, out_shape=[jax.ShapeDtypeStruct(right.shape,...]
  transfers between devices with their start and end apart: 22 -> 23, of which waited for: 10 -> 11; matrix products, arithmetic and copies ran while one was open for 4% -> 3% of each run, Pallas kernels for 26% -> 28%
where the time goes in v4:
time: 217 us; the launch traced here: 216 us
  Pallas kernels  72.6 us (33%)
  waiting for transfers between devices  64.8 us (30%)
  starting transfers between devices  50.1 us (23%)
  blocking collectives  16.4 us (8%)
  other arithmetic  7.05 us (3%)
  local copies, waits for them, and re-layouts  4.38 us (2%)
    pallas_call x4, Pallas kernels, grid_rows(): pl.pallas_call(lambda *refs: grid_rows_kernel(start, count, rels, *refs),...  24.4 us
    pallas_call x4, Pallas kernels, spectra(): pl.pallas_call(lambda *refs: spectra_kernel(start, count, rels, *refs), o...  23.7 us
    all_to_all x3, starting transfers between devices, exchange(): return lax.all_to_all(value, ('core', 'wave'), 0, 0, tiled=True)  19.5 us
    ppermute x2, waiting for transfers between devices, per_device(): right = lax.ppermute(new, 'z', DOWN)  18.4 us
    all_to_all x1, blocking collectives, exchange(): return lax.all_to_all(value, ('core', 'wave'), 0, 0, tiled=True)  16.4 us
    all_to_all x3, waiting for transfers between devices, exchange(): return lax.all_to_all(value, ('core', 'wave'), 0, 0, tiled=True)  15.7 us
    ppermute x2, waiting for transfers between devices, per_device(): top = lax.ppermute(top, 'z', UP)  9.08 us
    pallas_call x2, Pallas kernels, implicit(): pl.pallas_call(lambda *refs: implicit_kernel(start, count, *refs), out_sh...  8.48 us
  transfers between devices with their start and end apart: 23, of which 11 were waited for; matrix products, arithmetic and copies ran while one was open for 3% of the time, Pallas kernels for 28%

profile of v4, /device:TPU:1, one launch (start us, length us, event | category | flops | bytes accessed | tf_op | source)
XLA Modules:
  0.0 215.6 jit_solution(18077149029845416346)
XLA Ops:
  0.1 0.8 broadcast_in_dim.2.owner_ref
  0.9 1.3 copy-done.1
  2.2 1.0 copy-done.2
  4.0 8.4 %fourier.1 = (f32[16,3,24,128]{3,2,1,0:T(8,128)S(1)}, f32[16,3,16,128]{3,2,1,0:T(8,128)}, f32[24,40,1408]{2,1,0:T(8,128)S(1)}, f32[16,40,1408]{2,1,0:T(8,128)}) custom-call(s32[3]{0:T(128)S(1)} %pad_add_fusion.place_ref.refs_0_, s32[640,128]{1,0:T(8,128)S(1)} %broadcast_in_dim.2.owner_ref, f32[3,5,6,2560]{3,2,1,0:T(8,128)S(1)} %bitcast.15, ...), custom_call_target="tpu_custom_call" | custom-call | flops 4000000000 | bytes 26000000 | tf_op jit(solution)/shard_map/fourier/pallas_call | solution.py:472
  12.4 1.5 collective-permute-start
  13.9 16.4 %all_to_all.20 = f32[16,3,24,128]{3,2,1,0:T(8,128)S(1)} all-to-all(f32[16,3,24,128]{3,2,1,0:T(8,128)S(1)} %get-tuple-element.54), channel_id=1, replica_groups=mesh['yh'=2,'z'=4,'core'=2,'wave'=8] {'core','wave'}, dimensions={0} | all-to-all | bytes 1179648 | tf_op jit(solution)/shard_map/all_to_all | solution.py:568
  30.3 0.8 collective-permute-start.4
  31.1 4.2 %spectra.5 = (f32[112,1280]{1,0:T(8,128)S(1)}, f32[112,1280]{1,0:T(8,128)S(1)}) custom-call(s32[3]{0:T(128)S(1)} %pad_add_fusion.place_ref.refs_0_, s32[640]{0:T(1024)S(1)} %copy-done.3, f32[80,40,1408]{2,1,0:T(8,128)} %refs_2_.16, f32[24,40,1408]{2,1,0:T(8,128)S(1)} %collective-permute-done.refs_3_, f32[1152,128]{1,0:T(8,128)S(1)} %bitcast.11), custom_call_target="tpu_custom_call" | custom-call | flops 300000000 | bytes 3000000 | tf_op jit(solution)/shard_map/spectra/pallas_call | solution.py:519
  35.3 1.7 collective-permute-start.1
  37.0 2.2 %collective-permute-start.2 = (f32[112,1280]{1,0:T(8,128)S(1)}, f32[112,1280]{1,0:T(8,128)S(1)}, u32[]{:S(2)}, u32[]{:S(2)}) collective-permute-start(f32[112,1280]{1,0:T(8,128)S(1)} %get-tuple-element.59), channel_id=1, source_target_pairs={{0,48},{16,0},{32,16},{48,32},{1,49},{17,1},{33,17},{49,33},{2,50}... | collective-permute-start | bytes 1720328 | tf_op jit(solution)/shard_map/ppermute | solution.py:594
  39.2 8.7 %spectra.4 = (f32[224,1280]{1,0:T(8,128)S(1)}, f32[224,1280]{1,0:T(8,128)S(1)}, f32[224,1280]{1,0:T(8,128)S(1)}) custom-call(s32[3]{0:T(128)S(1)} %pad_add_fusion.place_ref.refs_0_, s32[640]{0:T(1024)S(1)} %copy-done.3, f32[80,40,1408]{2,1,0:T(8,128)} %refs_2_.16, f32[24,40,1408]{2,1,0:T(8,128)S(1)} %collective-permute-done.refs_3_, f32[1152,128]{1,0:T(8,128)S(1)} %bitcast.12), custom_call_target="tpu_custom_call" | custom-call | flops 900000000 | bytes 9000000 | tf_op jit(solution)/shard_map/spectra/pallas_call | solution.py:519
  47.9 4.5 %collective-permute-done.1.top_ref = f32[112,1280]{1,0:T(8,128)S(1)} collective-permute-done((f32[112,1280]{1,0:T(8,128)S(1)}, f32[112,1280]{1,0:T(8,128)S(1)}, u32[]{:S(2)}, u32[]{:S(2)}) %collective-permute-start.1) | collective-permute-done | bytes 573472 | tf_op jit(solution)/shard_map/ppermute | solution.py:593
  52.5 1.6 fold.1
  54.5 2.2 %collective-permute-start.5 = (f32[224,1280]{1,0:T(8,128)}, f32[224,1280]{1,0:T(8,128)}, u32[]{:S(2)}, u32[]{:S(2)}) collective-permute-start(f32[224,1280]{1,0:T(8,128)} %get-tuple-element.64), channel_id=1, source_target_pairs={{0,48},{16,0},{32,16},{48,32},{1,49},{17,1},{33,17},{49,33},{2,50}... | collective-permute-start | bytes 3440648 | tf_op jit(solution)/shard_map/ppermute | solution.py:608
  56.8 4.5 %all-to-all-start.1 = ((f32[16,3,16,128]{3,2,1,0:T(8,128)}), f32[16,3,16,128]{3,2,1,0:T(8,128)S(1)}, u32[]{:S(2)}, u32[]{:S(2)}) async-start(f32[16,3,16,128]{3,2,1,0:T(8,128)} %get-tuple-element.65), calls=%async_computation.1 | async-start | bytes 786432 | tf_op jit(solution)/shard_map/all_to_all | solution.py:568
  61.3 8.5 %all-to-all-done.1 = f32[16,3,16,128]{3,2,1,0:T(8,128)S(1)} async-done(((f32[16,3,16,128]{3,2,1,0:T(8,128)}), f32[16,3,16,128]{3,2,1,0:T(8,128)S(1)}, u32[]{:S(2)}, u32[]{:S(2)}) %all-to-all-start.1) | async-done | bytes 393248 | tf_op jit(solution)/shard_map/all_to_all | solution.py:568
  69.8 3.0 %spectra.7 = (f32[72,1280]{1,0:T(8,128)S(1)}, f32[80,1280]{1,0:T(8,128)S(1)}) custom-call(s32[3]{0:T(128)S(1)} %pad_add_fusion.place_ref.refs_0_, s32[640]{0:T(1024)S(1)} %copy-done.3, f32[80,40,1408]{2,1,0:T(8,128)} %refs_2_.16, f32[16,40,1408]{2,1,0:T(8,128)} %collective-permute-done.4.refs_3_, f32[768,128]{1,0:T(8,128)S(1)} %bitcast.13), custom_call_target="tpu_custom_call" | custom-call | flops 200000000 | bytes 2000000 | tf_op jit(solution)/shard_map/spectra/pallas_call | solution.py:519
  72.8 7.8 %spectra.6 = (f32[152,1280]{1,0:T(8,128)}, f32[152,1280]{1,0:T(8,128)}, f32[152,1280]{1,0:T(8,128)S(1)}) custom-call(s32[3]{0:T(128)S(1)} %pad_add_fusion.place_ref.refs_0_, s32[640]{0:T(1024)S(1)} %copy-done.3, f32[80,40,1408]{2,1,0:T(8,128)} %refs_2_.16, f32[16,40,1408]{2,1,0:T(8,128)} %collective-permute-done.4.refs_3_, f32[768,128]{1,0:T(8,128)S(1)} %bitcast.14), custom_call_target="tpu_custom_call" | custom-call | flops 600000000 | bytes 6000000 | tf_op jit(solution)/shard_map/spectra/pallas_call | solution.py:519
  80.6 1.2 collective-permute-done.3
  81.8 1.8 add_add_fusion.refs_7_
  83.7 2.7 %collective-permute-start.6 = (f32[224,1280]{1,0:T(8,128)S(1)}, f32[224,1280]{1,0:T(8,128)S(1)}, u32[]{:S(2)}, u32[]{:S(2)}) collective-permute-start(f32[224,1280]{1,0:T(8,128)S(1)} %add_add_fusion.refs_7_), channel_id=1, source_target_pairs={{0,64},{64,0},{1,65},{65,1},{2,66},{66,2},{3,67},{67,3},{4,68},{68... | collective-permute-start | bytes 3440648 | tf_op jit(solution)/shard_map/ppermute | solution.py:577
  86.4 2.6 %collective-permute-start.13 = (f32[80,1280]{1,0:T(8,128)S(1)}, f32[80,1280]{1,0:T(8,128)S(1)}, u32[]{:S(2)}, u32[]{:S(2)}) collective-permute-start(f32[80,1280]{1,0:T(8,128)S(1)} %get-tuple-element.73), channel_id=1, source_target_pairs={{0,48},{16,0},{32,16},{48,32},{1,49},{17,1},{33,17},{49,33},{2,50}... | collective-permute-start | bytes 1228808 | tf_op jit(solution)/shard_map/ppermute | solution.py:594
  89.0 4.5 %collective-permute-done.11 = f32[72,1280]{1,0:T(8,128)S(1)} collective-permute-done((f32[72,1280]{1,0:T(8,128)S(1)}, f32[72,1280]{1,0:T(8,128)S(1)}, u32[]{:S(2)}, u32[]{:S(2)}) %collective-permute-start.11) | collective-permute-done | bytes 368672 | tf_op jit(solution)/shard_map/ppermute | solution.py:593
  93.6 1.8 add_dynamic-update-slice_fusion.1
  95.8 1.8 add_dynamic-update-slice_fusion
  97.6 3.4 %collective-permute-start.14 = (f32[152,1280]{1,0:T(8,128)}, f32[152,1280]{1,0:T(8,128)}, u32[]{:S(2)}, u32[]{:S(2)}) collective-permute-start(f32[152,1280]{1,0:T(8,128)} %add_dynamic-update-slice_fusion), channel_id=1, source_target_pairs={{0,48},{16,0},{32,16},{48,32},{1,49},{17,1},{33,17},{49,33},{2,50}... | collective-permute-start | bytes 2334728 | tf_op jit(solution)/shard_map/ppermute | solution.py:608
  101.3 8.4 %collective-permute-done.6.refs_8_ = f32[224,1280]{1,0:T(8,128)S(1)} collective-permute-done((f32[224,1280]{1,0:T(8,128)S(1)}, f32[224,1280]{1,0:T(8,128)S(1)}, u32[]{:S(2)}, u32[]{:S(2)}) %collective-permute-start.6) | collective-permute-done | bytes 1146912 | tf_op jit(solution)/shard_map/ppermute | solution.py:577
  109.7 4.2 %implicit.2.refs_4_ = f32[224,1280]{1,0:T(8,128)S(1)} custom-call(s32[3]{0:T(128)S(1)} %pad_add_fusion.place_ref.refs_0_, s32[640]{0:T(1024)S(1)} %copy-done.3, f32[36]{0:T(128)S(1)} %reshape.74.refs_2_, f32[36]{0:T(128)S(1)} %reshape.75.refs_3_, f32[6]{0:T(128)S(1)} %copy-done.6, f32[36]{0:T(128)S(1)} %reshape.76.refs_5_, f32[36]{0:T(128)S(1)} %reshape.77.refs_6_, ...), custom_call_target="tpu_custom_call" | custom-call | flops 60000000 | bytes 3600000 | tf_op jit(solution)/shard_map/implicit/pallas_call | solution.py:536
  114.0 3.5 %collective-permute-start.9 = (f32[224,1280]{1,0:T(8,128)S(1)}, f32[224,1280]{1,0:T(8,128)S(1)}, u32[]{:S(2)}, u32[]{:S(2)}) collective-permute-start(f32[224,1280]{1,0:T(8,128)S(1)} %implicit.2.refs_4_), channel_id=1, source_target_pairs={{0,48},{16,0},{32,16},{48,32},{1,49},{17,1},{33,17},{49,33},{2,50}... | collective-permute-start | bytes 3440648 | tf_op jit(solution)/shard_map/ppermute | solution.py:617
  117.4 1.5 add_add_fusion.1.refs_7_
  119.0 2.8 %collective-permute-start.15 = (f32[152,1280]{1,0:T(8,128)S(1)}, f32[152,1280]{1,0:T(8,128)S(1)}, u32[]{:S(2)}, u32[]{:S(2)}) collective-permute-start(f32[152,1280]{1,0:T(8,128)S(1)} %add_add_fusion.1.refs_7_), channel_id=1, source_target_pairs={{0,64},{64,0},{1,65},{65,1},{2,66},{66,2},{3,67},{67,3},{4,68},{68... | collective-permute-start | bytes 2334728 | tf_op jit(solution)/shard_map/ppermute | solution.py:577
  121.8 18.4 %collective-permute-done.9.refs_5_ = f32[224,1280]{1,0:T(8,128)S(1)} collective-permute-done((f32[224,1280]{1,0:T(8,128)S(1)}, f32[224,1280]{1,0:T(8,128)S(1)}, u32[]{:S(2)}, u32[]{:S(2)}) %collective-permute-start.9) | collective-permute-done | bytes 1146912 | tf_op jit(solution)/shard_map/ppermute | solution.py:617
  140.2 3.5 %collective-permute-start.10 = (f32[112,1280]{1,0:T(8,128)S(1)}, f32[112,1280]{1,0:T(8,128)S(1)}, u32[]{:S(2)}, u32[]{:S(2)}) collective-permute-start(f32[112,1280]{1,0:T(8,128)S(1)} %slice.57), channel_id=1, source_target_pairs={{0,48},{16,0},{32,16},{48,32},{1,49},{17,1},{33,17},{49,33},{2,50}... | collective-permute-start | bytes 1720328 | tf_op jit(solution)/shard_map/ppermute | solution.py:621
  143.9 4.2 %implicit.3.refs_4_ = f32[152,1280]{1,0:T(8,128)S(1)} custom-call(s32[3]{0:T(128)S(1)} %pad_add_fusion.place_ref.refs_0_, s32[640]{0:T(1024)S(1)} %copy-done.3, f32[36]{0:T(128)S(1)} %reshape.74.refs_2_, f32[36]{0:T(128)S(1)} %reshape.75.refs_3_, f32[6]{0:T(128)S(1)} %copy-done.6, f32[36]{0:T(128)S(1)} %reshape.76.refs_5_, f32[36]{0:T(128)S(1)} %reshape.77.refs_6_, ...), custom_call_target="tpu_custom_call" | custom-call | flops 40000000 | bytes 2400000 | tf_op jit(solution)/shard_map/implicit/pallas_call | solution.py:536
  148.1 4.7 %collective-permute-done.10.refs_5_ = f32[112,1280]{1,0:T(8,128)S(1)} collective-permute-done((f32[112,1280]{1,0:T(8,128)S(1)}, f32[112,1280]{1,0:T(8,128)S(1)}, u32[]{:S(2)}, u32[]{:S(2)}) %collective-permute-start.10) | collective-permute-done | bytes 573472 | tf_op jit(solution)/shard_map/ppermute | solution.py:621
  152.8 3.2 %collective-permute-done.8.refs_4_ = f32[112,1280]{1,0:T(8,128)S(1)} collective-permute-done((f32[112,1280]{1,0:T(8,128)S(1)}, f32[112,1280]{1,0:T(8,128)S(1)}, u32[]{:S(2)}, u32[]{:S(2)}) %collective-permute-start.8) | collective-permute-done | bytes 573472 | tf_op jit(solution)/shard_map/ppermute | solution.py:620
  156.3 1.3 collective-permute-start.16
  157.6 9.0 %grid_rows.4.refs_6_ = f32[1152,128]{1,0:T(8,128)S(1)} custom-call(s32[3]{0:T(128)S(1)} %pad_add_fusion.place_ref.refs_0_, s32[640]{0:T(1024)S(1)} %copy-done.3, f32[80,40,1408]{2,1,0:T(8,128)} %refs_2_.16, f32[24,40,1408]{2,1,0:T(8,128)S(1)} %bitcast.10, f32[224,1280]{1,0:T(8,128)S(1)} %implicit.2.refs_4_, f32[224,1280]{1,0:T(8,128)S(1)} %collective-permute-done.9.refs_5_, ...), custom_call_target="tpu_custom_call" | custom-call | flops 1260000000 | bytes 9000000 | tf_op jit(solution)/shard_map/grid_rows/pallas_call | solution.py:549
  166.6 4.8 %grid_rows.5 = f32[1152,128]{1,0:T(8,128)} custom-call(s32[3]{0:T(128)S(1)} %pad_add_fusion.place_ref.refs_0_, s32[640]{0:T(1024)S(1)} %copy-done.3, f32[80,40,1408]{2,1,0:T(8,128)} %refs_2_.16, f32[24,40,1408]{2,1,0:T(8,128)S(1)} %bitcast.10, f32[112,1280]{1,0:T(8,128)S(1)} %collective-permute-done.8.refs_4_, ...), custom_call_target="tpu_custom_call" | custom-call | flops 420000000 | bytes 3000000 | tf_op jit(solution)/shard_map/grid_rows/pallas_call | solution.py:549
  171.3 8.3 %all-to-all-start.2 = ((f32[16,3,24,128]{3,2,1,0:T(8,128)}), f32[16,3,24,128]{3,2,1,0:T(8,128)S(1)}, u32[]{:S(2)}, u32[]{:S(2)}) async-start(f32[16,3,24,128]{3,2,1,0:T(8,128)} %bitcast.6), calls=%async_computation.2 | async-start | bytes 1179648 | tf_op jit(solution)/shard_map/all_to_all | solution.py:568
  179.7 1.2 collective-permute-start.19
  181.4 6.8 %grid_rows.6.refs_6_ = f32[768,128]{1,0:T(8,128)S(1)} custom-call(s32[3]{0:T(128)S(1)} %pad_add_fusion.place_ref.refs_0_, s32[640]{0:T(1024)S(1)} %copy-done.3, f32[80,40,1408]{2,1,0:T(8,128)} %refs_2_.16, f32[16,40,1408]{2,1,0:T(8,128)} %collective-permute-done.4.refs_3_, f32[152,1280]{1,0:T(8,128)S(1)} %implicit.3.refs_4_, ...), custom_call_target="tpu_custom_call" | custom-call | flops 840000000 | bytes 6000000 | tf_op jit(solution)/shard_map/grid_rows/pallas_call | solution.py:549
  188.2 3.7 %collective-permute-done.17.refs_4_ = f32[72,1280]{1,0:T(8,128)S(1)} collective-permute-done((f32[72,1280]{1,0:T(8,128)S(1)}, f32[72,1280]{1,0:T(8,128)S(1)}, u32[]{:S(2)}, u32[]{:S(2)}) %collective-permute-start.17) | collective-permute-done | bytes 368672 | tf_op jit(solution)/shard_map/ppermute | solution.py:620
  191.9 3.8 %grid_rows.7 = f32[768,128]{1,0:T(8,128)} custom-call(s32[3]{0:T(128)S(1)} %pad_add_fusion.place_ref.refs_0_, s32[640]{0:T(1024)S(1)} %copy-done.3, f32[80,40,1408]{2,1,0:T(8,128)} %refs_2_.16, f32[16,40,1408]{2,1,0:T(8,128)} %collective-permute-done.4.refs_3_, f32[72,1280]{1,0:T(8,128)S(1)} %collective-permute-done.17.refs_4_, ...), custom_call_target="tpu_custom_call" | custom-call | flops 280000000 | bytes 2000000 | tf_op jit(solution)/shard_map/grid_rows/pallas_call | solution.py:549
  195.7 6.7 %all-to-all-start.3 = ((f32[16,3,16,128]{3,2,1,0:T(8,128)}), f32[16,3,16,128]{3,2,1,0:T(8,128)S(1)}, u32[]{:S(2)}, u32[]{:S(2)}) async-start(f32[16,3,16,128]{3,2,1,0:T(8,128)} %bitcast.7), calls=%async_computation.3 | async-start | bytes 786432 | tf_op jit(solution)/shard_map/all_to_all | solution.py:568
  202.4 1.3 scatter.1.early_ref
  203.7 7.1 %all-to-all-done.3.got_ref = f32[16,3,16,128]{3,2,1,0:T(8,128)S(1)} async-done(((f32[16,3,16,128]{3,2,1,0:T(8,128)}), f32[16,3,16,128]{3,2,1,0:T(8,128)S(1)}, u32[]{:S(2)}, u32[]{:S(2)}) %all-to-all-start.3) | async-done | bytes 393248 | tf_op jit(solution)/shard_map/all_to_all | solution.py:568
  210.9 4.7 %inverse.1 = f32[3,5,6,2560]{3,2,1,0:T(8,128)} custom-call(s32[640,128]{1,0:T(8,128)S(1)} %broadcast_in_dim.2.owner_ref, f32[40]{0:T(128)S(1)} %copy-done.7, s32[3]{0:T(128)S(1)} %pad_add_fusion.place_ref.refs_0_, f32[2,20,128]{2,1,0:T(8,128)S(1)} %copy-done.5, bf16[512,512]{1,0:T(8,128)(2,1)S(1)} %copy-done.8, f32[184,1280]{1,0:T(8,128)S(1)} %scatter.1.early_ref, ...), custom_call_target="tpu_custom_call" | custom-call | flops 4000000000 | bytes 8000000 | tf_op jit(solution)/shard_map/inverse/pallas_call | solution.py:641
  (58 shorter events, 2.9 us)
Async XLA Ops:
  0.9 1.3 copy-start.1
  2.2 1.0 copy-start.2
  3.2 0.7 copy-start.4
  12.4 18.7 %copy-start.3 = (s32[640]{0:T(1024)S(1)}, s32[640]{0:T(1024)}, u32[]{:S(2)}) copy-start(s32[640]{0:T(1024)} %refs_1_.20) | copy-start | bytes 7684
  12.4 18.7 %collective-permute-start = (f32[24,40,1408]{2,1,0:T(8,128)S(1)}, f32[24,40,1408]{2,1,0:T(8,128)S(1)}, u32[]{:S(2)}, u32[]{:S(2)}) collective-permute-start(f32[24,40,1408]{2,1,0:T(8,128)S(1)} %get-tuple-element.53), channel_id=1, source_target_pairs={{0,8},{8,0},{1,9},{9,1},{2,10},{10,2},{3,11},{11,3},{4,12},{12,4},... | collective-permute-start | bytes 16220168 | tf_op jit(solution)/shard_map/ppermute | solution.py:586
  30.3 30.9 %collective-permute-start.4 = (f32[16,40,1408]{2,1,0:T(8,128)}, f32[16,40,1408]{2,1,0:T(8,128)}, u32[]{:S(2)}, u32[]{:S(2)}) collective-permute-start(f32[16,40,1408]{2,1,0:T(8,128)} %get-tuple-element.62), channel_id=1, source_target_pairs={{0,8},{8,0},{1,9},{9,1},{2,10},{10,2},{3,11},{11,3},{4,12},{12,4},... | collective-permute-start | bytes 10813448 | tf_op jit(solution)/shard_map/ppermute | solution.py:586
  31.1 8.1 %copy-start = (f32[24,40,1408]{2,1,0:T(8,128)}, f32[24,40,1408]{2,1,0:T(8,128)S(1)}, u32[]{:S(2)}) copy-start(f32[24,40,1408]{2,1,0:T(8,128)S(1)} %collective-permute-done.refs_3_) | copy-start | bytes 16220164
  35.3 17.2 %collective-permute-start.1 = (f32[112,1280]{1,0:T(8,128)S(1)}, f32[112,1280]{1,0:T(8,128)S(1)}, u32[]{:S(2)}, u32[]{:S(2)}) collective-permute-start(f32[112,1280]{1,0:T(8,128)S(1)} %get-tuple-element.57), channel_id=1, source_target_pairs={{0,16},{16,32},{32,48},{48,0},{1,17},{17,33},{33,49},{49,1},{2,18}... | collective-permute-start | bytes 1720328 | tf_op jit(solution)/shard_map/ppermute | solution.py:593
  37.0 15.5 %collective-permute-start.2 = (f32[112,1280]{1,0:T(8,128)S(1)}, f32[112,1280]{1,0:T(8,128)S(1)}, u32[]{:S(2)}, u32[]{:S(2)}) collective-permute-start(f32[112,1280]{1,0:T(8,128)S(1)} %get-tuple-element.59), channel_id=1, source_target_pairs={{0,48},{16,0},{32,16},{48,32},{1,49},{17,1},{33,17},{49,33},{2,50}... | collective-permute-start | bytes 1720328 | tf_op jit(solution)/shard_map/ppermute | solution.py:594
  54.1 27.8 %collective-permute-start.3 = (f32[224,1280]{1,0:T(8,128)}, f32[224,1280]{1,0:T(8,128)}, u32[]{:S(2)}, u32[]{:S(2)}) collective-permute-start(f32[224,1280]{1,0:T(8,128)} %get-tuple-element.60), channel_id=1, source_target_pairs={{0,16},{16,32},{32,48},{48,0},{1,17},{17,33},{33,49},{49,1},{2,18}... | collective-permute-start | bytes 3440648 | tf_op jit(solution)/shard_map/ppermute | solution.py:608
  54.5 27.3 %collective-permute-start.5 = (f32[224,1280]{1,0:T(8,128)}, f32[224,1280]{1,0:T(8,128)}, u32[]{:S(2)}, u32[]{:S(2)}) collective-permute-start(f32[224,1280]{1,0:T(8,128)} %get-tuple-element.64), channel_id=1, source_target_pairs={{0,48},{16,0},{32,16},{48,32},{1,49},{17,1},{33,17},{49,33},{2,50}... | collective-permute-start | bytes 3440648 | tf_op jit(solution)/shard_map/ppermute | solution.py:608
  56.8 13.1 %all-to-all-start.1 = ((f32[16,3,16,128]{3,2,1,0:T(8,128)}), f32[16,3,16,128]{3,2,1,0:T(8,128)S(1)}, u32[]{:S(2)}, u32[]{:S(2)}) async-start(f32[16,3,16,128]{3,2,1,0:T(8,128)} %get-tuple-element.65), calls=%async_computation.1 | async-start | bytes 786432 | tf_op jit(solution)/shard_map/all_to_all | solution.py:568
  83.6 9.9 %collective-permute-start.11 = (f32[72,1280]{1,0:T(8,128)S(1)}, f32[72,1280]{1,0:T(8,128)S(1)}, u32[]{:S(2)}, u32[]{:S(2)}) collective-permute-start(f32[72,1280]{1,0:T(8,128)S(1)} %get-tuple-element.71), channel_id=1, source_target_pairs={{0,16},{16,32},{32,48},{48,0},{1,17},{17,33},{33,49},{49,1},{2,18}... | collective-permute-start | bytes 1105928 | tf_op jit(solution)/shard_map/ppermute | solution.py:593
  83.7 26.0 %collective-permute-start.6 = (f32[224,1280]{1,0:T(8,128)S(1)}, f32[224,1280]{1,0:T(8,128)S(1)}, u32[]{:S(2)}, u32[]{:S(2)}) collective-permute-start(f32[224,1280]{1,0:T(8,128)S(1)} %add_add_fusion.refs_7_), channel_id=1, source_target_pairs={{0,64},{64,0},{1,65},{65,1},{2,66},{66,2},{3,67},{67,3},{4,68},{68... | collective-permute-start | bytes 3440648 | tf_op jit(solution)/shard_map/ppermute | solution.py:577
  86.4 9.3 %collective-permute-start.13 = (f32[80,1280]{1,0:T(8,128)S(1)}, f32[80,1280]{1,0:T(8,128)S(1)}, u32[]{:S(2)}, u32[]{:S(2)}) collective-permute-start(f32[80,1280]{1,0:T(8,128)S(1)} %get-tuple-element.73), channel_id=1, source_target_pairs={{0,48},{16,0},{32,16},{48,32},{1,49},{17,1},{33,17},{49,33},{2,50}... | collective-permute-start | bytes 1228808 | tf_op jit(solution)/shard_map/ppermute | solution.py:594
  93.6 7.4 %copy-start.9 = (f32[6,6]{1,0:T(8,128)S(1)}, f32[6,6]{1,0:T(8,128)}, u32[]{:S(2)}) copy-start(f32[6,6]{1,0:T(8,128)} %param.20) | copy-start | bytes 436
  93.6 7.5 %copy-start.10 = (f32[6,6]{1,0:T(8,128)S(1)}, f32[6,6]{1,0:T(8,128)}, u32[]{:S(2)}) copy-start(f32[6,6]{1,0:T(8,128)} %param.21) | copy-start | bytes 436
  93.6 7.6 %copy-start.11 = (f32[6,6]{1,0:T(8,128)S(1)}, f32[6,6]{1,0:T(8,128)}, u32[]{:S(2)}) copy-start(f32[6,6]{1,0:T(8,128)} %param.23) | copy-start | bytes 436
  93.6 7.7 %copy-start.12 = (f32[6,6]{1,0:T(8,128)S(1)}, f32[6,6]{1,0:T(8,128)}, u32[]{:S(2)}) copy-start(f32[6,6]{1,0:T(8,128)} %param.24) | copy-start | bytes 436
  93.6 16.1 %copy-start.6 = (f32[6]{0:T(128)S(1)}, f32[6]{0:T(128)}, u32[]{:S(2)}) copy-start(f32[6]{0:T(128)} %refs_4_.3) | copy-start | bytes 76
  95.4 22.0 %collective-permute-start.12 = (f32[152,1280]{1,0:T(8,128)}, f32[152,1280]{1,0:T(8,128)}, u32[]{:S(2)}, u32[]{:S(2)}) collective-permute-start(f32[152,1280]{1,0:T(8,128)} %add_dynamic-update-slice_fusion.1), channel_id=1, source_target_pairs={{0,16},{16,32},{32,48},{48,0},{1,17},{17,33},{33,49},{49,1},{2,18}... | collective-permute-start | bytes 2334728 | tf_op jit(solution)/shard_map/ppermute | solution.py:608
  97.6 19.9 %collective-permute-start.14 = (f32[152,1280]{1,0:T(8,128)}, f32[152,1280]{1,0:T(8,128)}, u32[]{:S(2)}, u32[]{:S(2)}) collective-permute-start(f32[152,1280]{1,0:T(8,128)} %add_dynamic-update-slice_fusion), channel_id=1, source_target_pairs={{0,48},{16,0},{32,16},{48,32},{1,49},{17,1},{33,17},{49,33},{2,50}... | collective-permute-start | bytes 2334728 | tf_op jit(solution)/shard_map/ppermute | solution.py:608
  109.7 47.9 %slice-start = ((s8[5406720]{0:T(1024)(128)(4,1)}), s8[4194304]{0:T(1024)(128)(4,1)S(1)}, s32[]{:S(2)}) async-start(s8[5406720]{0:T(1024)(128)(4,1)} %bitcast.9), calls=%async_computation.4 | async-start | bytes 8388608
  114.0 43.6 %slice-start.1 = ((s8[5406720]{0:T(1024)(128)(4,1)}), s8[1212416]{0:T(1024)(128)(4,1)S(1)}, s32[]{:S(2)}) async-start(s8[5406720]{0:T(1024)(128)(4,1)} %bitcast.9), calls=%async_computation.5 | async-start | bytes 2424832
  114.0 26.2 %collective-permute-start.9 = (f32[224,1280]{1,0:T(8,128)S(1)}, f32[224,1280]{1,0:T(8,128)S(1)}, u32[]{:S(2)}, u32[]{:S(2)}) collective-permute-start(f32[224,1280]{1,0:T(8,128)S(1)} %implicit.2.refs_4_), channel_id=1, source_target_pairs={{0,48},{16,0},{32,16},{48,32},{1,49},{17,1},{33,17},{49,33},{2,50}... | collective-permute-start | bytes 3440648 | tf_op jit(solution)/shard_map/ppermute | solution.py:617
  117.4 26.3 %collective-permute-start.7 = (f32[224,1280]{1,0:T(8,128)S(1)}, f32[224,1280]{1,0:T(8,128)S(1)}, u32[]{:S(2)}, u32[]{:S(2)}) collective-permute-start(f32[224,1280]{1,0:T(8,128)S(1)} %implicit.2.refs_4_), channel_id=1, source_target_pairs={{0,16},{16,32},{32,48},{48,0},{1,17},{17,33},{33,49},{49,1},{2,18}... | collective-permute-start | bytes 3440648 | tf_op jit(solution)/shard_map/ppermute | solution.py:616
  119.0 24.9 %collective-permute-start.15 = (f32[152,1280]{1,0:T(8,128)S(1)}, f32[152,1280]{1,0:T(8,128)S(1)}, u32[]{:S(2)}, u32[]{:S(2)}) collective-permute-start(f32[152,1280]{1,0:T(8,128)S(1)} %add_add_fusion.1.refs_7_), channel_id=1, source_target_pairs={{0,64},{64,0},{1,65},{65,1},{2,66},{66,2},{3,67},{67,3},{4,68},{68... | collective-permute-start | bytes 2334728 | tf_op jit(solution)/shard_map/ppermute | solution.py:577
  140.2 12.6 %collective-permute-start.10 = (f32[112,1280]{1,0:T(8,128)S(1)}, f32[112,1280]{1,0:T(8,128)S(1)}, u32[]{:S(2)}, u32[]{:S(2)}) collective-permute-start(f32[112,1280]{1,0:T(8,128)S(1)} %slice.57), channel_id=1, source_target_pairs={{0,48},{16,0},{32,16},{48,32},{1,49},{17,1},{33,17},{49,33},{2,50}... | collective-permute-start | bytes 1720328 | tf_op jit(solution)/shard_map/ppermute | solution.py:621
  143.8 12.3 %collective-permute-start.8 = (f32[112,1280]{1,0:T(8,128)S(1)}, f32[112,1280]{1,0:T(8,128)S(1)}, u32[]{:S(2)}, u32[]{:S(2)}) collective-permute-start(f32[112,1280]{1,0:T(8,128)S(1)} %slice.56), channel_id=1, source_target_pairs={{0,16},{16,32},{32,48},{48,0},{1,17},{17,33},{33,49},{49,1},{2,18}... | collective-permute-start | bytes 1720328 | tf_op jit(solution)/shard_map/ppermute | solution.py:620
  156.1 23.6 %collective-permute-start.18 = (f32[152,1280]{1,0:T(8,128)S(1)}, f32[152,1280]{1,0:T(8,128)S(1)}, u32[]{:S(2)}, u32[]{:S(2)}) collective-permute-start(f32[152,1280]{1,0:T(8,128)S(1)} %implicit.3.refs_4_), channel_id=1, source_target_pairs={{0,48},{16,0},{32,16},{48,32},{1,49},{17,1},{33,17},{49,33},{2,50}... | collective-permute-start | bytes 2334728 | tf_op jit(solution)/shard_map/ppermute | solution.py:617
  156.3 24.6 %collective-permute-start.16 = (f32[152,1280]{1,0:T(8,128)S(1)}, f32[152,1280]{1,0:T(8,128)S(1)}, u32[]{:S(2)}, u32[]{:S(2)}) collective-permute-start(f32[152,1280]{1,0:T(8,128)S(1)} %implicit.3.refs_4_), channel_id=1, source_target_pairs={{0,16},{16,32},{32,48},{48,0},{1,17},{17,33},{33,49},{49,1},{2,18}... | collective-permute-start | bytes 2334728 | tf_op jit(solution)/shard_map/ppermute | solution.py:616
  171.3 24.4 %all-to-all-start.2 = ((f32[16,3,24,128]{3,2,1,0:T(8,128)}), f32[16,3,24,128]{3,2,1,0:T(8,128)S(1)}, u32[]{:S(2)}, u32[]{:S(2)}) async-start(f32[16,3,24,128]{3,2,1,0:T(8,128)} %bitcast.6), calls=%async_computation.2 | async-start | bytes 1179648 | tf_op jit(solution)/shard_map/all_to_all | solution.py:568
  179.7 12.2 %collective-permute-start.19 = (f32[80,1280]{1,0:T(8,128)S(1)}, f32[80,1280]{1,0:T(8,128)S(1)}, u32[]{:S(2)}, u32[]{:S(2)}) collective-permute-start(f32[80,1280]{1,0:T(8,128)S(1)} %slice.59), channel_id=1, source_target_pairs={{0,48},{16,0},{32,16},{48,32},{1,49},{17,1},{33,17},{49,33},{2,50}... | collective-permute-start | bytes 1228808 | tf_op jit(solution)/shard_map/ppermute | solution.py:621
  180.9 11.0 %collective-permute-start.17 = (f32[72,1280]{1,0:T(8,128)S(1)}, f32[72,1280]{1,0:T(8,128)S(1)}, u32[]{:S(2)}, u32[]{:S(2)}) collective-permute-start(f32[72,1280]{1,0:T(8,128)S(1)} %slice.58), channel_id=1, source_target_pairs={{0,16},{16,32},{32,48},{48,0},{1,17},{17,33},{33,49},{49,1},{2,18}... | collective-permute-start | bytes 1105928 | tf_op jit(solution)/shard_map/ppermute | solution.py:620
  195.7 15.2 %all-to-all-start.3 = ((f32[16,3,16,128]{3,2,1,0:T(8,128)}), f32[16,3,16,128]{3,2,1,0:T(8,128)S(1)}, u32[]{:S(2)}, u32[]{:S(2)}) async-start(f32[16,3,16,128]{3,2,1,0:T(8,128)} %bitcast.7), calls=%async_computation.3 | async-start | bytes 786432 | tf_op jit(solution)/shard_map/all_to_all | solution.py:568
  202.4 8.5 %copy-start.5 = (f32[2,20,128]{2,1,0:T(8,128)S(1)}, f32[2,20,128]{2,1,0:T(8,128)}, u32[]{:S(2)}) copy-start(f32[2,20,128]{2,1,0:T(8,128)} %constant.76.clone.refs_1_.twiddle_ref) | copy-start | bytes 61444
  202.4 8.5 %copy-start.7 = (f32[40]{0:T(128)S(1)}, f32[40]{0:T(128)}, u32[]{:S(2)}) copy-start(f32[40]{0:T(128)} %weight_ref.1) | copy-start | bytes 484
  202.4 8.5 %copy-start.8 = (bf16[512,512]{1,0:T(8,128)(2,1)S(1)}, bf16[512,512]{1,0:T(8,128)(2,1)}, u32[]{:S(2)}) copy-start(bf16[512,512]{1,0:T(8,128)(2,1)} %constant.78.clone.table_ref) | copy-start | bytes 1572868

commit v5 on v4

--- a/solution.py
+++ b/solution.py
@@ -611,10 +611,10 @@
         now, before = steps[k], steps[k - 1] if k else None
         theirs = after(now["theirs"], *before["ends"]) if k else now["theirs"]
         now["new"] = new = implicit(start, count, now["sum"], theirs)
-        if k:
-            new = after(new, before["top"], before["bottom"])
-        left = lax.ppermute(new, "z", UP)
-        right = lax.ppermute(new, "z", DOWN)
+        upward = after(new, before["top"]) if k else new
+        downward = after(new, before["bottom"]) if k else new
+        left = lax.ppermute(upward, "z", UP)
+        right = lax.ppermute(downward, "z", DOWN)
         now["left"], now["right"] = left, right
         now["ends"] = left[: now["cut"]], right[now["cut"] :]
         now["top"] = lax.ppermute(now["ends"][0], "z", UP)

time: 217 us -> 217 us (level)
  starting transfers between devices: 50.1 us -> 52.9 us
  waiting for transfers between devices: 64.8 us -> 62 us
    ppermute x2, waiting for transfers between devices: 6.93 us -> 4.05 us  [per_device(): now['top'] = lax.ppermute(now['ends'][0], 'z', UP)]
  transfers between devices with their start and end apart: 23 -> 23, of which waited for: 11 -> 10; matrix products, arithmetic and copies ran while one was open for 3% -> 3% of each run, Pallas kernels for 28% -> 28%
where the time goes in v5:
time: 217 us; the launch traced here: 216 us
  Pallas kernels  72.6 us (33%)
  waiting for transfers between devices  62 us (29%)
  starting transfers between devices  52.9 us (24%)
  blocking collectives  16.4 us (8%)
  other arithmetic  7.05 us (3%)
  local copies, waits for them, and re-layouts  4.38 us (2%)
    pallas_call x4, Pallas kernels, grid_rows(): pl.pallas_call(lambda *refs: grid_rows_kernel(start, count, rels, *refs),...  24.4 us
    pallas_call x4, Pallas kernels, spectra(): pl.pallas_call(lambda *refs: spectra_kernel(start, count, rels, *refs), o...  23.7 us
    all_to_all x3, starting transfers between devices, exchange(): return lax.all_to_all(value, ('core', 'wave'), 0, 0, tiled=True)  19 us
    ppermute x2, waiting for transfers between devices, per_device(): right = lax.ppermute(downward, 'z', DOWN)  18.4 us
    all_to_all x1, blocking collectives, exchange(): return lax.all_to_all(value, ('core', 'wave'), 0, 0, tiled=True)  16.4 us
    all_to_all x3, waiting for transfers between devices, exchange(): return lax.all_to_all(value, ('core', 'wave'), 0, 0, tiled=True)  15.7 us
    ppermute x2, waiting for transfers between devices, per_device(): top = lax.ppermute(top, 'z', UP)  9.08 us
    pallas_call x2, Pallas kernels, implicit(): pl.pallas_call(lambda *refs: implicit_kernel(start, count, *refs), out_sh...  8.48 us
  transfers between devices with their start and end apart: 23, of which 10 were waited for; matrix products, arithmetic and copies ran while one was open for 3% of the time, Pallas kernels for 28%

profile of v5, /device:TPU:1, one launch (start us, length us, event | category | flops | bytes accessed | tf_op | source)
XLA Modules:
  0.0 215.6 jit_solution(17343767725091536025)
XLA Ops:
  0.1 0.8 broadcast_in_dim.2.owner_ref
  0.9 1.3 copy-done.1
  2.2 1.0 copy-done.2
  3.2 0.7 copy-done.4
  4.0 8.4 %fourier.1 = (f32[16,3,24,128]{3,2,1,0:T(8,128)S(1)}, f32[16,3,16,128]{3,2,1,0:T(8,128)}, f32[24,40,1408]{2,1,0:T(8,128)S(1)}, f32[16,40,1408]{2,1,0:T(8,128)}) custom-call(s32[3]{0:T(128)S(1)} %pad_add_fusion.place_ref.refs_0_, s32[640,128]{1,0:T(8,128)S(1)} %broadcast_in_dim.2.owner_ref, f32[3,5,6,2560]{3,2,1,0:T(8,128)S(1)} %bitcast.15, ...), custom_call_target="tpu_custom_call" | custom-call | flops 4000000000 | bytes 26000000 | tf_op jit(solution)/shard_map/fourier/pallas_call | solution.py:472
  12.4 1.5 collective-permute-start
  13.9 16.4 %all_to_all.20 = f32[16,3,24,128]{3,2,1,0:T(8,128)S(1)} all-to-all(f32[16,3,24,128]{3,2,1,0:T(8,128)S(1)} %get-tuple-element.55), channel_id=1, replica_groups=mesh['yh'=2,'z'=4,'core'=2,'wave'=8] {'core','wave'}, dimensions={0} | all-to-all | bytes 1179648 | tf_op jit(solution)/shard_map/all_to_all | solution.py:568
  30.3 0.8 collective-permute-start.4
  31.1 4.2 %spectra.5 = (f32[112,1280]{1,0:T(8,128)S(1)}, f32[112,1280]{1,0:T(8,128)S(1)}) custom-call(s32[3]{0:T(128)S(1)} %pad_add_fusion.place_ref.refs_0_, s32[640]{0:T(1024)S(1)} %copy-done.3, f32[80,40,1408]{2,1,0:T(8,128)} %refs_2_.16, f32[24,40,1408]{2,1,0:T(8,128)S(1)} %collective-permute-done.refs_3_, f32[1152,128]{1,0:T(8,128)S(1)} %bitcast.11), custom_call_target="tpu_custom_call" | custom-call | flops 300000000 | bytes 3000000 | tf_op jit(solution)/shard_map/spectra/pallas_call | solution.py:519
  35.3 1.7 collective-permute-start.1
  37.0 2.2 %collective-permute-start.2 = (f32[112,1280]{1,0:T(8,128)S(1)}, f32[112,1280]{1,0:T(8,128)S(1)}, u32[]{:S(2)}, u32[]{:S(2)}) collective-permute-start(f32[112,1280]{1,0:T(8,128)S(1)} %get-tuple-element.60), channel_id=1, source_target_pairs={{0,48},{16,0},{32,16},{48,32},{1,49},{17,1},{33,17},{49,33},{2,50}... | collective-permute-start | bytes 1720328 | tf_op jit(solution)/shard_map/ppermute | solution.py:594
  39.2 8.7 %spectra.4 = (f32[224,1280]{1,0:T(8,128)S(1)}, f32[224,1280]{1,0:T(8,128)S(1)}, f32[224,1280]{1,0:T(8,128)S(1)}) custom-call(s32[3]{0:T(128)S(1)} %pad_add_fusion.place_ref.refs_0_, s32[640]{0:T(1024)S(1)} %copy-done.3, f32[80,40,1408]{2,1,0:T(8,128)} %refs_2_.16, f32[24,40,1408]{2,1,0:T(8,128)S(1)} %collective-permute-done.refs_3_, f32[1152,128]{1,0:T(8,128)S(1)} %bitcast.12), custom_call_target="tpu_custom_call" | custom-call | flops 900000000 | bytes 9000000 | tf_op jit(solution)/shard_map/spectra/pallas_call | solution.py:519
  47.9 4.5 %collective-permute-done.1.top_ref = f32[112,1280]{1,0:T(8,128)S(1)} collective-permute-done((f32[112,1280]{1,0:T(8,128)S(1)}, f32[112,1280]{1,0:T(8,128)S(1)}, u32[]{:S(2)}, u32[]{:S(2)}) %collective-permute-start.1) | collective-permute-done | bytes 573472 | tf_op jit(solution)/shard_map/ppermute | solution.py:593
  52.5 1.6 fold.1
  54.5 2.2 %collective-permute-start.5 = (f32[224,1280]{1,0:T(8,128)}, f32[224,1280]{1,0:T(8,128)}, u32[]{:S(2)}, u32[]{:S(2)}) collective-permute-start(f32[224,1280]{1,0:T(8,128)} %get-tuple-element.65), channel_id=1, source_target_pairs={{0,48},{16,0},{32,16},{48,32},{1,49},{17,1},{33,17},{49,33},{2,50}... | collective-permute-start | bytes 3440648 | tf_op jit(solution)/shard_map/ppermute | solution.py:608
  56.8 4.5 %all-to-all-start.1 = ((f32[16,3,16,128]{3,2,1,0:T(8,128)}), f32[16,3,16,128]{3,2,1,0:T(8,128)S(1)}, u32[]{:S(2)}, u32[]{:S(2)}) async-start(f32[16,3,16,128]{3,2,1,0:T(8,128)} %get-tuple-element.66), calls=%async_computation.1 | async-start | bytes 786432 | tf_op jit(solution)/shard_map/all_to_all | solution.py:568
  61.3 8.5 %all-to-all-done.1 = f32[16,3,16,128]{3,2,1,0:T(8,128)S(1)} async-done(((f32[16,3,16,128]{3,2,1,0:T(8,128)}), f32[16,3,16,128]{3,2,1,0:T(8,128)S(1)}, u32[]{:S(2)}, u32[]{:S(2)}) %all-to-all-start.1) | async-done | bytes 393248 | tf_op jit(solution)/shard_map/all_to_all | solution.py:568
  69.8 3.0 %spectra.7 = (f32[72,1280]{1,0:T(8,128)S(1)}, f32[80,1280]{1,0:T(8,128)S(1)}) custom-call(s32[3]{0:T(128)S(1)} %pad_add_fusion.place_ref.refs_0_, s32[640]{0:T(1024)S(1)} %copy-done.3, f32[80,40,1408]{2,1,0:T(8,128)} %refs_2_.16, f32[16,40,1408]{2,1,0:T(8,128)} %collective-permute-done.4.refs_3_, f32[768,128]{1,0:T(8,128)S(1)} %bitcast.13), custom_call_target="tpu_custom_call" | custom-call | flops 200000000 | bytes 2000000 | tf_op jit(solution)/shard_map/spectra/pallas_call | solution.py:519
  72.8 7.8 %spectra.6 = (f32[152,1280]{1,0:T(8,128)}, f32[152,1280]{1,0:T(8,128)}, f32[152,1280]{1,0:T(8,128)S(1)}) custom-call(s32[3]{0:T(128)S(1)} %pad_add_fusion.place_ref.refs_0_, s32[640]{0:T(1024)S(1)} %copy-done.3, f32[80,40,1408]{2,1,0:T(8,128)} %refs_2_.16, f32[16,40,1408]{2,1,0:T(8,128)} %collective-permute-done.4.refs_3_, f32[768,128]{1,0:T(8,128)S(1)} %bitcast.14), custom_call_target="tpu_custom_call" | custom-call | flops 600000000 | bytes 6000000 | tf_op jit(solution)/shard_map/spectra/pallas_call | solution.py:519
  80.6 1.2 collective-permute-done.3
  81.8 1.8 add_add_fusion.refs_7_
  83.7 2.7 %collective-permute-start.6 = (f32[224,1280]{1,0:T(8,128)S(1)}, f32[224,1280]{1,0:T(8,128)S(1)}, u32[]{:S(2)}, u32[]{:S(2)}) collective-permute-start(f32[224,1280]{1,0:T(8,128)S(1)} %add_add_fusion.refs_7_), channel_id=1, source_target_pairs={{0,64},{64,0},{1,65},{65,1},{2,66},{66,2},{3,67},{67,3},{4,68},{68... | collective-permute-start | bytes 3440648 | tf_op jit(solution)/shard_map/ppermute | solution.py:577
  86.4 2.6 %collective-permute-start.13 = (f32[80,1280]{1,0:T(8,128)S(1)}, f32[80,1280]{1,0:T(8,128)S(1)}, u32[]{:S(2)}, u32[]{:S(2)}) collective-permute-start(f32[80,1280]{1,0:T(8,128)S(1)} %get-tuple-element.74), channel_id=1, source_target_pairs={{0,48},{16,0},{32,16},{48,32},{1,49},{17,1},{33,17},{49,33},{2,50}... | collective-permute-start | bytes 1228808 | tf_op jit(solution)/shard_map/ppermute | solution.py:594
  89.0 4.5 %collective-permute-done.11 = f32[72,1280]{1,0:T(8,128)S(1)} collective-permute-done((f32[72,1280]{1,0:T(8,128)S(1)}, f32[72,1280]{1,0:T(8,128)S(1)}, u32[]{:S(2)}, u32[]{:S(2)}) %collective-permute-start.11) | collective-permute-done | bytes 368672 | tf_op jit(solution)/shard_map/ppermute | solution.py:593
  93.6 1.8 add_dynamic-update-slice_fusion.1
  95.8 1.8 add_dynamic-update-slice_fusion
  97.6 3.4 %collective-permute-start.14 = (f32[152,1280]{1,0:T(8,128)}, f32[152,1280]{1,0:T(8,128)}, u32[]{:S(2)}, u32[]{:S(2)}) collective-permute-start(f32[152,1280]{1,0:T(8,128)} %add_dynamic-update-slice_fusion), channel_id=1, source_target_pairs={{0,48},{16,0},{32,16},{48,32},{1,49},{17,1},{33,17},{49,33},{2,50}... | collective-permute-start | bytes 2334728 | tf_op jit(solution)/shard_map/ppermute | solution.py:608
  101.3 8.4 %collective-permute-done.6.refs_8_ = f32[224,1280]{1,0:T(8,128)S(1)} collective-permute-done((f32[224,1280]{1,0:T(8,128)S(1)}, f32[224,1280]{1,0:T(8,128)S(1)}, u32[]{:S(2)}, u32[]{:S(2)}) %collective-permute-start.6) | collective-permute-done | bytes 1146912 | tf_op jit(solution)/shard_map/ppermute | solution.py:577
  109.7 4.2 %implicit.2.refs_4_ = f32[224,1280]{1,0:T(8,128)S(1)} custom-call(s32[3]{0:T(128)S(1)} %pad_add_fusion.place_ref.refs_0_, s32[640]{0:T(1024)S(1)} %copy-done.3, f32[36]{0:T(128)S(1)} %reshape.74.refs_2_, f32[36]{0:T(128)S(1)} %reshape.75.refs_3_, f32[6]{0:T(128)S(1)} %copy-done.6, f32[36]{0:T(128)S(1)} %reshape.76.refs_5_, f32[36]{0:T(128)S(1)} %reshape.77.refs_6_, ...), custom_call_target="tpu_custom_call" | custom-call | flops 60000000 | bytes 3600000 | tf_op jit(solution)/shard_map/implicit/pallas_call | solution.py:536
  114.0 3.5 %collective-permute-start.9 = (f32[224,1280]{1,0:T(8,128)S(1)}, f32[224,1280]{1,0:T(8,128)S(1)}, u32[]{:S(2)}, u32[]{:S(2)}) collective-permute-start(f32[224,1280]{1,0:T(8,128)S(1)} %implicit.2.refs_4_), channel_id=1, source_target_pairs={{0,48},{16,0},{32,16},{48,32},{1,49},{17,1},{33,17},{49,33},{2,50}... | collective-permute-start | bytes 3440648 | tf_op jit(solution)/shard_map/ppermute | solution.py:617
  117.4 1.5 add_add_fusion.1.refs_7_
  119.0 2.8 %collective-permute-start.15 = (f32[152,1280]{1,0:T(8,128)S(1)}, f32[152,1280]{1,0:T(8,128)S(1)}, u32[]{:S(2)}, u32[]{:S(2)}) collective-permute-start(f32[152,1280]{1,0:T(8,128)S(1)} %add_add_fusion.1.refs_7_), channel_id=1, source_target_pairs={{0,64},{64,0},{1,65},{65,1},{2,66},{66,2},{3,67},{67,3},{4,68},{68... | collective-permute-start | bytes 2334728 | tf_op jit(solution)/shard_map/ppermute | solution.py:577
  121.8 18.4 %collective-permute-done.9.refs_5_ = f32[224,1280]{1,0:T(8,128)S(1)} collective-permute-done((f32[224,1280]{1,0:T(8,128)S(1)}, f32[224,1280]{1,0:T(8,128)S(1)}, u32[]{:S(2)}, u32[]{:S(2)}) %collective-permute-start.9) | collective-permute-done | bytes 1146912 | tf_op jit(solution)/shard_map/ppermute | solution.py:617
  140.2 3.5 %collective-permute-start.10 = (f32[112,1280]{1,0:T(8,128)S(1)}, f32[112,1280]{1,0:T(8,128)S(1)}, u32[]{:S(2)}, u32[]{:S(2)}) collective-permute-start(f32[112,1280]{1,0:T(8,128)S(1)} %slice.57), channel_id=1, source_target_pairs={{0,48},{16,0},{32,16},{48,32},{1,49},{17,1},{33,17},{49,33},{2,50}... | collective-permute-start | bytes 1720328 | tf_op jit(solution)/shard_map/ppermute | solution.py:621
  143.9 4.2 %implicit.3.refs_4_ = f32[152,1280]{1,0:T(8,128)S(1)} custom-call(s32[3]{0:T(128)S(1)} %pad_add_fusion.place_ref.refs_0_, s32[640]{0:T(1024)S(1)} %copy-done.3, f32[36]{0:T(128)S(1)} %reshape.74.refs_2_, f32[36]{0:T(128)S(1)} %reshape.75.refs_3_, f32[6]{0:T(128)S(1)} %copy-done.6, f32[36]{0:T(128)S(1)} %reshape.76.refs_5_, f32[36]{0:T(128)S(1)} %reshape.77.refs_6_, ...), custom_call_target="tpu_custom_call" | custom-call | flops 40000000 | bytes 2400000 | tf_op jit(solution)/shard_map/implicit/pallas_call | solution.py:536
  148.1 4.7 %collective-permute-done.10.refs_5_ = f32[112,1280]{1,0:T(8,128)S(1)} collective-permute-done((f32[112,1280]{1,0:T(8,128)S(1)}, f32[112,1280]{1,0:T(8,128)S(1)}, u32[]{:S(2)}, u32[]{:S(2)}) %collective-permute-start.10) | collective-permute-done | bytes 573472 | tf_op jit(solution)/shard_map/ppermute | solution.py:621
  152.8 3.4 %collective-permute-start.18 = (f32[152,1280]{1,0:T(8,128)S(1)}, f32[152,1280]{1,0:T(8,128)S(1)}, u32[]{:S(2)}, u32[]{:S(2)}) collective-permute-start(f32[152,1280]{1,0:T(8,128)S(1)} %implicit.3.refs_4_), channel_id=1, source_target_pairs={{0,48},{16,0},{32,16},{48,32},{1,49},{17,1},{33,17},{49,33},{2,50}... | collective-permute-start | bytes 2334728 | tf_op jit(solution)/shard_map/ppermute | solution.py:617
  156.3 9.0 %grid_rows.4.refs_6_ = f32[1152,128]{1,0:T(8,128)S(1)} custom-call(s32[3]{0:T(128)S(1)} %pad_add_fusion.place_ref.refs_0_, s32[640]{0:T(1024)S(1)} %copy-done.3, f32[80,40,1408]{2,1,0:T(8,128)} %refs_2_.16, f32[24,40,1408]{2,1,0:T(8,128)S(1)} %bitcast.10, f32[224,1280]{1,0:T(8,128)S(1)} %implicit.2.refs_4_, f32[224,1280]{1,0:T(8,128)S(1)} %collective-permute-done.9.refs_5_, ...), custom_call_target="tpu_custom_call" | custom-call | flops 1260000000 | bytes 9000000 | tf_op jit(solution)/shard_map/grid_rows/pallas_call | solution.py:549
  165.3 4.8 %grid_rows.5 = f32[1152,128]{1,0:T(8,128)} custom-call(s32[3]{0:T(128)S(1)} %pad_add_fusion.place_ref.refs_0_, s32[640]{0:T(1024)S(1)} %copy-done.3, f32[80,40,1408]{2,1,0:T(8,128)} %refs_2_.16, f32[24,40,1408]{2,1,0:T(8,128)S(1)} %bitcast.10, f32[112,1280]{1,0:T(8,128)S(1)} %collective-permute-done.8.refs_4_, ...), custom_call_target="tpu_custom_call" | custom-call | flops 420000000 | bytes 3000000 | tf_op jit(solution)/shard_map/grid_rows/pallas_call | solution.py:549
  170.1 7.8 %all-to-all-start.2 = ((f32[16,3,24,128]{3,2,1,0:T(8,128)}), f32[16,3,24,128]{3,2,1,0:T(8,128)S(1)}, u32[]{:S(2)}, u32[]{:S(2)}) async-start(f32[16,3,24,128]{3,2,1,0:T(8,128)} %bitcast.6), calls=%async_computation.2 | async-start | bytes 1179648 | tf_op jit(solution)/shard_map/all_to_all | solution.py:568
  177.9 3.0 %collective-permute-start.19 = (f32[80,1280]{1,0:T(8,128)S(1)}, f32[80,1280]{1,0:T(8,128)S(1)}, u32[]{:S(2)}, u32[]{:S(2)}) collective-permute-start(f32[80,1280]{1,0:T(8,128)S(1)} %slice.59), channel_id=1, source_target_pairs={{0,48},{16,0},{32,16},{48,32},{1,49},{17,1},{33,17},{49,33},{2,50}... | collective-permute-start | bytes 1228808 | tf_op jit(solution)/shard_map/ppermute | solution.py:621
  181.0 6.8 %grid_rows.6.refs_6_ = f32[768,128]{1,0:T(8,128)S(1)} custom-call(s32[3]{0:T(128)S(1)} %pad_add_fusion.place_ref.refs_0_, s32[640]{0:T(1024)S(1)} %copy-done.3, f32[80,40,1408]{2,1,0:T(8,128)} %refs_2_.16, f32[16,40,1408]{2,1,0:T(8,128)} %collective-permute-done.4.refs_3_, f32[152,1280]{1,0:T(8,128)S(1)} %implicit.3.refs_4_, ...), custom_call_target="tpu_custom_call" | custom-call | flops 840000000 | bytes 6000000 | tf_op jit(solution)/shard_map/grid_rows/pallas_call | solution.py:549
  187.8 4.0 %collective-permute-done.17.refs_4_ = f32[72,1280]{1,0:T(8,128)S(1)} collective-permute-done((f32[72,1280]{1,0:T(8,128)S(1)}, f32[72,1280]{1,0:T(8,128)S(1)}, u32[]{:S(2)}, u32[]{:S(2)}) %collective-permute-start.17) | collective-permute-done | bytes 368672 | tf_op jit(solution)/shard_map/ppermute | solution.py:620
  191.9 3.8 %grid_rows.7 = f32[768,128]{1,0:T(8,128)} custom-call(s32[3]{0:T(128)S(1)} %pad_add_fusion.place_ref.refs_0_, s32[640]{0:T(1024)S(1)} %copy-done.3, f32[80,40,1408]{2,1,0:T(8,128)} %refs_2_.16, f32[16,40,1408]{2,1,0:T(8,128)} %collective-permute-done.4.refs_3_, f32[72,1280]{1,0:T(8,128)S(1)} %collective-permute-done.17.refs_4_, ...), custom_call_target="tpu_custom_call" | custom-call | flops 280000000 | bytes 2000000 | tf_op jit(solution)/shard_map/grid_rows/pallas_call | solution.py:549
  195.7 6.7 %all-to-all-start.3 = ((f32[16,3,16,128]{3,2,1,0:T(8,128)}), f32[16,3,16,128]{3,2,1,0:T(8,128)S(1)}, u32[]{:S(2)}, u32[]{:S(2)}) async-start(f32[16,3,16,128]{3,2,1,0:T(8,128)} %bitcast.7), calls=%async_computation.3 | async-start | bytes 786432 | tf_op jit(solution)/shard_map/all_to_all | solution.py:568
  202.4 1.3 scatter.1.early_ref
  203.7 7.1 %all-to-all-done.3.got_ref = f32[16,3,16,128]{3,2,1,0:T(8,128)S(1)} async-done(((f32[16,3,16,128]{3,2,1,0:T(8,128)}), f32[16,3,16,128]{3,2,1,0:T(8,128)S(1)}, u32[]{:S(2)}, u32[]{:S(2)}) %all-to-all-start.3) | async-done | bytes 393248 | tf_op jit(solution)/shard_map/all_to_all | solution.py:568
  210.9 4.7 %inverse.1 = f32[3,5,6,2560]{3,2,1,0:T(8,128)} custom-call(s32[640,128]{1,0:T(8,128)S(1)} %broadcast_in_dim.2.owner_ref, f32[40]{0:T(128)S(1)} %copy-done.7, s32[3]{0:T(128)S(1)} %pad_add_fusion.place_ref.refs_0_, f32[2,20,128]{2,1,0:T(8,128)S(1)} %copy-done.5, bf16[512,512]{1,0:T(8,128)(2,1)S(1)} %copy-done.8, f32[184,1280]{1,0:T(8,128)S(1)} %scatter.1.early_ref, ...), custom_call_target="tpu_custom_call" | custom-call | flops 4000000000 | bytes 8000000 | tf_op jit(solution)/shard_map/inverse/pallas_call | solution.py:641
  (58 shorter events, 1.7 us)
Async XLA Ops:
  0.9 1.3 copy-start.1
  2.2 1.0 copy-start.2
  3.2 0.7 copy-start.4
  12.4 18.7 %copy-start.3 = (s32[640]{0:T(1024)S(1)}, s32[640]{0:T(1024)}, u32[]{:S(2)}) copy-start(s32[640]{0:T(1024)} %refs_1_.20) | copy-start | bytes 7684
  12.4 18.7 %collective-permute-start = (f32[24,40,1408]{2,1,0:T(8,128)S(1)}, f32[24,40,1408]{2,1,0:T(8,128)S(1)}, u32[]{:S(2)}, u32[]{:S(2)}) collective-permute-start(f32[24,40,1408]{2,1,0:T(8,128)S(1)} %get-tuple-element.54), channel_id=1, source_target_pairs={{0,8},{8,0},{1,9},{9,1},{2,10},{10,2},{3,11},{11,3},{4,12},{12,4},... | collective-permute-start | bytes 16220168 | tf_op jit(solution)/shard_map/ppermute | solution.py:586
  30.3 30.9 %collective-permute-start.4 = (f32[16,40,1408]{2,1,0:T(8,128)}, f32[16,40,1408]{2,1,0:T(8,128)}, u32[]{:S(2)}, u32[]{:S(2)}) collective-permute-start(f32[16,40,1408]{2,1,0:T(8,128)} %get-tuple-element.63), channel_id=1, source_target_pairs={{0,8},{8,0},{1,9},{9,1},{2,10},{10,2},{3,11},{11,3},{4,12},{12,4},... | collective-permute-start | bytes 10813448 | tf_op jit(solution)/shard_map/ppermute | solution.py:586
  31.1 8.1 %copy-start = (f32[24,40,1408]{2,1,0:T(8,128)}, f32[24,40,1408]{2,1,0:T(8,128)S(1)}, u32[]{:S(2)}) copy-start(f32[24,40,1408]{2,1,0:T(8,128)S(1)} %collective-permute-done.refs_3_) | copy-start | bytes 16220164
  35.3 17.2 %collective-permute-start.1 = (f32[112,1280]{1,0:T(8,128)S(1)}, f32[112,1280]{1,0:T(8,128)S(1)}, u32[]{:S(2)}, u32[]{:S(2)}) collective-permute-start(f32[112,1280]{1,0:T(8,128)S(1)} %get-tuple-element.58), channel_id=1, source_target_pairs={{0,16},{16,32},{32,48},{48,0},{1,17},{17,33},{33,49},{49,1},{2,18}... | collective-permute-start | bytes 1720328 | tf_op jit(solution)/shard_map/ppermute | solution.py:593
  37.0 15.5 %collective-permute-start.2 = (f32[112,1280]{1,0:T(8,128)S(1)}, f32[112,1280]{1,0:T(8,128)S(1)}, u32[]{:S(2)}, u32[]{:S(2)}) collective-permute-start(f32[112,1280]{1,0:T(8,128)S(1)} %get-tuple-element.60), channel_id=1, source_target_pairs={{0,48},{16,0},{32,16},{48,32},{1,49},{17,1},{33,17},{49,33},{2,50}... | collective-permute-start | bytes 1720328 | tf_op jit(solution)/shard_map/ppermute | solution.py:594
  54.1 27.8 %collective-permute-start.3 = (f32[224,1280]{1,0:T(8,128)}, f32[224,1280]{1,0:T(8,128)}, u32[]{:S(2)}, u32[]{:S(2)}) collective-permute-start(f32[224,1280]{1,0:T(8,128)} %get-tuple-element.61), channel_id=1, source_target_pairs={{0,16},{16,32},{32,48},{48,0},{1,17},{17,33},{33,49},{49,1},{2,18}... | collective-permute-start | bytes 3440648 | tf_op jit(solution)/shard_map/ppermute | solution.py:608
  54.5 27.3 %collective-permute-start.5 = (f32[224,1280]{1,0:T(8,128)}, f32[224,1280]{1,0:T(8,128)}, u32[]{:S(2)}, u32[]{:S(2)}) collective-permute-start(f32[224,1280]{1,0:T(8,128)} %get-tuple-element.65), channel_id=1, source_target_pairs={{0,48},{16,0},{32,16},{48,32},{1,49},{17,1},{33,17},{49,33},{2,50}... | collective-permute-start | bytes 3440648 | tf_op jit(solution)/shard_map/ppermute | solution.py:608
  56.8 13.1 %all-to-all-start.1 = ((f32[16,3,16,128]{3,2,1,0:T(8,128)}), f32[16,3,16,128]{3,2,1,0:T(8,128)S(1)}, u32[]{:S(2)}, u32[]{:S(2)}) async-start(f32[16,3,16,128]{3,2,1,0:T(8,128)} %get-tuple-element.66), calls=%async_computation.1 | async-start | bytes 786432 | tf_op jit(solution)/shard_map/all_to_all | solution.py:568
  83.6 9.9 %collective-permute-start.11 = (f32[72,1280]{1,0:T(8,128)S(1)}, f32[72,1280]{1,0:T(8,128)S(1)}, u32[]{:S(2)}, u32[]{:S(2)}) collective-permute-start(f32[72,1280]{1,0:T(8,128)S(1)} %get-tuple-element.72), channel_id=1, source_target_pairs={{0,16},{16,32},{32,48},{48,0},{1,17},{17,33},{33,49},{49,1},{2,18}... | collective-permute-start | bytes 1105928 | tf_op jit(solution)/shard_map/ppermute | solution.py:593
  83.7 26.0 %collective-permute-start.6 = (f32[224,1280]{1,0:T(8,128)S(1)}, f32[224,1280]{1,0:T(8,128)S(1)}, u32[]{:S(2)}, u32[]{:S(2)}) collective-permute-start(f32[224,1280]{1,0:T(8,128)S(1)} %add_add_fusion.refs_7_), channel_id=1, source_target_pairs={{0,64},{64,0},{1,65},{65,1},{2,66},{66,2},{3,67},{67,3},{4,68},{68... | collective-permute-start | bytes 3440648 | tf_op jit(solution)/shard_map/ppermute | solution.py:577
  86.4 9.3 %collective-permute-start.13 = (f32[80,1280]{1,0:T(8,128)S(1)}, f32[80,1280]{1,0:T(8,128)S(1)}, u32[]{:S(2)}, u32[]{:S(2)}) collective-permute-start(f32[80,1280]{1,0:T(8,128)S(1)} %get-tuple-element.74), channel_id=1, source_target_pairs={{0,48},{16,0},{32,16},{48,32},{1,49},{17,1},{33,17},{49,33},{2,50}... | collective-permute-start | bytes 1228808 | tf_op jit(solution)/shard_map/ppermute | solution.py:594
  93.6 7.4 %copy-start.9 = (f32[6,6]{1,0:T(8,128)S(1)}, f32[6,6]{1,0:T(8,128)}, u32[]{:S(2)}) copy-start(f32[6,6]{1,0:T(8,128)} %param.20) | copy-start | bytes 436
  93.6 7.5 %copy-start.10 = (f32[6,6]{1,0:T(8,128)S(1)}, f32[6,6]{1,0:T(8,128)}, u32[]{:S(2)}) copy-start(f32[6,6]{1,0:T(8,128)} %param.21) | copy-start | bytes 436
  93.6 7.6 %copy-start.11 = (f32[6,6]{1,0:T(8,128)S(1)}, f32[6,6]{1,0:T(8,128)}, u32[]{:S(2)}) copy-start(f32[6,6]{1,0:T(8,128)} %param.23) | copy-start | bytes 436
  93.6 7.7 %copy-start.12 = (f32[6,6]{1,0:T(8,128)S(1)}, f32[6,6]{1,0:T(8,128)}, u32[]{:S(2)}) copy-start(f32[6,6]{1,0:T(8,128)} %param.24) | copy-start | bytes 436
  93.6 16.1 %copy-start.6 = (f32[6]{0:T(128)S(1)}, f32[6]{0:T(128)}, u32[]{:S(2)}) copy-start(f32[6]{0:T(128)} %refs_4_.3) | copy-start | bytes 76
  95.4 22.0 %collective-permute-start.12 = (f32[152,1280]{1,0:T(8,128)}, f32[152,1280]{1,0:T(8,128)}, u32[]{:S(2)}, u32[]{:S(2)}) collective-permute-start(f32[152,1280]{1,0:T(8,128)} %add_dynamic-update-slice_fusion.1), channel_id=1, source_target_pairs={{0,16},{16,32},{32,48},{48,0},{1,17},{17,33},{33,49},{49,1},{2,18}... | collective-permute-start | bytes 2334728 | tf_op jit(solution)/shard_map/ppermute | solution.py:608
  97.6 19.9 %collective-permute-start.14 = (f32[152,1280]{1,0:T(8,128)}, f32[152,1280]{1,0:T(8,128)}, u32[]{:S(2)}, u32[]{:S(2)}) collective-permute-start(f32[152,1280]{1,0:T(8,128)} %add_dynamic-update-slice_fusion), channel_id=1, source_target_pairs={{0,48},{16,0},{32,16},{48,32},{1,49},{17,1},{33,17},{49,33},{2,50}... | collective-permute-start | bytes 2334728 | tf_op jit(solution)/shard_map/ppermute | solution.py:608
  109.7 46.6 %slice-start = ((s8[5406720]{0:T(1024)(128)(4,1)}), s8[4194304]{0:T(1024)(128)(4,1)S(1)}, s32[]{:S(2)}) async-start(s8[5406720]{0:T(1024)(128)(4,1)} %bitcast.9), calls=%async_computation.4 | async-start | bytes 8388608
  114.0 42.3 %slice-start.1 = ((s8[5406720]{0:T(1024)(128)(4,1)}), s8[1212416]{0:T(1024)(128)(4,1)S(1)}, s32[]{:S(2)}) async-start(s8[5406720]{0:T(1024)(128)(4,1)} %bitcast.9), calls=%async_computation.5 | async-start | bytes 2424832
  114.0 26.2 %collective-permute-start.9 = (f32[224,1280]{1,0:T(8,128)S(1)}, f32[224,1280]{1,0:T(8,128)S(1)}, u32[]{:S(2)}, u32[]{:S(2)}) collective-permute-start(f32[224,1280]{1,0:T(8,128)S(1)} %implicit.2.refs_4_), channel_id=1, source_target_pairs={{0,48},{16,0},{32,16},{48,32},{1,49},{17,1},{33,17},{49,33},{2,50}... | collective-permute-start | bytes 3440648 | tf_op jit(solution)/shard_map/ppermute | solution.py:617
  117.4 26.3 %collective-permute-start.7 = (f32[224,1280]{1,0:T(8,128)S(1)}, f32[224,1280]{1,0:T(8,128)S(1)}, u32[]{:S(2)}, u32[]{:S(2)}) collective-permute-start(f32[224,1280]{1,0:T(8,128)S(1)} %implicit.2.refs_4_), channel_id=1, source_target_pairs={{0,16},{16,32},{32,48},{48,0},{1,17},{17,33},{33,49},{49,1},{2,18}... | collective-permute-start | bytes 3440648 | tf_op jit(solution)/shard_map/ppermute | solution.py:616
  119.0 24.9 %collective-permute-start.15 = (f32[152,1280]{1,0:T(8,128)S(1)}, f32[152,1280]{1,0:T(8,128)S(1)}, u32[]{:S(2)}, u32[]{:S(2)}) collective-permute-start(f32[152,1280]{1,0:T(8,128)S(1)} %add_add_fusion.1.refs_7_), channel_id=1, source_target_pairs={{0,64},{64,0},{1,65},{65,1},{2,66},{66,2},{3,67},{67,3},{4,68},{68... | collective-permute-start | bytes 2334728 | tf_op jit(solution)/shard_map/ppermute | solution.py:577
  140.2 12.6 %collective-permute-start.10 = (f32[112,1280]{1,0:T(8,128)S(1)}, f32[112,1280]{1,0:T(8,128)S(1)}, u32[]{:S(2)}, u32[]{:S(2)}) collective-permute-start(f32[112,1280]{1,0:T(8,128)S(1)} %slice.57), channel_id=1, source_target_pairs={{0,48},{16,0},{32,16},{48,32},{1,49},{17,1},{33,17},{49,33},{2,50}... | collective-permute-start | bytes 1720328 | tf_op jit(solution)/shard_map/ppermute | solution.py:621
  143.8 12.5 %collective-permute-start.8 = (f32[112,1280]{1,0:T(8,128)S(1)}, f32[112,1280]{1,0:T(8,128)S(1)}, u32[]{:S(2)}, u32[]{:S(2)}) collective-permute-start(f32[112,1280]{1,0:T(8,128)S(1)} %slice.56), channel_id=1, source_target_pairs={{0,16},{16,32},{32,48},{48,0},{1,17},{17,33},{33,49},{49,1},{2,18}... | collective-permute-start | bytes 1720328 | tf_op jit(solution)/shard_map/ppermute | solution.py:620
  152.8 25.0 %collective-permute-start.18 = (f32[152,1280]{1,0:T(8,128)S(1)}, f32[152,1280]{1,0:T(8,128)S(1)}, u32[]{:S(2)}, u32[]{:S(2)}) collective-permute-start(f32[152,1280]{1,0:T(8,128)S(1)} %implicit.3.refs_4_), channel_id=1, source_target_pairs={{0,48},{16,0},{32,16},{48,32},{1,49},{17,1},{33,17},{49,33},{2,50}... | collective-permute-start | bytes 2334728 | tf_op jit(solution)/shard_map/ppermute | solution.py:617
  156.3 24.6 %collective-permute-start.16 = (f32[152,1280]{1,0:T(8,128)S(1)}, f32[152,1280]{1,0:T(8,128)S(1)}, u32[]{:S(2)}, u32[]{:S(2)}) collective-permute-start(f32[152,1280]{1,0:T(8,128)S(1)} %implicit.3.refs_4_), channel_id=1, source_target_pairs={{0,16},{16,32},{32,48},{48,0},{1,17},{17,33},{33,49},{49,1},{2,18}... | collective-permute-start | bytes 2334728 | tf_op jit(solution)/shard_map/ppermute | solution.py:616
  170.1 25.6 %all-to-all-start.2 = ((f32[16,3,24,128]{3,2,1,0:T(8,128)}), f32[16,3,24,128]{3,2,1,0:T(8,128)S(1)}, u32[]{:S(2)}, u32[]{:S(2)}) async-start(f32[16,3,24,128]{3,2,1,0:T(8,128)} %bitcast.6), calls=%async_computation.2 | async-start | bytes 1179648 | tf_op jit(solution)/shard_map/all_to_all | solution.py:568
  177.9 14.0 %collective-permute-start.19 = (f32[80,1280]{1,0:T(8,128)S(1)}, f32[80,1280]{1,0:T(8,128)S(1)}, u32[]{:S(2)}, u32[]{:S(2)}) collective-permute-start(f32[80,1280]{1,0:T(8,128)S(1)} %slice.59), channel_id=1, source_target_pairs={{0,48},{16,0},{32,16},{48,32},{1,49},{17,1},{33,17},{49,33},{2,50}... | collective-permute-start | bytes 1228808 | tf_op jit(solution)/shard_map/ppermute | solution.py:621
  180.9 11.0 %collective-permute-start.17 = (f32[72,1280]{1,0:T(8,128)S(1)}, f32[72,1280]{1,0:T(8,128)S(1)}, u32[]{:S(2)}, u32[]{:S(2)}) collective-permute-start(f32[72,1280]{1,0:T(8,128)S(1)} %slice.58), channel_id=1, source_target_pairs={{0,16},{16,32},{32,48},{48,0},{1,17},{17,33},{33,49},{49,1},{2,18}... | collective-permute-start | bytes 1105928 | tf_op jit(solution)/shard_map/ppermute | solution.py:620
  195.7 15.2 %all-to-all-start.3 = ((f32[16,3,16,128]{3,2,1,0:T(8,128)}), f32[16,3,16,128]{3,2,1,0:T(8,128)S(1)}, u32[]{:S(2)}, u32[]{:S(2)}) async-start(f32[16,3,16,128]{3,2,1,0:T(8,128)} %bitcast.7), calls=%async_computation.3 | async-start | bytes 786432 | tf_op jit(solution)/shard_map/all_to_all | solution.py:568
  202.4 8.5 %copy-start.5 = (f32[2,20,128]{2,1,0:T(8,128)S(1)}, f32[2,20,128]{2,1,0:T(8,128)}, u32[]{:S(2)}) copy-start(f32[2,20,128]{2,1,0:T(8,128)} %constant.76.clone.refs_1_.twiddle_ref) | copy-start | bytes 61444
  202.4 8.5 %copy-start.7 = (f32[40]{0:T(128)S(1)}, f32[40]{0:T(128)}, u32[]{:S(2)}) copy-start(f32[40]{0:T(128)} %weight_ref.1) | copy-start | bytes 484
  202.4 8.5 %copy-start.8 = (bf16[512,512]{1,0:T(8,128)(2,1)S(1)}, bf16[512,512]{1,0:T(8,128)(2,1)}, u32[]{:S(2)}) copy-start(bf16[512,512]{1,0:T(8,128)(2,1)} %constant.78.clone.table_ref) | copy-start | bytes 1572868

commit v6 on v4

--- a/solution.py
+++ b/solution.py
@@ -628,6 +628,8 @@
             right = after(right, later["new"])
         rows = grid_rows(start, count, (0, 1, 3), now["other"], (now["new"], right, now["left"]))
         rows = grid_rows(start, count, (2,), now["other"], (top, now["bottom"], rows))
+        if later:
+            rows = after(rows, *later["ends"])
         results.append(exchange(rows.reshape(16, 3, 4 * count, N2)))
     early = pl.pallas_call(
         scatter_kernel,

time: 217 us -> 219 us (level)
  transfers between devices with their start and end apart: 23 -> 23, of which waited for: 11 -> 11; matrix products, arithmetic and copies ran while one was open for 3% -> 3% of each run, Pallas kernels for 28% -> 27%
where the time goes in v6:
time: 219 us; the launch traced here: 217 us
  Pallas kernels  72.6 us (33%)
  waiting for transfers between devices  64.8 us (30%)
  starting transfers between devices  50.2 us (23%)
  blocking collectives  16.4 us (7%)
  other arithmetic  7.05 us (3%)
  local copies, waits for them, and re-layouts  5.89 us (3%)
    pallas_call x4, Pallas kernels, grid_rows(): pl.pallas_call(lambda *refs: grid_rows_kernel(start, count, rels, *refs),...  24.4 us
    pallas_call x4, Pallas kernels, spectra(): pl.pallas_call(lambda *refs: spectra_kernel(start, count, rels, *refs), o...  23.7 us
    all_to_all x3, starting transfers between devices, exchange(): return lax.all_to_all(value, ('core', 'wave'), 0, 0, tiled=True)  19.8 us
    ppermute x2, waiting for transfers between devices, per_device(): right = lax.ppermute(new, 'z', DOWN)  18.4 us
    all_to_all x1, blocking collectives, exchange(): return lax.all_to_all(value, ('core', 'wave'), 0, 0, tiled=True)  16.4 us
    all_to_all x3, waiting for transfers between devices, exchange(): return lax.all_to_all(value, ('core', 'wave'), 0, 0, tiled=True)  15.7 us
    ppermute x2, waiting for transfers between devices, per_device(): top = lax.ppermute(top, 'z', UP)  9.08 us
    pallas_call x2, Pallas kernels, implicit(): pl.pallas_call(lambda *refs: implicit_kernel(start, count, *refs), out_sh...  8.48 us
  transfers between devices with their start and end apart: 23, of which 11 were waited for; matrix products, arithmetic and copies ran while one was open for 3% of the time, Pallas kernels for 27%

profile of v6, /device:TPU:1, one launch (start us, length us, event | category | flops | bytes accessed | tf_op | source)
XLA Modules:
  0.0 217.1 jit_solution(5027183960606379788)
XLA Ops:
  0.1 0.8 broadcast_in_dim.2.owner_ref
  0.9 1.3 copy-done.1
  2.2 1.0 copy-done.2
  4.0 8.4 %fourier.1 = (f32[16,3,24,128]{3,2,1,0:T(8,128)S(1)}, f32[16,3,16,128]{3,2,1,0:T(8,128)}, f32[24,40,1408]{2,1,0:T(8,128)S(1)}, f32[16,40,1408]{2,1,0:T(8,128)}) custom-call(s32[3]{0:T(128)S(1)} %pad_add_fusion.place_ref.refs_0_, s32[640,128]{1,0:T(8,128)S(1)} %broadcast_in_dim.2.owner_ref, f32[3,5,6,2560]{3,2,1,0:T(8,128)S(1)} %bitcast.15, ...), custom_call_target="tpu_custom_call" | custom-call | flops 4000000000 | bytes 26000000 | tf_op jit(solution)/shard_map/fourier/pallas_call | solution.py:472
  12.4 1.5 collective-permute-start
  13.9 16.4 %all_to_all.20 = f32[16,3,24,128]{3,2,1,0:T(8,128)S(1)} all-to-all(f32[16,3,24,128]{3,2,1,0:T(8,128)S(1)} %get-tuple-element.55), channel_id=1, replica_groups=mesh['yh'=2,'z'=4,'core'=2,'wave'=8] {'core','wave'}, dimensions={0} | all-to-all | bytes 1179648 | tf_op jit(solution)/shard_map/all_to_all | solution.py:568
  31.1 4.2 %spectra.5 = (f32[112,1280]{1,0:T(8,128)S(1)}, f32[112,1280]{1,0:T(8,128)S(1)}) custom-call(s32[3]{0:T(128)S(1)} %pad_add_fusion.place_ref.refs_0_, s32[640]{0:T(1024)S(1)} %copy-done.3, f32[80,40,1408]{2,1,0:T(8,128)} %refs_2_.16, f32[24,40,1408]{2,1,0:T(8,128)S(1)} %collective-permute-done.refs_3_, f32[1152,128]{1,0:T(8,128)S(1)} %bitcast.11), custom_call_target="tpu_custom_call" | custom-call | flops 300000000 | bytes 3000000 | tf_op jit(solution)/shard_map/spectra/pallas_call | solution.py:519
  35.3 1.7 collective-permute-start.1
  37.0 2.2 %collective-permute-start.2 = (f32[112,1280]{1,0:T(8,128)S(1)}, f32[112,1280]{1,0:T(8,128)S(1)}, u32[]{:S(2)}, u32[]{:S(2)}) collective-permute-start(f32[112,1280]{1,0:T(8,128)S(1)} %get-tuple-element.60), channel_id=1, source_target_pairs={{0,48},{16,0},{32,16},{48,32},{1,49},{17,1},{33,17},{49,33},{2,50}... | collective-permute-start | bytes 1720328 | tf_op jit(solution)/shard_map/ppermute | solution.py:594
  39.2 8.7 %spectra.4 = (f32[224,1280]{1,0:T(8,128)S(1)}, f32[224,1280]{1,0:T(8,128)S(1)}, f32[224,1280]{1,0:T(8,128)S(1)}) custom-call(s32[3]{0:T(128)S(1)} %pad_add_fusion.place_ref.refs_0_, s32[640]{0:T(1024)S(1)} %copy-done.3, f32[80,40,1408]{2,1,0:T(8,128)} %refs_2_.16, f32[24,40,1408]{2,1,0:T(8,128)S(1)} %collective-permute-done.refs_3_, f32[1152,128]{1,0:T(8,128)S(1)} %bitcast.12), custom_call_target="tpu_custom_call" | custom-call | flops 900000000 | bytes 9000000 | tf_op jit(solution)/shard_map/spectra/pallas_call | solution.py:519
  47.9 4.5 %collective-permute-done.1.top_ref = f32[112,1280]{1,0:T(8,128)S(1)} collective-permute-done((f32[112,1280]{1,0:T(8,128)S(1)}, f32[112,1280]{1,0:T(8,128)S(1)}, u32[]{:S(2)}, u32[]{:S(2)}) %collective-permute-start.1) | collective-permute-done | bytes 573472 | tf_op jit(solution)/shard_map/ppermute | solution.py:593
  52.5 1.6 fold.1
  54.5 2.2 %collective-permute-start.5 = (f32[224,1280]{1,0:T(8,128)}, f32[224,1280]{1,0:T(8,128)}, u32[]{:S(2)}, u32[]{:S(2)}) collective-permute-start(f32[224,1280]{1,0:T(8,128)} %get-tuple-element.65), channel_id=1, source_target_pairs={{0,48},{16,0},{32,16},{48,32},{1,49},{17,1},{33,17},{49,33},{2,50}... | collective-permute-start | bytes 3440648 | tf_op jit(solution)/shard_map/ppermute | solution.py:608
  56.8 4.5 %all-to-all-start.1 = ((f32[16,3,16,128]{3,2,1,0:T(8,128)}), f32[16,3,16,128]{3,2,1,0:T(8,128)S(1)}, u32[]{:S(2)}, u32[]{:S(2)}) async-start(f32[16,3,16,128]{3,2,1,0:T(8,128)} %get-tuple-element.66), calls=%async_computation.1 | async-start | bytes 786432 | tf_op jit(solution)/shard_map/all_to_all | solution.py:568
  61.3 8.5 %all-to-all-done.1 = f32[16,3,16,128]{3,2,1,0:T(8,128)S(1)} async-done(((f32[16,3,16,128]{3,2,1,0:T(8,128)}), f32[16,3,16,128]{3,2,1,0:T(8,128)S(1)}, u32[]{:S(2)}, u32[]{:S(2)}) %all-to-all-start.1) | async-done | bytes 393248 | tf_op jit(solution)/shard_map/all_to_all | solution.py:568
  69.8 3.0 %spectra.7 = (f32[72,1280]{1,0:T(8,128)S(1)}, f32[80,1280]{1,0:T(8,128)S(1)}) custom-call(s32[3]{0:T(128)S(1)} %pad_add_fusion.place_ref.refs_0_, s32[640]{0:T(1024)S(1)} %copy-done.3, f32[80,40,1408]{2,1,0:T(8,128)} %refs_2_.16, f32[16,40,1408]{2,1,0:T(8,128)} %collective-permute-done.4.refs_3_, f32[768,128]{1,0:T(8,128)S(1)} %bitcast.13), custom_call_target="tpu_custom_call" | custom-call | flops 200000000 | bytes 2000000 | tf_op jit(solution)/shard_map/spectra/pallas_call | solution.py:519
  72.8 7.8 %spectra.6 = (f32[152,1280]{1,0:T(8,128)}, f32[152,1280]{1,0:T(8,128)}, f32[152,1280]{1,0:T(8,128)S(1)}) custom-call(s32[3]{0:T(128)S(1)} %pad_add_fusion.place_ref.refs_0_, s32[640]{0:T(1024)S(1)} %copy-done.3, f32[80,40,1408]{2,1,0:T(8,128)} %refs_2_.16, f32[16,40,1408]{2,1,0:T(8,128)} %collective-permute-done.4.refs_3_, f32[768,128]{1,0:T(8,128)S(1)} %bitcast.14), custom_call_target="tpu_custom_call" | custom-call | flops 600000000 | bytes 6000000 | tf_op jit(solution)/shard_map/spectra/pallas_call | solution.py:519
  80.6 1.2 collective-permute-done.3
  81.8 1.8 add_add_fusion.refs_7_
  83.7 2.7 %collective-permute-start.6 = (f32[224,1280]{1,0:T(8,128)S(1)}, f32[224,1280]{1,0:T(8,128)S(1)}, u32[]{:S(2)}, u32[]{:S(2)}) collective-permute-start(f32[224,1280]{1,0:T(8,128)S(1)} %add_add_fusion.refs_7_), channel_id=1, source_target_pairs={{0,64},{64,0},{1,65},{65,1},{2,66},{66,2},{3,67},{67,3},{4,68},{68... | collective-permute-start | bytes 3440648 | tf_op jit(solution)/shard_map/ppermute | solution.py:577
  86.4 2.6 %collective-permute-start.13 = (f32[80,1280]{1,0:T(8,128)S(1)}, f32[80,1280]{1,0:T(8,128)S(1)}, u32[]{:S(2)}, u32[]{:S(2)}) collective-permute-start(f32[80,1280]{1,0:T(8,128)S(1)} %get-tuple-element.74), channel_id=1, source_target_pairs={{0,48},{16,0},{32,16},{48,32},{1,49},{17,1},{33,17},{49,33},{2,50}... | collective-permute-start | bytes 1228808 | tf_op jit(solution)/shard_map/ppermute | solution.py:594
  89.0 4.5 %collective-permute-done.11 = f32[72,1280]{1,0:T(8,128)S(1)} collective-permute-done((f32[72,1280]{1,0:T(8,128)S(1)}, f32[72,1280]{1,0:T(8,128)S(1)}, u32[]{:S(2)}, u32[]{:S(2)}) %collective-permute-start.11) | collective-permute-done | bytes 368672 | tf_op jit(solution)/shard_map/ppermute | solution.py:593
  93.6 1.8 add_dynamic-update-slice_fusion.1
  95.8 1.8 add_dynamic-update-slice_fusion
  97.6 3.4 %collective-permute-start.14 = (f32[152,1280]{1,0:T(8,128)}, f32[152,1280]{1,0:T(8,128)}, u32[]{:S(2)}, u32[]{:S(2)}) collective-permute-start(f32[152,1280]{1,0:T(8,128)} %add_dynamic-update-slice_fusion), channel_id=1, source_target_pairs={{0,48},{16,0},{32,16},{48,32},{1,49},{17,1},{33,17},{49,33},{2,50}... | collective-permute-start | bytes 2334728 | tf_op jit(solution)/shard_map/ppermute | solution.py:608
  101.3 8.4 %collective-permute-done.6.refs_8_ = f32[224,1280]{1,0:T(8,128)S(1)} collective-permute-done((f32[224,1280]{1,0:T(8,128)S(1)}, f32[224,1280]{1,0:T(8,128)S(1)}, u32[]{:S(2)}, u32[]{:S(2)}) %collective-permute-start.6) | collective-permute-done | bytes 1146912 | tf_op jit(solution)/shard_map/ppermute | solution.py:577
  109.7 4.2 %implicit.2.refs_4_ = f32[224,1280]{1,0:T(8,128)S(1)} custom-call(s32[3]{0:T(128)S(1)} %pad_add_fusion.place_ref.refs_0_, s32[640]{0:T(1024)S(1)} %copy-done.3, f32[36]{0:T(128)S(1)} %reshape.74.refs_2_, f32[36]{0:T(128)S(1)} %reshape.75.refs_3_, f32[6]{0:T(128)S(1)} %copy-done.6, f32[36]{0:T(128)S(1)} %reshape.76.refs_5_, f32[36]{0:T(128)S(1)} %reshape.77.refs_6_, ...), custom_call_target="tpu_custom_call" | custom-call | flops 60000000 | bytes 3600000 | tf_op jit(solution)/shard_map/implicit/pallas_call | solution.py:536
  114.0 3.5 %collective-permute-start.9 = (f32[224,1280]{1,0:T(8,128)S(1)}, f32[224,1280]{1,0:T(8,128)S(1)}, u32[]{:S(2)}, u32[]{:S(2)}) collective-permute-start(f32[224,1280]{1,0:T(8,128)S(1)} %implicit.2.refs_4_), channel_id=1, source_target_pairs={{0,48},{16,0},{32,16},{48,32},{1,49},{17,1},{33,17},{49,33},{2,50}... | collective-permute-start | bytes 3440648 | tf_op jit(solution)/shard_map/ppermute | solution.py:617
  117.4 1.5 add_add_fusion.1.refs_7_
  119.0 2.8 %collective-permute-start.15 = (f32[152,1280]{1,0:T(8,128)S(1)}, f32[152,1280]{1,0:T(8,128)S(1)}, u32[]{:S(2)}, u32[]{:S(2)}) collective-permute-start(f32[152,1280]{1,0:T(8,128)S(1)} %add_add_fusion.1.refs_7_), channel_id=1, source_target_pairs={{0,64},{64,0},{1,65},{65,1},{2,66},{66,2},{3,67},{67,3},{4,68},{68... | collective-permute-start | bytes 2334728 | tf_op jit(solution)/shard_map/ppermute | solution.py:577
  121.8 18.4 %collective-permute-done.9.refs_5_ = f32[224,1280]{1,0:T(8,128)S(1)} collective-permute-done((f32[224,1280]{1,0:T(8,128)S(1)}, f32[224,1280]{1,0:T(8,128)S(1)}, u32[]{:S(2)}, u32[]{:S(2)}) %collective-permute-start.9) | collective-permute-done | bytes 1146912 | tf_op jit(solution)/shard_map/ppermute | solution.py:617
  140.2 3.5 %collective-permute-start.10 = (f32[112,1280]{1,0:T(8,128)S(1)}, f32[112,1280]{1,0:T(8,128)S(1)}, u32[]{:S(2)}, u32[]{:S(2)}) collective-permute-start(f32[112,1280]{1,0:T(8,128)S(1)} %slice.57), channel_id=1, source_target_pairs={{0,48},{16,0},{32,16},{48,32},{1,49},{17,1},{33,17},{49,33},{2,50}... | collective-permute-start | bytes 1720328 | tf_op jit(solution)/shard_map/ppermute | solution.py:621
  143.9 4.2 %implicit.3.refs_4_ = f32[152,1280]{1,0:T(8,128)S(1)} custom-call(s32[3]{0:T(128)S(1)} %pad_add_fusion.place_ref.refs_0_, s32[640]{0:T(1024)S(1)} %copy-done.3, f32[36]{0:T(128)S(1)} %reshape.74.refs_2_, f32[36]{0:T(128)S(1)} %reshape.75.refs_3_, f32[6]{0:T(128)S(1)} %copy-done.6, f32[36]{0:T(128)S(1)} %reshape.76.refs_5_, f32[36]{0:T(128)S(1)} %reshape.77.refs_6_, ...), custom_call_target="tpu_custom_call" | custom-call | flops 40000000 | bytes 2400000 | tf_op jit(solution)/shard_map/implicit/pallas_call | solution.py:536
  148.1 4.7 %collective-permute-done.10.refs_5_ = f32[112,1280]{1,0:T(8,128)S(1)} collective-permute-done((f32[112,1280]{1,0:T(8,128)S(1)}, f32[112,1280]{1,0:T(8,128)S(1)}, u32[]{:S(2)}, u32[]{:S(2)}) %collective-permute-start.10) | collective-permute-done | bytes 573472 | tf_op jit(solution)/shard_map/ppermute | solution.py:621
  152.8 3.2 %collective-permute-done.8.refs_4_ = f32[112,1280]{1,0:T(8,128)S(1)} collective-permute-done((f32[112,1280]{1,0:T(8,128)S(1)}, f32[112,1280]{1,0:T(8,128)S(1)}, u32[]{:S(2)}, u32[]{:S(2)}) %collective-permute-start.8) | collective-permute-done | bytes 573472 | tf_op jit(solution)/shard_map/ppermute | solution.py:620
  156.3 1.3 collective-permute-start.16
  157.6 9.0 %grid_rows.4.refs_6_ = f32[1152,128]{1,0:T(8,128)S(1)} custom-call(s32[3]{0:T(128)S(1)} %pad_add_fusion.place_ref.refs_0_, s32[640]{0:T(1024)S(1)} %copy-done.3, f32[80,40,1408]{2,1,0:T(8,128)} %refs_2_.16, f32[24,40,1408]{2,1,0:T(8,128)S(1)} %bitcast.10, f32[224,1280]{1,0:T(8,128)S(1)} %implicit.2.refs_4_, f32[224,1280]{1,0:T(8,128)S(1)} %collective-permute-done.9.refs_5_, ...), custom_call_target="tpu_custom_call" | custom-call | flops 1260000000 | bytes 9000000 | tf_op jit(solution)/shard_map/grid_rows/pallas_call | solution.py:549
  166.6 4.8 %grid_rows.5 = f32[1152,128]{1,0:T(8,128)} custom-call(s32[3]{0:T(128)S(1)} %pad_add_fusion.place_ref.refs_0_, s32[640]{0:T(1024)S(1)} %copy-done.3, f32[80,40,1408]{2,1,0:T(8,128)} %refs_2_.16, f32[24,40,1408]{2,1,0:T(8,128)S(1)} %bitcast.10, f32[112,1280]{1,0:T(8,128)S(1)} %collective-permute-done.8.refs_4_, ...), custom_call_target="tpu_custom_call" | custom-call | flops 420000000 | bytes 3000000 | tf_op jit(solution)/shard_map/grid_rows/pallas_call | solution.py:549
  172.1 0.8 slice.58
  172.9 8.6 %all-to-all-start.2 = ((f32[16,3,24,128]{3,2,1,0:T(8,128)}), f32[16,3,24,128]{3,2,1,0:T(8,128)S(1)}, u32[]{:S(2)}, u32[]{:S(2)}) async-start(f32[16,3,24,128]{3,2,1,0:T(8,128)} %bitcast.6), calls=%async_computation.2 | async-start | bytes 1179648 | tf_op jit(solution)/shard_map/all_to_all | solution.py:568
  181.5 0.9 collective-permute-start.19
  182.9 6.8 %grid_rows.6.refs_6_ = f32[768,128]{1,0:T(8,128)S(1)} custom-call(s32[3]{0:T(128)S(1)} %pad_add_fusion.place_ref.refs_0_, s32[640]{0:T(1024)S(1)} %copy-done.3, f32[80,40,1408]{2,1,0:T(8,128)} %refs_2_.16, f32[16,40,1408]{2,1,0:T(8,128)} %collective-permute-done.4.refs_3_, f32[152,1280]{1,0:T(8,128)S(1)} %implicit.3.refs_4_, ...), custom_call_target="tpu_custom_call" | custom-call | flops 840000000 | bytes 6000000 | tf_op jit(solution)/shard_map/grid_rows/pallas_call | solution.py:549
  189.8 3.6 %collective-permute-done.18.refs_4_ = f32[72,1280]{1,0:T(8,128)S(1)} collective-permute-done((f32[72,1280]{1,0:T(8,128)}, f32[72,1280]{1,0:T(8,128)S(1)}, u32[]{:S(2)}, u32[]{:S(2)}) %collective-permute-start.18) | collective-permute-done | bytes 368672 | tf_op jit(solution)/shard_map/ppermute | solution.py:620
  193.4 3.8 %grid_rows.7 = f32[768,128]{1,0:T(8,128)} custom-call(s32[3]{0:T(128)S(1)} %pad_add_fusion.place_ref.refs_0_, s32[640]{0:T(1024)S(1)} %copy-done.3, f32[80,40,1408]{2,1,0:T(8,128)} %refs_2_.16, f32[16,40,1408]{2,1,0:T(8,128)} %collective-permute-done.4.refs_3_, f32[72,1280]{1,0:T(8,128)S(1)} %collective-permute-done.18.refs_4_, ...), custom_call_target="tpu_custom_call" | custom-call | flops 280000000 | bytes 2000000 | tf_op jit(solution)/shard_map/grid_rows/pallas_call | solution.py:549
  197.2 6.7 %all-to-all-start.3 = ((f32[16,3,16,128]{3,2,1,0:T(8,128)}), f32[16,3,16,128]{3,2,1,0:T(8,128)S(1)}, u32[]{:S(2)}, u32[]{:S(2)}) async-start(f32[16,3,16,128]{3,2,1,0:T(8,128)} %bitcast.7), calls=%async_computation.3 | async-start | bytes 786432 | tf_op jit(solution)/shard_map/all_to_all | solution.py:568
  204.0 1.3 scatter.1.early_ref
  205.3 7.1 %all-to-all-done.3.got_ref = f32[16,3,16,128]{3,2,1,0:T(8,128)S(1)} async-done(((f32[16,3,16,128]{3,2,1,0:T(8,128)}), f32[16,3,16,128]{3,2,1,0:T(8,128)S(1)}, u32[]{:S(2)}, u32[]{:S(2)}) %all-to-all-start.3) | async-done | bytes 393248 | tf_op jit(solution)/shard_map/all_to_all | solution.py:568
  212.4 4.7 %inverse.1 = f32[3,5,6,2560]{3,2,1,0:T(8,128)} custom-call(s32[640,128]{1,0:T(8,128)S(1)} %broadcast_in_dim.2.owner_ref, f32[40]{0:T(128)S(1)} %copy-done.7, s32[3]{0:T(128)S(1)} %pad_add_fusion.place_ref.refs_0_, f32[2,20,128]{2,1,0:T(8,128)S(1)} %copy-done.5, bf16[512,512]{1,0:T(8,128)(2,1)S(1)} %copy-done.8, f32[184,1280]{1,0:T(8,128)S(1)} %scatter.1.early_ref, ...), custom_call_target="tpu_custom_call" | custom-call | flops 4000000000 | bytes 8000000 | tf_op jit(solution)/shard_map/inverse/pallas_call | solution.py:643
  (58 shorter events, 4.6 us)
Async XLA Ops:
  0.9 1.3 copy-start.1
  2.2 1.0 copy-start.2
  3.2 0.7 copy-start.4
  12.4 18.7 %copy-start.3 = (s32[640]{0:T(1024)S(1)}, s32[640]{0:T(1024)}, u32[]{:S(2)}) copy-start(s32[640]{0:T(1024)} %refs_1_.20) | copy-start | bytes 7684
  12.4 18.7 %collective-permute-start = (f32[24,40,1408]{2,1,0:T(8,128)S(1)}, f32[24,40,1408]{2,1,0:T(8,128)S(1)}, u32[]{:S(2)}, u32[]{:S(2)}) collective-permute-start(f32[24,40,1408]{2,1,0:T(8,128)S(1)} %get-tuple-element.54), channel_id=1, source_target_pairs={{0,8},{8,0},{1,9},{9,1},{2,10},{10,2},{3,11},{11,3},{4,12},{12,4},... | collective-permute-start | bytes 16220168 | tf_op jit(solution)/shard_map/ppermute | solution.py:586
  30.3 30.9 %collective-permute-start.4 = (f32[16,40,1408]{2,1,0:T(8,128)}, f32[16,40,1408]{2,1,0:T(8,128)}, u32[]{:S(2)}, u32[]{:S(2)}) collective-permute-start(f32[16,40,1408]{2,1,0:T(8,128)} %get-tuple-element.63), channel_id=1, source_target_pairs={{0,8},{8,0},{1,9},{9,1},{2,10},{10,2},{3,11},{11,3},{4,12},{12,4},... | collective-permute-start | bytes 10813448 | tf_op jit(solution)/shard_map/ppermute | solution.py:586
  31.1 8.1 %copy-start = (f32[24,40,1408]{2,1,0:T(8,128)}, f32[24,40,1408]{2,1,0:T(8,128)S(1)}, u32[]{:S(2)}) copy-start(f32[24,40,1408]{2,1,0:T(8,128)S(1)} %collective-permute-done.refs_3_) | copy-start | bytes 16220164
  35.3 17.2 %collective-permute-start.1 = (f32[112,1280]{1,0:T(8,128)S(1)}, f32[112,1280]{1,0:T(8,128)S(1)}, u32[]{:S(2)}, u32[]{:S(2)}) collective-permute-start(f32[112,1280]{1,0:T(8,128)S(1)} %get-tuple-element.58), channel_id=1, source_target_pairs={{0,16},{16,32},{32,48},{48,0},{1,17},{17,33},{33,49},{49,1},{2,18}... | collective-permute-start | bytes 1720328 | tf_op jit(solution)/shard_map/ppermute | solution.py:593
  37.0 15.5 %collective-permute-start.2 = (f32[112,1280]{1,0:T(8,128)S(1)}, f32[112,1280]{1,0:T(8,128)S(1)}, u32[]{:S(2)}, u32[]{:S(2)}) collective-permute-start(f32[112,1280]{1,0:T(8,128)S(1)} %get-tuple-element.60), channel_id=1, source_target_pairs={{0,48},{16,0},{32,16},{48,32},{1,49},{17,1},{33,17},{49,33},{2,50}... | collective-permute-start | bytes 1720328 | tf_op jit(solution)/shard_map/ppermute | solution.py:594
  54.1 27.8 %collective-permute-start.3 = (f32[224,1280]{1,0:T(8,128)}, f32[224,1280]{1,0:T(8,128)}, u32[]{:S(2)}, u32[]{:S(2)}) collective-permute-start(f32[224,1280]{1,0:T(8,128)} %get-tuple-element.61), channel_id=1, source_target_pairs={{0,16},{16,32},{32,48},{48,0},{1,17},{17,33},{33,49},{49,1},{2,18}... | collective-permute-start | bytes 3440648 | tf_op jit(solution)/shard_map/ppermute | solution.py:608
  54.5 27.3 %collective-permute-start.5 = (f32[224,1280]{1,0:T(8,128)}, f32[224,1280]{1,0:T(8,128)}, u32[]{:S(2)}, u32[]{:S(2)}) collective-permute-start(f32[224,1280]{1,0:T(8,128)} %get-tuple-element.65), channel_id=1, source_target_pairs={{0,48},{16,0},{32,16},{48,32},{1,49},{17,1},{33,17},{49,33},{2,50}... | collective-permute-start | bytes 3440648 | tf_op jit(solution)/shard_map/ppermute | solution.py:608
  56.8 13.1 %all-to-all-start.1 = ((f32[16,3,16,128]{3,2,1,0:T(8,128)}), f32[16,3,16,128]{3,2,1,0:T(8,128)S(1)}, u32[]{:S(2)}, u32[]{:S(2)}) async-start(f32[16,3,16,128]{3,2,1,0:T(8,128)} %get-tuple-element.66), calls=%async_computation.1 | async-start | bytes 786432 | tf_op jit(solution)/shard_map/all_to_all | solution.py:568
  83.6 9.9 %collective-permute-start.11 = (f32[72,1280]{1,0:T(8,128)S(1)}, f32[72,1280]{1,0:T(8,128)S(1)}, u32[]{:S(2)}, u32[]{:S(2)}) collective-permute-start(f32[72,1280]{1,0:T(8,128)S(1)} %get-tuple-element.72), channel_id=1, source_target_pairs={{0,16},{16,32},{32,48},{48,0},{1,17},{17,33},{33,49},{49,1},{2,18}... | collective-permute-start | bytes 1105928 | tf_op jit(solution)/shard_map/ppermute | solution.py:593
  83.7 26.0 %collective-permute-start.6 = (f32[224,1280]{1,0:T(8,128)S(1)}, f32[224,1280]{1,0:T(8,128)S(1)}, u32[]{:S(2)}, u32[]{:S(2)}) collective-permute-start(f32[224,1280]{1,0:T(8,128)S(1)} %add_add_fusion.refs_7_), channel_id=1, source_target_pairs={{0,64},{64,0},{1,65},{65,1},{2,66},{66,2},{3,67},{67,3},{4,68},{68... | collective-permute-start | bytes 3440648 | tf_op jit(solution)/shard_map/ppermute | solution.py:577
  86.4 9.3 %collective-permute-start.13 = (f32[80,1280]{1,0:T(8,128)S(1)}, f32[80,1280]{1,0:T(8,128)S(1)}, u32[]{:S(2)}, u32[]{:S(2)}) collective-permute-start(f32[80,1280]{1,0:T(8,128)S(1)} %get-tuple-element.74), channel_id=1, source_target_pairs={{0,48},{16,0},{32,16},{48,32},{1,49},{17,1},{33,17},{49,33},{2,50}... | collective-permute-start | bytes 1228808 | tf_op jit(solution)/shard_map/ppermute | solution.py:594
  93.6 7.4 %copy-start.9 = (f32[6,6]{1,0:T(8,128)S(1)}, f32[6,6]{1,0:T(8,128)}, u32[]{:S(2)}) copy-start(f32[6,6]{1,0:T(8,128)} %param.20) | copy-start | bytes 436
  93.6 7.5 %copy-start.10 = (f32[6,6]{1,0:T(8,128)S(1)}, f32[6,6]{1,0:T(8,128)}, u32[]{:S(2)}) copy-start(f32[6,6]{1,0:T(8,128)} %param.21) | copy-start | bytes 436
  93.6 7.6 %copy-start.11 = (f32[6,6]{1,0:T(8,128)S(1)}, f32[6,6]{1,0:T(8,128)}, u32[]{:S(2)}) copy-start(f32[6,6]{1,0:T(8,128)} %param.23) | copy-start | bytes 436
  93.6 7.7 %copy-start.12 = (f32[6,6]{1,0:T(8,128)S(1)}, f32[6,6]{1,0:T(8,128)}, u32[]{:S(2)}) copy-start(f32[6,6]{1,0:T(8,128)} %param.24) | copy-start | bytes 436
  93.6 16.1 %copy-start.6 = (f32[6]{0:T(128)S(1)}, f32[6]{0:T(128)}, u32[]{:S(2)}) copy-start(f32[6]{0:T(128)} %refs_4_.3) | copy-start | bytes 76
  95.4 22.0 %collective-permute-start.12 = (f32[152,1280]{1,0:T(8,128)}, f32[152,1280]{1,0:T(8,128)}, u32[]{:S(2)}, u32[]{:S(2)}) collective-permute-start(f32[152,1280]{1,0:T(8,128)} %add_dynamic-update-slice_fusion.1), channel_id=1, source_target_pairs={{0,16},{16,32},{32,48},{48,0},{1,17},{17,33},{33,49},{49,1},{2,18}... | collective-permute-start | bytes 2334728 | tf_op jit(solution)/shard_map/ppermute | solution.py:608
  97.6 19.9 %collective-permute-start.14 = (f32[152,1280]{1,0:T(8,128)}, f32[152,1280]{1,0:T(8,128)}, u32[]{:S(2)}, u32[]{:S(2)}) collective-permute-start(f32[152,1280]{1,0:T(8,128)} %add_dynamic-update-slice_fusion), channel_id=1, source_target_pairs={{0,48},{16,0},{32,16},{48,32},{1,49},{17,1},{33,17},{49,33},{2,50}... | collective-permute-start | bytes 2334728 | tf_op jit(solution)/shard_map/ppermute | solution.py:608
  109.7 47.9 %slice-start = ((s8[5406720]{0:T(1024)(128)(4,1)}), s8[4194304]{0:T(1024)(128)(4,1)S(1)}, s32[]{:S(2)}) async-start(s8[5406720]{0:T(1024)(128)(4,1)} %bitcast.9), calls=%async_computation.4 | async-start | bytes 8388608
  114.0 43.6 %slice-start.1 = ((s8[5406720]{0:T(1024)(128)(4,1)}), s8[1212416]{0:T(1024)(128)(4,1)S(1)}, s32[]{:S(2)}) async-start(s8[5406720]{0:T(1024)(128)(4,1)} %bitcast.9), calls=%async_computation.5 | async-start | bytes 2424832
  114.0 26.2 %collective-permute-start.9 = (f32[224,1280]{1,0:T(8,128)S(1)}, f32[224,1280]{1,0:T(8,128)S(1)}, u32[]{:S(2)}, u32[]{:S(2)}) collective-permute-start(f32[224,1280]{1,0:T(8,128)S(1)} %implicit.2.refs_4_), channel_id=1, source_target_pairs={{0,48},{16,0},{32,16},{48,32},{1,49},{17,1},{33,17},{49,33},{2,50}... | collective-permute-start | bytes 3440648 | tf_op jit(solution)/shard_map/ppermute | solution.py:617
  117.4 26.3 %collective-permute-start.7 = (f32[224,1280]{1,0:T(8,128)S(1)}, f32[224,1280]{1,0:T(8,128)S(1)}, u32[]{:S(2)}, u32[]{:S(2)}) collective-permute-start(f32[224,1280]{1,0:T(8,128)S(1)} %implicit.2.refs_4_), channel_id=1, source_target_pairs={{0,16},{16,32},{32,48},{48,0},{1,17},{17,33},{33,49},{49,1},{2,18}... | collective-permute-start | bytes 3440648 | tf_op jit(solution)/shard_map/ppermute | solution.py:616
  119.0 24.9 %collective-permute-start.15 = (f32[152,1280]{1,0:T(8,128)S(1)}, f32[152,1280]{1,0:T(8,128)S(1)}, u32[]{:S(2)}, u32[]{:S(2)}) collective-permute-start(f32[152,1280]{1,0:T(8,128)S(1)} %add_add_fusion.1.refs_7_), channel_id=1, source_target_pairs={{0,64},{64,0},{1,65},{65,1},{2,66},{66,2},{3,67},{67,3},{4,68},{68... | collective-permute-start | bytes 2334728 | tf_op jit(solution)/shard_map/ppermute | solution.py:577
  140.2 12.6 %collective-permute-start.10 = (f32[112,1280]{1,0:T(8,128)S(1)}, f32[112,1280]{1,0:T(8,128)S(1)}, u32[]{:S(2)}, u32[]{:S(2)}) collective-permute-start(f32[112,1280]{1,0:T(8,128)S(1)} %slice.57), channel_id=1, source_target_pairs={{0,48},{16,0},{32,16},{48,32},{1,49},{17,1},{33,17},{49,33},{2,50}... | collective-permute-start | bytes 1720328 | tf_op jit(solution)/shard_map/ppermute | solution.py:621
  143.8 12.3 %collective-permute-start.8 = (f32[112,1280]{1,0:T(8,128)S(1)}, f32[112,1280]{1,0:T(8,128)S(1)}, u32[]{:S(2)}, u32[]{:S(2)}) collective-permute-start(f32[112,1280]{1,0:T(8,128)S(1)} %slice.56), channel_id=1, source_target_pairs={{0,16},{16,32},{32,48},{48,0},{1,17},{17,33},{33,49},{49,1},{2,18}... | collective-permute-start | bytes 1720328 | tf_op jit(solution)/shard_map/ppermute | solution.py:620
  156.1 15.3 %collective-permute-start.17 = (f32[152,1280]{1,0:T(8,128)S(1)}, f32[152,1280]{1,0:T(8,128)S(1)}, u32[]{:S(2)}, u32[]{:S(2)}) collective-permute-start(f32[152,1280]{1,0:T(8,128)S(1)} %implicit.3.refs_4_), channel_id=1, source_target_pairs={{0,48},{16,0},{32,16},{48,32},{1,49},{17,1},{33,17},{49,33},{2,50}... | collective-permute-start | bytes 2334728 | tf_op jit(solution)/shard_map/ppermute | solution.py:617
  156.3 15.9 %collective-permute-start.16 = (f32[152,1280]{1,0:T(8,128)S(1)}, f32[152,1280]{1,0:T(8,128)S(1)}, u32[]{:S(2)}, u32[]{:S(2)}) collective-permute-start(f32[152,1280]{1,0:T(8,128)S(1)} %implicit.3.refs_4_), channel_id=1, source_target_pairs={{0,16},{16,32},{32,48},{48,0},{1,17},{17,33},{33,49},{49,1},{2,18}... | collective-permute-start | bytes 2334728 | tf_op jit(solution)/shard_map/ppermute | solution.py:616
  172.9 24.3 %all-to-all-start.2 = ((f32[16,3,24,128]{3,2,1,0:T(8,128)}), f32[16,3,24,128]{3,2,1,0:T(8,128)S(1)}, u32[]{:S(2)}, u32[]{:S(2)}) async-start(f32[16,3,24,128]{3,2,1,0:T(8,128)} %bitcast.6), calls=%async_computation.2 | async-start | bytes 1179648 | tf_op jit(solution)/shard_map/all_to_all | solution.py:568
  181.5 11.9 %collective-permute-start.19 = (f32[80,1280]{1,0:T(8,128)}, f32[80,1280]{1,0:T(8,128)S(1)}, u32[]{:S(2)}, u32[]{:S(2)}) collective-permute-start(f32[80,1280]{1,0:T(8,128)} %slice.59), channel_id=1, source_target_pairs={{0,48},{16,0},{32,16},{48,32},{1,49},{17,1},{33,17},{49,33},{2,50}... | collective-permute-start | bytes 1228808 | tf_op jit(solution)/shard_map/ppermute | solution.py:621
  182.3 11.1 %collective-permute-start.18 = (f32[72,1280]{1,0:T(8,128)}, f32[72,1280]{1,0:T(8,128)S(1)}, u32[]{:S(2)}, u32[]{:S(2)}) collective-permute-start(f32[72,1280]{1,0:T(8,128)} %slice.58), channel_id=1, source_target_pairs={{0,16},{16,32},{32,48},{48,0},{1,17},{17,33},{33,49},{49,1},{2,18}... | collective-permute-start | bytes 1105928 | tf_op jit(solution)/shard_map/ppermute | solution.py:620
  197.2 15.2 %all-to-all-start.3 = ((f32[16,3,16,128]{3,2,1,0:T(8,128)}), f32[16,3,16,128]{3,2,1,0:T(8,128)S(1)}, u32[]{:S(2)}, u32[]{:S(2)}) async-start(f32[16,3,16,128]{3,2,1,0:T(8,128)} %bitcast.7), calls=%async_computation.3 | async-start | bytes 786432 | tf_op jit(solution)/shard_map/all_to_all | solution.py:568
  203.9 8.5 %copy-start.5 = (f32[2,20,128]{2,1,0:T(8,128)S(1)}, f32[2,20,128]{2,1,0:T(8,128)}, u32[]{:S(2)}) copy-start(f32[2,20,128]{2,1,0:T(8,128)} %constant.76.clone.refs_1_.twiddle_ref) | copy-start | bytes 61444
  203.9 8.5 %copy-start.7 = (f32[40]{0:T(128)S(1)}, f32[40]{0:T(128)}, u32[]{:S(2)}) copy-start(f32[40]{0:T(128)} %weight_ref.1) | copy-start | bytes 484
  203.9 8.5 %copy-start.8 = (bf16[512,512]{1,0:T(8,128)(2,1)S(1)}, bf16[512,512]{1,0:T(8,128)(2,1)}, u32[]{:S(2)}) copy-start(bf16[512,512]{1,0:T(8,128)(2,1)} %constant.78.clone.table_ref) | copy-start | bytes 1572868
